TPU v7x, 32 devices: a whole 2x2x4 slice. The times are simulated.
32 devices in a mesh: row: 4 (over z), col: 8 (over y, x, core).
Axes of the slice: x: 2, y: 2, z: 4, core: 2. Of those that a mesh axis runs over, the one named last changes fastest.
Arguments:
- primitive: float32 [8, 32, 128, 512], P(None, None, 'col', 'row'), may hold values from -4 to 4, as said below
- current_sheet_bricks: int32 [4, 8, 8], P('row', 'col'), may hold values from 0 to 15, as said below
- brick_count: int32 [4, 8], P('row', 'col'), may hold values from 1 to 8, as said below
- w_in: bfloat16 [8, 128], replicated, may hold values from -2 to 2
- w_hid: bfloat16 [2, 128, 128], replicated, may hold values from -0.5 to 0.5
- w_out: bfloat16 [128], replicated, may hold values from -0.5 to 0.5
- b_hid: float32 [3, 128], replicated, may hold values from -3 to 3
Outputs:
- state_next: float32 [8, 32, 128, 512], P(None, None, 'col', 'row')
Inputs may be any that keep to these rules, and one draw needn't show every extreme that they name: `primitive`: row 0 (density) lies in 0.5 to 2 and row 7 (pressure) in 0.2 to 2. `current_sheet_bricks`: each device's 8 entries are distinct numbers of its own bricks. `brick_count`: in every row of devices some device lists 8 bricks.
All inputs are finite; a program needn't handle non-finite values.
Results may differ from a plain program's by a relative error of at most 0.0013.
Values may be sent and summed in bfloat16 or wider, within the bound.
No kernel may reach another device: no remote copies, remote signals or barrier semaphores. Data moves between devices by JAX's collectives and lax.ppermute only.
A program may use at most 256 MiB of HBM per device.

v0:
```python
import jax
import jax.numpy as jnp
from jax import lax
from jax.experimental import pallas as pl
from jax.experimental.pallas import tpu as pltpu
from jax.sharding import PartitionSpec as P

BRICK = 16
SUB = 4
ADIABATIC = 5.0 / 3.0
TIME_STEP = 0.02
RATE_LOW = 0.02
RATE_SPAN = 0.14
GELU_A = 0.7978845608
GELU_B = 0.7978845608 * 0.044715
F32 = jnp.float32
BF16 = jnp.bfloat16
LANES = 128
NZ = 32
CX = 16
HID = 128
PLANE = NZ * CX
KIN = 80
KHID = HID + 16
VMEM_LIMIT = 48 << 20


def iota(shape, dim):
    return lax.broadcasted_iota(jnp.int32, shape, dim)


def take(values, index):
    return jnp.take_along_axis(values, index, axis=1, mode="promise_in_bounds")


def next_row(v):
    return pltpu.roll(v, v.shape[0] - 1, 0)


def prev_row(v):
    return pltpu.roll(v, 1, 0)


def next_lane(v):
    return pltpu.roll(v, v.shape[1] - 1, 1)


def prev_lane(v):
    return pltpu.roll(v, 1, 1)


def derive(p):
    rho, pr = p[0], p[7]
    v, b = p[1:4], p[4:7]
    m = [rho * c for c in v]
    b2 = b[0] * b[0] + b[1] * b[1] + b[2] * b[2]
    v2 = v[0] * v[0] + v[1] * v[1] + v[2] * v[2]
    vb = v[0] * b[0] + v[1] * b[1] + v[2] * b[2]
    pt = pr + 0.5 * b2
    en = 1.5 * pr + 0.5 * (rho * v2 + b2)
    fast = jnp.sqrt((ADIABATIC * pr + b2) / rho)
    ep = en + pt
    tens = {(i, j): m[i] * v[j] - b[i] * b[j] for i in range(3) for j in range(i, 3)}
    elec = {(i, j): v[i] * b[j] - b[i] * v[j] for i in range(3) for j in range(i + 1, 3)}
    fluxes = []
    for d in range(3):
        rows = [m[d]]
        for c in range(3):
            t = tens[(min(c, d), max(c, d))]
            rows.append(t + pt if c == d else t)
        for c in range(3):
            rows.append(None if c == d else (elec[(d, c)] if d < c else -elec[(c, d)]))
        rows.append(ep * v[d] - b[d] * vb)
        fluxes.append(rows)
    speeds = [jnp.abs(c) + fast for c in v]
    return [rho] + m + list(b) + [en], fluxes, speeds


def face(u, un, f, fn, s, sn):
    a = 0.5 * jnp.maximum(s, sn)
    out = []
    for c in range(8):
        diss = a * (un[c] - u[c])
        out.append(-diss if f[c] is None else 0.5 * (f[c] + fn[c]) - diss)
    return out


def gelu_twice(u):
    u = u.astype(BF16)
    t = jnp.tanh(u * (jnp.asarray(GELU_A, BF16) + jnp.asarray(GELU_B, BF16) * (u * u)))
    return u + u * t


def closure_rates(first, w1, w2, wo):
    us = first
    for w in (w1, w2):
        hs = [jnp.concatenate([gelu_twice(u), bias_rows(u.shape[1]).astype(BF16)], axis=0) for u in us]
        us = [jnp.dot(w, h, preferred_element_type=F32) for h in hs]
    hs = [gelu_twice(u) for u in us]
    scores = [jnp.dot(wo, h, preferred_element_type=F32) for h in hs]
    return [(RATE_LOW + 0.5 * RATE_SPAN) + (0.5 * RATE_SPAN) * jnp.tanh(0.5 * s) for s in scores]


def features(load, z, patch_x=None, patch_y=None):
    zn, zp = lax.rem(z + 1, NZ), lax.rem(z + NZ - 1, NZ)
    row, lane = iota((CX, LANES), 0), iota((CX, LANES), 1)

    def dx(f, v):
        up, dn = next_row(v), prev_row(v)
        if patch_x is not None:
            lo, hi = patch_x(f, z)
            up = jnp.where(row == CX - 1, hi, up)
            dn = jnp.where(row == 0, lo, dn)
        return 0.5 * (up - dn)

    def dy(f, v):
        up, dn = next_lane(v), prev_lane(v)
        if patch_y is not None:
            edge = patch_y(f, z)
            up = jnp.where(lane == LANES - 1, edge, up)
            dn = jnp.where(lane == 0, edge, dn)
        return 0.5 * (up - dn)

    def dz(f):
        return 0.5 * (load(f, zn) - load(f, zp))

    rho, vx, vy, vz, bx, by, bz, pr = [load(f, z) for f in range(8)]
    jx = dy(6, bz) - dz(5)
    jy = dz(4) - dx(6, bz)
    jz = dx(5, by) - dy(4, bx)
    div = dx(1, vx) + dy(2, vy) + dz(3)
    return [jx, jy, jz, div, rho, pr, bx * bx + by * by + bz * bz, vx * vx + vy * vy + vz * vz]


def bias_rows(n):
    return jnp.where(iota((16, n), 0) < 3, 1.0, 0.0)


def plane_loader(prim_ref):
    def load(f, z):
        return prim_ref[pl.ds(pl.multiple_of((f * NZ + z) * CX, CX), CX), :]

    return load


def edge_lane_index():
    return jnp.where(iota((8, LANES), 1) % 2 == 0, 0, LANES - 1)


def pack_kernel(prim_ref, lo_ref, hi_ref, py_ref):
    lane = iota((8, LANES), 1)
    index = edge_lane_index()
    for f in range(8):
        lo_ref[pl.ds(f * NZ, NZ), :] = prim_ref[pl.ds(f * PLANE, NZ, stride=CX), :]
        hi_ref[pl.ds(f * NZ, NZ), :] = prim_ref[pl.ds(f * PLANE + CX - 1, NZ, stride=CX), :]
        acc = jnp.zeros((8, LANES), F32)
        for z in range(NZ):
            for o in range(2):
                v = prim_ref[pl.ds((f * NZ + z) * CX + o * 8, 8), :]
                acc = jnp.where(lane // 2 == o * NZ + z, take(v, index), acc)
        py_ref[pl.ds(f * 8, 8), :] = acc


def brick_rows(bricks_ref, count_ref):
    lane = iota((8, LANES), 1)
    slot, inner = lane // BRICK, lane % BRICK
    source = jnp.zeros((8, LANES), jnp.int32)
    half = jnp.zeros((8, LANES), jnp.int32)
    back = [jnp.full((8, LANES), -1, jnp.int32) for _ in range(2)]
    per_half = LANES // BRICK
    for j in range(8):
        b = bricks_ref[0, j]
        bz, by = b // per_half, b % per_half
        source = jnp.where(slot == j, by * BRICK + inner, source)
        half = jnp.where(slot == j, bz, half)
        for h in range(2):
            use = jnp.logical_and(bz == h, j < count_ref[0, 0])
            want = jnp.where(use, by, -1)
            back[h] = jnp.where(slot == want, j * BRICK + inner, back[h])
    return source, half, back


def main_kernel(bricks_ref, count_ref, prim_ref, win_ref, whid_ref, wout_ref, bias_ref,
                adv_ref, kap_ref, wb_ref, w1_ref, w2_ref, wo_ref,
                x_ref, u_ref, fz_ref, sz_ref, ch_ref):
    load = plane_loader(prim_ref)
    def split(b):
        hi = b.astype(BF16)
        r = b - hi.astype(F32)
        mid = r.astype(BF16)
        return [hi.astype(F32), mid.astype(F32), r - mid.astype(F32)]

    cols = (((0,), (0,)), ((), ()))
    rows = iota((16, KIN), 0)
    col = iota((16, KIN), 1)
    first = jnp.concatenate(
        [win_ref[...].astype(F32)] + split(bias_ref[0:1, :]) + [jnp.zeros((5, HID), F32)], axis=0
    ).astype(BF16)
    for s in range(8):
        place = jnp.where(rows < 8, rows * 8 + s, jnp.where(rows < 11, 64 + rows - 8, -1))
        pick = jnp.where(col == place, 1.0, 0.0).astype(BF16)
        wb_ref[pl.ds(s * HID, HID), :] = lax.dot_general(
            first, pick, cols, preferred_element_type=F32).astype(BF16)
    eye = jnp.where(iota((HID, HID), 0) == iota((HID, HID), 1), 0.5, 0.0).astype(BF16)
    eye16 = jnp.where(iota((16, 16), 0) == iota((16, 16), 1), 1.0, 0.0).astype(BF16)
    for layer, ref in ((0, w1_ref), (1, w2_ref)):
        turned = lax.dot_general(whid_ref[pl.ds(layer * HID, HID), :], eye, cols,
                                 preferred_element_type=F32)
        brow = jnp.concatenate(
            split(bias_ref[layer + 1 : layer + 2, :]) + [jnp.zeros((13, HID), F32)], axis=0
        ).astype(BF16)
        bcol = lax.dot_general(brow, eye16, cols, preferred_element_type=F32)
        ref[...] = jnp.concatenate([turned, bcol], axis=1).astype(BF16)
    wo_ref[...] = jnp.broadcast_to(0.5 * wout_ref[...].astype(F32), (16, HID)).astype(BF16)

    source, half, _ = brick_rows(bricks_ref, count_ref)
    tail = bias_rows(LANES)

    @pl.loop(0, NZ // 2)
    def _(z):
        low = features(load, z)
        high = features(load, z + NZ // 2)
        at = pl.ds(pl.multiple_of(z * LANES, LANES), LANES)
        for o in range(2):
            parts = []
            for a, b in zip(low, high):
                a, b = a[o * 8 : o * 8 + 8], b[o * 8 : o * 8 + 8]
                parts.append(jnp.where(half == 1, take(b, source), take(a, source)))
            x_ref[pl.ds(o * KIN, KIN), at] = jnp.concatenate(parts + [tail], axis=0).astype(BF16)

    w1, w2, wo = w1_ref[...], w2_ref[...], wo_ref[...]
    chunk = 8 * LANES

    @pl.loop(0, 4)
    def _(i):
        o, part = i // 2, i % 2
        x = x_ref[pl.ds(pl.multiple_of(o * KIN, 16), KIN),
                  pl.ds(pl.multiple_of(part * chunk, LANES), chunk)]
        us = [jnp.dot(wb_ref[pl.ds(s * HID, HID), :], x, preferred_element_type=F32)
              for s in range(8)]
        rates = closure_rates(us, w1, w2, wo)
        sub = iota((8, chunk), 0)
        out = rates[0][:8]
        for s in range(1, 8):
            out = jnp.where(sub == s, rates[s][:8], out)
        for j in range(8):
            kap_ref[pl.ds(pl.multiple_of((part * 8 + j) * CX + o * 8, 8), 8), :] = (
                out[:, j * LANES : (j + 1) * LANES])

    row, lane = iota((CX, LANES), 0), iota((CX, LANES), 1)

    @pl.loop(0, NZ)
    def _(z):
        u, f, s = derive([load(k, z) for k in range(8)])

        def along(d, nxt, prv, last):
            sn = nxt(s[d])
            fc = face(u, [nxt(c) for c in u], f[d],
                      [None if c is None else nxt(c) for c in f[d]], s[d], sn)
            fc = [jnp.where(last, 0.0, c) for c in fc]
            return [c - prv(c) for c in fc]

        cx = along(0, next_row, prev_row, row == CX - 1)
        cy = along(1, next_lane, prev_lane, lane == LANES - 1)
        at = [pl.ds(pl.multiple_of((k * NZ + z) * CX, CX), CX) for k in range(8)]
        for k in range(8):
            ch_ref[at[k], :] = cx[k] + cy[k]
            u_ref[at[k], :] = u[k]
            if f[2][k] is not None:
                fz_ref[at[k], :] = f[2][k]
        sz_ref[at[0], :] = s[2]

    def zface(z):
        zn = lax.rem(z + 1, NZ)

        def get(ref, k, zz):
            return ref[pl.ds(pl.multiple_of((k * NZ + zz) * CX, CX), CX), :]

        ks = range(8)
        f = [None if k == 6 else get(fz_ref, k, z) for k in ks]
        fn = [None if k == 6 else get(fz_ref, k, zn) for k in ks]
        return face([get(u_ref, k, z) for k in ks], [get(u_ref, k, zn) for k in ks], f, fn,
                    get(sz_ref, 0, z), get(sz_ref, 0, zn))

    def finish(z, before):
        here = zface(z)
        for k in range(8):
            at = pl.ds(pl.multiple_of((k * NZ + z) * CX, CX), CX)
            adv_ref[at, :] = u_ref[at, :] - TIME_STEP * (ch_ref[at, :] + (here[k] - before[k]))
        return tuple(here)

    lax.fori_loop(0, NZ, finish, tuple(zface(NZ - 1)))


def edge_kernel(bricks_ref, count_ref, prim_ref, advin_ref, kapin_ref, py_ref,
                xlo_ref, xhi_ref, yfl_ref, yfr_ref, wb_ref, w1_ref, w2_ref, wo_ref,
                adv_ref, kap_ref, ylo_ref, yhi_ref, sxlo_ref, sxhi_ref,
                x_ref, yh_ref, d_ref):
    load = plane_loader(prim_ref)
    lane8 = iota((8, LANES), 1)
    side0 = lane8 % 2 == 0
    last_lane = jnp.where(lane8 == LANES - 1, 1, 0)
    on_edge = jnp.logical_or(lane8 == 0, lane8 == LANES - 1)

    halo, own = [], []
    for f in range(8):
        at = pl.ds(f * 8, 8)
        h = jnp.where(side0, next_lane(yfl_ref[at, :]), prev_lane(yfr_ref[at, :]))
        yh_ref[at, :] = h
        halo.append(h)
        own.append(py_ref[at, :])
    uh, fh, sh = derive(halo)
    uo, fo, so = derive(own)

    def pair(a, b):
        return [None if p is None else jnp.where(side0, p, q) for p, q in zip(a, b)]

    fc = face(pair(uh, uo), pair(uo, uh), pair(fh[1], fo[1]), pair(fo[1], fh[1]),
              jnp.where(side0, sh[1], so[1]), jnp.where(side0, so[1], sh[1]))
    for c in range(8):
        d_ref[pl.ds(c * 8, 8), :] = jnp.where(side0, TIME_STEP, -TIME_STEP) * fc[c]

    @pl.loop(0, NZ)
    def _(z):
        for c in range(8):
            delta = d_ref[pl.ds(c * 8, 8), :]
            for o in range(2):
                at = pl.ds(pl.multiple_of((c * NZ + z) * CX + o * 8, 8), 8)
                g = take(delta, (o * NZ + z) * 2 + last_lane)
                adv_ref[at, :] = advin_ref[at, :] + jnp.where(on_edge, g, 0.0)

    for k in range(NZ // 8):
        zs = k * 8
        for lo in (True, False):
            start = 0 if lo else CX - 1
            ref = xlo_ref if lo else xhi_ref
            rows = [pl.ds(f * PLANE + zs * CX + start, 8, stride=CX) for f in range(8)]
            uo, fo, so = derive([prim_ref[r, :] for r in rows])
            uh, fh, sh = derive([ref[pl.ds(f * NZ + zs, 8), :].astype(F32) for f in range(8)])
            if lo:
                fc = face(uh, uo, fh[0], fo[0], sh[0], so[0])
            else:
                fc = face(uo, uh, fo[0], fh[0], so[0], sh[0])
            for c in range(8):
                step = TIME_STEP * fc[c]
                adv_ref[rows[c], :] = adv_ref[rows[c], :] + (step if lo else -step)

    source, half, back = brick_rows(bricks_ref, count_ref)
    tail = bias_rows(LANES)
    index = edge_lane_index()
    sub = iota((8, LANES), 0)

    def patch_x(f, z):
        return (xlo_ref[pl.ds(f * NZ + z, 1), :].astype(F32), xhi_ref[pl.ds(f * NZ + z, 1), :].astype(F32))

    def patch_y(f, z):
        h = yh_ref[pl.ds(f * 8, 8), :]
        return jnp.concatenate([take(h, (o * NZ + z) * 2 + last_lane) for o in range(2)], axis=0)

    def gather_edges(z, acc):
        sets = []
        for zz in (z, z + NZ // 2):
            fs = features(load, zz, patch_x, patch_y)
            for o in range(2):
                acc = tuple(
                    jnp.where(lane8 // 2 == o * NZ + zz, take(v[o * 8 : o * 8 + 8], index), a)
                    for v, a in zip(fs, acc))
            sets.append([jnp.where(sub == 7, v[8:16], v[0:8]) for v in fs])
        parts = [jnp.where(half == 1, take(b, source), take(a, source)) for a, b in zip(*sets)]
        at = pl.ds(pl.multiple_of(z * LANES, LANES), LANES)
        x_ref[:, at] = jnp.concatenate(parts + [tail], axis=0).astype(BF16)
        return acc

    zero = jnp.zeros((8, LANES), F32)
    acc = lax.fori_loop(0, NZ // 2, gather_edges, (zero,) * 8)
    w1, w2, wo = w1_ref[...], w2_ref[...], wo_ref[...]
    ycells = jnp.concatenate(list(acc) + [tail], axis=0).astype(BF16)
    xcells = x_ref[...]
    us = [jnp.dot(wb_ref[pl.ds(s * HID, HID), :], xcells, preferred_element_type=F32)
          for s in (0, 7)]
    uy = jnp.dot(wb_ref[...], ycells, preferred_element_type=F32)
    us.append(jnp.concatenate([uy[s * HID : (s + 1) * HID] for s in range(8)], axis=1))
    r0, r7, ry = closure_rates(us, w1, w2, wo)
    kapy = ry[:8, 0:LANES]
    for s in range(1, 8):
        kapy = jnp.where(sub == s, ry[:8, s * LANES : (s + 1) * LANES], kapy)
    for z in range(NZ // 2):
        at = slice(z * LANES, (z + 1) * LANES)
        for o in range(2):
            k = kapin_ref[pl.ds(z * CX + o * 8, 8), :]
            k = jnp.where(sub == 0, r0[:8, at], k) if o == 0 else jnp.where(sub == 7, r7[:8, at], k)
            for h in range(2):
                zz = z + h * (NZ // 2)
                listed = back[h] >= 0
                full = take(k, jnp.where(listed, back[h], 0))
                edge = take(kapy, (o * NZ + zz) * 2 + last_lane)
                full = jnp.where(on_edge, edge, full)
                kap_ref[pl.ds(zz * CX + o * 8, 8), :] = jnp.where(listed, full, RATE_LOW)

    low4 = lane8 % 4
    high4 = LANES - 4 + low4
    for f in range(4):
        src, base = (adv_ref, (4 + f) * PLANE) if f < 3 else (kap_ref, 0)
        lows, highs = [], []
        for o in range(2):
            lo = jnp.zeros((8, LANES), F32)
            hi = jnp.zeros((8, LANES), F32)
            for z in range(NZ):
                v = src[pl.ds(base + z * CX + o * 8, 8), :]
                mine = lane8 // 4 == z
                lo = jnp.where(mine, take(v, low4), lo)
                hi = jnp.where(mine, take(v, high4), hi)
            lows.append(lo)
            highs.append(hi)
        ylo_ref[pl.ds(f * CX, CX), :] = jnp.concatenate(lows, axis=0).astype(BF16)
        yhi_ref[pl.ds(f * CX, CX), :] = jnp.concatenate(highs, axis=0).astype(BF16)
        for r in range(4):
            at = pl.ds((f * 4 + r) * NZ, NZ)
            sxlo_ref[at, :] = src[pl.ds(base + r, NZ, stride=CX), :].astype(BF16)
            sxhi_ref[at, :] = src[pl.ds(base + CX - 4 + r, NZ, stride=CX), :].astype(BF16)


DEEP = CX + 8
YG = NZ // 4


def diffuse_kernel(adv_ref, kap_ref, xlo_ref, xhi_ref, ylo_ref, yhi_ref, out_ref,
                   m0, m1, km, y0, y1, ky, xl, xh, yl, yh):
    comp = pl.program_id(0)
    lane = iota((8, LANES), 1)
    sub = iota((8, LANES), 0)
    window = lane % 32
    block = lane // 32
    own_index = jnp.maximum(jnp.where(window < 16, window - 4, window + 100), 0)
    own_index = jnp.minimum(own_index, LANES - 1)

    def build(field, own_ref, main, edge):
        base = field * (4 * NZ)
        for z in range(NZ):
            main[pl.ds(z * DEEP, CX), :] = own_ref[pl.ds(z * CX, CX), :]
        for r in range(4):
            at = pl.ds(pl.multiple_of(base + r * NZ, 8), NZ)
            main[pl.ds(CX + r, NZ, stride=DEEP), :] = xh[at, :]
            main[pl.ds(CX + 4 + r, NZ, stride=DEEP), :] = xl[at, :]
        for o in range(3):
            if o < 2:
                at = pl.ds(pl.multiple_of(field * CX + o * 8, 8), 8)
                left, right = yl[at, :], yh[at, :]
            else:
                at = pl.ds(pl.multiple_of(16 * NZ + field * 8, 8), 8)
                left = jnp.where(sub < 4, xh[at, :], xl[at, :])
                at = pl.ds(pl.multiple_of(16 * NZ + 32 + field * 8, 8), 8)
                right = jnp.where(sub < 4, xh[at, :], xl[at, :])
            for g in range(YG):
                v = jnp.zeros((8, LANES), F32)
                for b in range(4):
                    piece = main[pl.ds((b * YG + g) * DEEP + o * 8, 8), :]
                    v = jnp.where(block == b, take(piece, own_index), v)
                v = jnp.where(window < 4, pltpu.roll(left, (LANES - 4 * g) % LANES, 1), v)
                v = jnp.where(window >= 28, pltpu.roll(right, (28 + LANES - 4 * g) % LANES, 1), v)
                edge[pl.ds(g * DEEP + o * 8, 8), :] = v

    @pl.when(comp == 0)
    def _():
        xl[...] = xlo_ref[...].astype(F32)
        xh[...] = xhi_ref[...].astype(F32)
        yl[...] = ylo_ref[...].astype(F32)
        yh[...] = yhi_ref[...].astype(F32)
        build(3, kap_ref, km, ky)

    build(comp, adv_ref, m0, y0)

    def relax(c, up, dn, k):
        total = next_row(c) + prev_row(c) + next_lane(c) + prev_lane(c) + (up + dn)
        return c + k * (total - 6.0 * c)

    mains, edges = (m0, m1), (y0, y1)
    for step in range(SUB):
        a, b = mains[step % 2], mains[1 - step % 2]
        ea, eb = edges[step % 2], edges[1 - step % 2]

        def at(z):
            return pl.ds(pl.multiple_of(z * DEEP, 8), DEEP)

        @pl.loop(0, NZ)
        def _(z):
            zn, zp = lax.rem(z + 1, NZ), lax.rem(z + NZ - 1, NZ)
            b[at(z), :] = relax(a[at(z), :], a[at(zn), :], a[at(zp), :], km[at(z), :])

        for g in range(YG):
            up = ea[at(g + 1), :] if g + 1 < YG else pltpu.roll(ea[at(0), :], LANES - 32, 1)
            dn = ea[at(g - 1), :] if g > 0 else pltpu.roll(ea[at(YG - 1), :], 32, 1)
            eb[at(g), :] = relax(ea[at(g), :], up, dn, ky[at(g), :])

    main, edge = mains[SUB % 2], edges[SUB % 2]
    on_edge = jnp.logical_or(lane < 4, lane >= LANES - 4)
    for z in range(NZ):
        b, g = z // YG, z % YG
        index = jnp.where(lane < 4, b * 32 + 4 + lane, b * 32 + 24 + lane - (LANES - 4))
        index = jnp.minimum(jnp.maximum(index, 0), LANES - 1)
        for o in range(2):
            e = take(edge[pl.ds(g * DEEP + o * 8, 8), :], index)
            out_ref[pl.ds(z * CX + o * 8, 8), :] = jnp.where(
                on_edge, e, main[pl.ds(z * DEEP + o * 8, 8), :])


def struct(shape, dtype=F32):
    return jax.ShapeDtypeStruct(shape, dtype)


def params():
    return pltpu.CompilerParams(vmem_limit_bytes=VMEM_LIMIT)


VSPEC = pl.BlockSpec(memory_space=pltpu.VMEM)
SSPEC = pl.BlockSpec(memory_space=pltpu.SMEM)


def step_up(axis):
    n = lax.axis_size(axis)
    return [(i, (i + 1) % n) for i in range(n)]


def step_down(axis):
    n = lax.axis_size(axis)
    return [((i + 1) % n, i) for i in range(n)]


def shards(primitive, current_sheet_bricks, brick_count, w_in, w_hid, w_out, b_hid):
    shape = primitive.shape
    prim = primitive.reshape(8 * PLANE, LANES)
    bricks = current_sheet_bricks.reshape(1, -1)
    count = brick_count.reshape(1, 1)

    lo, hi, py = pl.pallas_call(
        pack_kernel,
        out_shape=[struct((8 * NZ, LANES)), struct((8 * NZ, LANES)), struct((64, LANES))],
        compiler_params=params(),
        name="pack",
    )(prim)
    yfl = lax.ppermute(py, "row", step_up("row"))
    yfr = lax.ppermute(py, "row", step_down("row"))
    xlo = lax.ppermute(hi, "col", step_up("col"))
    xhi = lax.ppermute(lo, "col", step_down("col"))

    weights = [struct((8 * HID, KIN), BF16), struct((HID, KHID), BF16), struct((HID, KHID), BF16),
               struct((16, HID), BF16)]
    adv, kap, wb, w1, w2, wo = pl.pallas_call(
        main_kernel,
        in_specs=[SSPEC, SSPEC] + [VSPEC] * 5,
        out_shape=[struct((8 * PLANE, LANES)), struct((NZ // 2 * CX, LANES))] + weights,
        scratch_shapes=[pltpu.VMEM((2 * KIN, NZ // 2 * LANES), BF16),
                        pltpu.VMEM((8 * PLANE, LANES), F32), pltpu.VMEM((8 * PLANE, LANES), F32),
                        pltpu.VMEM((PLANE, LANES), F32), pltpu.VMEM((8 * PLANE, LANES), F32)],
        compiler_params=params(),
        cost_estimate=pl.CostEstimate(flops=6_000_000_000, bytes_accessed=4 << 20, transcendentals=0),
        name="bulk",
    )(bricks, count, prim, w_in, w_hid.reshape(2 * HID, HID), w_out.reshape(1, HID), b_hid)

    adv, kap, ylo, yhi, sxlo, sxhi = pl.pallas_call(
        edge_kernel,
        in_specs=[SSPEC, SSPEC] + [VSPEC] * 12,
        out_shape=[struct((8 * PLANE, LANES)), struct((PLANE, LANES)),
                   struct((4 * CX, LANES), BF16), struct((4 * CX, LANES), BF16),
                   struct((16 * NZ, LANES), BF16), struct((16 * NZ, LANES), BF16)],
        scratch_shapes=[pltpu.VMEM((KIN, NZ // 2 * LANES), BF16), pltpu.VMEM((64, LANES), F32),
                        pltpu.VMEM((64, LANES), F32)],
        compiler_params=params(),
        name="edges",
    )(bricks, count, prim, adv, kap, py, xlo, xhi, yfl, yfr, wb, w1, w2, wo)

    hlo = lax.ppermute(yhi, "row", step_up("row"))
    hhi = lax.ppermute(ylo, "row", step_down("row"))

    def with_corners(rows, start):
        parts = [h.reshape(4, CX, LANES)[:, start : start + 8].reshape(32, LANES) for h in (hlo, hhi)]
        return jnp.concatenate([rows] + parts, axis=0)

    dhi = lax.ppermute(with_corners(sxlo, 0), "col", step_down("col"))
    dlo = lax.ppermute(with_corners(sxhi, 8), "col", step_up("col"))

    full = lambda rows: pl.BlockSpec((rows, LANES), lambda c: (0, 0))
    part = pl.BlockSpec((PLANE, LANES), lambda c: (4 + c, 0))
    xrows = 16 * NZ + 64
    out = pl.pallas_call(
        diffuse_kernel,
        grid=(3,),
        in_specs=[part, full(PLANE), full(xrows), full(xrows), full(4 * CX), full(4 * CX)],
        out_specs=part,
        out_shape=struct((8 * PLANE, LANES)),
        input_output_aliases={0: 0},
        scratch_shapes=[pltpu.VMEM((NZ * DEEP, LANES), F32)] * 3
        + [pltpu.VMEM((YG * DEEP, LANES), F32)] * 3
        + [pltpu.VMEM((xrows, LANES), F32)] * 2
        + [pltpu.VMEM((4 * CX, LANES), F32)] * 2,
        compiler_params=params(),
        name="diffuse",
    )(adv, kap, dlo, dhi, hlo, hhi)
    return out.reshape(shape)


def solution(mesh):
    return jax.shard_map(
        shards,
        mesh=mesh,
        in_specs=(
            P(None, None, "col", "row"),
            P("row", "col", None),
            P("row", "col"),
            P(),
            P(),
            P(),
            P(),
        ),
        out_specs=P(None, None, "col", "row"),
        check_vma=False,
    )
```

profile of v0, /device:TPU:0, one launch (start us, length us, event | category | flops | bytes accessed | tf_op | source)
XLA Modules:
  0.0 86.3 jit_solution(3996805872411285071)
XLA Ops:
  0.0 1.6 %copy-done = f32[8,32,16,128]{3,2,1,0:T(8,128)S(1)} copy-done((f32[8,32,16,128]{3,2,1,0:T(8,128)S(1)}, f32[8,32,16,128]{3,2,1,0:T(8,128)}, u32[]{:S(2)}) %copy-start) | copy-done | bytes 2097176
  1.6 0.6 pack.1
  2.2 5.1 %collective-permute-start.3 = (f32[64,128]{1,0:T(8,128)S(1)}, f32[64,128]{1,0:T(8,128)S(1)}, u32[]{:S(2)}, u32[]{:S(2)}) collective-permute-start(f32[64,128]{1,0:T(8,128)S(1)} %get-tuple-element.22.py_ref), channel_id=1, source_target_pairs={{8,0},{16,8},{24,16},{0,24},{9,1},{17,9},{25,17},{1,25},{10,2},{18... | collective-permute-start | bytes 98312 | tf_op jit(solution)/shard_map/ppermute | solution.py:542
  7.4 0.0 collective-permute-start.2
  7.4 0.0 collective-permute-start
  7.4 2.6 %collective-permute-start.1 = (f32[256,128]{1,0:T(8,128)S(1)}, f32[256,128]{1,0:T(8,128)S(1)}, u32[]{:S(2)}, u32[]{:S(2)}) collective-permute-start(f32[256,128]{1,0:T(8,128)S(1)} %get-tuple-element.24), channel_id=1, source_target_pairs={{1,0},{2,1},{3,2},{4,3},{5,4},{6,5},{7,6},{0,7},{9,8},{10,9},{11,1... | collective-permute-start | bytes 393224 | tf_op jit(solution)/shard_map/ppermute | solution.py:544
  10.7 0.0 copy-done.6
  10.7 0.0 copy-start.3
  10.7 0.8 copy-done.3
  11.5 18.8 %bulk.1 = (f32[4096,128]{1,0:T(8,128)S(1)}, f32[256,128]{1,0:T(8,128)S(1)}, bf16[1024,80]{1,0:T(8,128)(2,1)S(1)}, bf16[128,144]{1,0:T(8,128)(2,1)S(1)}, bf16[128...) custom-call(s32[1,8]{1,0:T(1,128)S(1)} %bitcast.20, s32[1,1]{1,0:T(1,128)S(6)} %copy.10.count_ref, ...), custom_call_target="tpu_custom_call" | custom-call | flops 6000000000 | bytes 4194304 | tf_op jit(solution)/shard_map/bulk/pallas_call | solution.py:548
  30.4 0.0 collective-permute-done.3.yfr_ref
  30.4 0.0 collective-permute-done.2.yfl_ref
  30.4 0.0 collective-permute-done.xlo_ref
  30.4 0.0 collective-permute-done.1.xhi_ref
  30.4 9.8 %edges.1 = (f32[4096,128]{1,0:T(8,128)}, f32[512,128]{1,0:T(8,128)S(1)}, bf16[64,128]{1,0:T(8,128)(2,1)S(1)}, bf16[64,128]{1,0:T(8,128)(2,1)S(1)}, bf16[512,128]...) custom-call(s32[1,8]{1,0:T(1,128)S(1)} %bitcast.21, s32[1,1]{1,0:T(1,128)S(6)} %copy.10.count_ref, ...), custom_call_target="tpu_custom_call" | custom-call | tf_op jit(solution)/shard_map/edges/pallas_call | solution.py:560
  40.3 0.1 collective-permute-start.4
  40.3 3.9 %collective-permute-start.5 = (bf16[64,128]{1,0:T(8,128)(2,1)S(1)}, bf16[64,128]{1,0:T(8,128)(2,1)S(1)}, u32[]{:S(2)}, u32[]{:S(2)}) collective-permute-start(bf16[64,128]{1,0:T(8,128)(2,1)S(1)} %get-tuple-element.33), channel_id=1, source_target_pairs={{8,0},{16,8},{24,16},{0,24},{9,1},{17,9},{25,17},{1,25},{10,2},{18... | collective-permute-start | bytes 49160 | tf_op jit(solution)/shard_map/ppermute | solution.py:573
  44.2 1.7 %collective-permute-done.4.ylo_ref = bf16[64,128]{1,0:T(8,128)(2,1)S(1)} collective-permute-done((bf16[64,128]{1,0:T(8,128)(2,1)S(1)}, bf16[64,128]{1,0:T(8,128)(2,1)S(1)}, u32[]{:S(2)}, u32[]{:S(2)}) %collective-permute-start.4) | collective-permute-done | bytes 16416 | tf_op jit(solution)/shard_map/ppermute | solution.py:572
  45.9 0.0 collective-permute-done.5.yhi_ref
  45.9 0.1 collective-permute-start.6
  46.0 2.7 %collective-permute-start.7 = (bf16[576,128]{1,0:T(8,128)(2,1)S(1)}, bf16[576,128]{1,0:T(8,128)(2,1)S(1)}, u32[]{:S(2)}, u32[]{:S(2)}) collective-permute-start(bf16[576,128]{1,0:T(8,128)(2,1)S(1)} %pad_maximum_fusion.1), channel_id=1, source_target_pairs={{1,0},{2,1},{3,2},{4,3},{5,4},{6,5},{7,6},{0,7},{9,8},{10,9},{11,1... | collective-permute-start | bytes 442376 | tf_op jit(solution)/shard_map/ppermute | solution.py:579
  48.7 3.3 %collective-permute-done.6.xlo_ref = bf16[576,128]{1,0:T(8,128)(2,1)S(1)} collective-permute-done((bf16[576,128]{1,0:T(8,128)(2,1)S(1)}, bf16[576,128]{1,0:T(8,128)(2,1)S(1)}, u32[]{:S(2)}, u32[]{:S(2)}) %collective-permute-start.6) | collective-permute-done | bytes 147488 | tf_op jit(solution)/shard_map/ppermute | solution.py:580
  52.0 0.0 collective-permute-done.7.xhi_ref
  52.0 34.3 %diffuse.1 = f32[4096,128]{1,0:T(8,128)} custom-call(f32[4096,128]{1,0:T(8,128)} %get-tuple-element.29.adv_ref, f32[512,128]{1,0:T(8,128)S(1)} %get-tuple-element.30.kap_ref, bf16[576,128]{1,0:T(8,128)(2,1)S(1)} %collective-permute-done.6.xlo_ref, bf16[576,128]{1,0:T(8,128)(2,1)S(1)} %collective-permute-done.7.xhi_ref, ...), custom_call_target="tpu_custom_call", output_to_operand_aliasing={{}: (0, {})} | custom-call | tf_op jit(solution)/shard_map/diffuse/pallas_call | solution.py:585
  (14 shorter events, 0.0 us)
Async XLA Ops:
  0.0 10.7 %copy-start.6 = (bf16[128]{0:T(256)(128)(2,1)S(1)}, bf16[128]{0:T(256)(128)(2,1)}, u32[]{:S(2)}) copy-start(bf16[128]{0:T(256)(128)(2,1)} %param.12) | copy-start | bytes 772
  0.0 10.7 %copy-start.2 = (s32[1,1,8]{2,1,0:T(1,128)S(1)}, s32[1,1,8]{2,1,0:T(1,128)}, u32[]{:S(2)}) copy-start(s32[1,1,8]{2,1,0:T(1,128)} %param.8) | copy-start | bytes 100
  0.0 1.6 %copy-start = (f32[8,32,16,128]{3,2,1,0:T(8,128)S(1)}, f32[8,32,16,128]{3,2,1,0:T(8,128)}, u32[]{:S(2)}) copy-start(f32[8,32,16,128]{3,2,1,0:T(8,128)} %param.7) | copy-start | bytes 6291460
  1.6 9.1 %copy-start.1 = (f32[8,32,16,128]{3,2,1,0:T(8,128)S(1)}, f32[8,32,16,128]{3,2,1,0:T(8,128)}, u32[]{:S(2)}) copy-start(f32[8,32,16,128]{3,2,1,0:T(8,128)} %param.7) | copy-start | bytes 6291460
  1.6 9.1 %copy-start.4 = (bf16[8,128]{1,0:T(8,128)(2,1)S(1)}, bf16[8,128]{1,0:T(8,128)(2,1)}, u32[]{:S(2)}) copy-start(bf16[8,128]{1,0:T(8,128)(2,1)} %win_ref.1) | copy-start | bytes 6148
  1.6 9.1 %copy-start.5 = (f32[3,128]{1,0:T(4,128)S(1)}, f32[3,128]{1,0:T(4,128)}, u32[]{:S(2)}) copy-start(f32[3,128]{1,0:T(4,128)} %bias_ref.1) | copy-start | bytes 4612
  2.2 28.1 %collective-permute-start.3 = (f32[64,128]{1,0:T(8,128)S(1)}, f32[64,128]{1,0:T(8,128)S(1)}, u32[]{:S(2)}, u32[]{:S(2)}) collective-permute-start(f32[64,128]{1,0:T(8,128)S(1)} %get-tuple-element.22.py_ref), channel_id=1, source_target_pairs={{8,0},{16,8},{24,16},{0,24},{9,1},{17,9},{25,17},{1,25},{10,2},{18... | collective-permute-start | bytes 98312 | tf_op jit(solution)/shard_map/ppermute | solution.py:542
  7.4 23.1 %collective-permute-start.2 = (f32[64,128]{1,0:T(8,128)S(1)}, f32[64,128]{1,0:T(8,128)S(1)}, u32[]{:S(2)}, u32[]{:S(2)}) collective-permute-start(f32[64,128]{1,0:T(8,128)S(1)} %get-tuple-element.22.py_ref), channel_id=1, source_target_pairs={{0,8},{8,16},{16,24},{24,0},{1,9},{9,17},{17,25},{25,1},{2,10},{10... | collective-permute-start | bytes 98312 | tf_op jit(solution)/shard_map/ppermute | solution.py:541
  7.4 23.1 %collective-permute-start = (f32[256,128]{1,0:T(8,128)S(1)}, f32[256,128]{1,0:T(8,128)S(1)}, u32[]{:S(2)}, u32[]{:S(2)}) collective-permute-start(f32[256,128]{1,0:T(8,128)S(1)} %get-tuple-element.23), channel_id=1, source_target_pairs={{0,1},{1,2},{2,3},{3,4},{4,5},{5,6},{6,7},{7,0},{8,9},{9,10},{10,1... | collective-permute-start | bytes 393224 | tf_op jit(solution)/shard_map/ppermute | solution.py:543
  7.4 23.1 %collective-permute-start.1 = (f32[256,128]{1,0:T(8,128)S(1)}, f32[256,128]{1,0:T(8,128)S(1)}, u32[]{:S(2)}, u32[]{:S(2)}) collective-permute-start(f32[256,128]{1,0:T(8,128)S(1)} %get-tuple-element.24), channel_id=1, source_target_pairs={{1,0},{2,1},{3,2},{4,3},{5,4},{6,5},{7,6},{0,7},{9,8},{10,9},{11,1... | collective-permute-start | bytes 393224 | tf_op jit(solution)/shard_map/ppermute | solution.py:544
  10.7 0.8 copy-start.3
  40.3 5.6 %collective-permute-start.4 = (bf16[64,128]{1,0:T(8,128)(2,1)S(1)}, bf16[64,128]{1,0:T(8,128)(2,1)S(1)}, u32[]{:S(2)}, u32[]{:S(2)}) collective-permute-start(bf16[64,128]{1,0:T(8,128)(2,1)S(1)} %get-tuple-element.32), channel_id=1, source_target_pairs={{0,8},{8,16},{16,24},{24,0},{1,9},{9,17},{17,25},{25,1},{2,10},{10... | collective-permute-start | bytes 49160 | tf_op jit(solution)/shard_map/ppermute | solution.py:572
  40.3 5.5 %collective-permute-start.5 = (bf16[64,128]{1,0:T(8,128)(2,1)S(1)}, bf16[64,128]{1,0:T(8,128)(2,1)S(1)}, u32[]{:S(2)}, u32[]{:S(2)}) collective-permute-start(bf16[64,128]{1,0:T(8,128)(2,1)S(1)} %get-tuple-element.33), channel_id=1, source_target_pairs={{8,0},{16,8},{24,16},{0,24},{9,1},{17,9},{25,17},{1,25},{10,2},{18... | collective-permute-start | bytes 49160 | tf_op jit(solution)/shard_map/ppermute | solution.py:573
  45.9 6.1 %collective-permute-start.6 = (bf16[576,128]{1,0:T(8,128)(2,1)S(1)}, bf16[576,128]{1,0:T(8,128)(2,1)S(1)}, u32[]{:S(2)}, u32[]{:S(2)}) collective-permute-start(bf16[576,128]{1,0:T(8,128)(2,1)S(1)} %pad_maximum_fusion), channel_id=1, source_target_pairs={{0,1},{1,2},{2,3},{3,4},{4,5},{5,6},{6,7},{7,0},{8,9},{9,10},{10,1... | collective-permute-start | bytes 442376 | tf_op jit(solution)/shard_map/ppermute | solution.py:580
  46.0 6.0 %collective-permute-start.7 = (bf16[576,128]{1,0:T(8,128)(2,1)S(1)}, bf16[576,128]{1,0:T(8,128)(2,1)S(1)}, u32[]{:S(2)}, u32[]{:S(2)}) collective-permute-start(bf16[576,128]{1,0:T(8,128)(2,1)S(1)} %pad_maximum_fusion.1), channel_id=1, source_target_pairs={{1,0},{2,1},{3,2},{4,3},{5,4},{6,5},{7,6},{0,7},{9,8},{10,9},{11,1... | collective-permute-start | bytes 442376 | tf_op jit(solution)/shard_map/ppermute | solution.py:579
where the time goes:
time: 86.9 us; the launch traced here: 86.3 us
  Pallas kernels  63.6 us (73%)
  starting transfers between devices  14.4 us (17%)
  waiting for transfers between devices  4.99 us (6%)
  local copies, waits for them, and re-layouts  2.48 us (3%)
    pallas_call x1, Pallas kernels, shards(): pl.pallas_call(diffuse_kernel, grid=(3,), in_specs=[part, full(PLANE), fu...  34.3 us
    pallas_call x1, Pallas kernels, shards(): pl.pallas_call(main_kernel, in_specs=[SSPEC, SSPEC] + [VSPEC] * 5, out_sh...  18.8 us
    pallas_call x1, Pallas kernels, shards(): pl.pallas_call(edge_kernel, in_specs=[SSPEC, SSPEC] + [VSPEC] * 12, out_s...  9.84 us
    ppermute x1, starting transfers between devices, shards(): yfr = lax.ppermute(py, 'row', step_down('row'))  5.1 us
    ppermute x1, starting transfers between devices, shards(): hhi = lax.ppermute(ylo, 'row', step_down('row'))  3.88 us
    ppermute x1, waiting for transfers between devices, shards(): dlo = lax.ppermute(with_corners(sxhi, 8), 'col', step_up('col'))  3.33 us
    ppermute x1, starting transfers between devices, shards(): dhi = lax.ppermute(with_corners(sxlo, 0), 'col', step_down('col'))  2.68 us
    ppermute x1, starting transfers between devices, shards(): xhi = lax.ppermute(lo, 'col', step_down('col'))  2.64 us
  transfers between devices with their start and end apart: 8, of which 2 were waited for; matrix products, arithmetic and copies ran while one was open for 0% of the time, Pallas kernels for 22%

commit v1 on v0

v1 whole, which is shorter than its diff:
```python
import jax
import jax.numpy as jnp
from jax import lax
from jax.experimental import pallas as pl
from jax.experimental.pallas import tpu as pltpu
from jax.sharding import PartitionSpec as P

BRICK = 16
SUB = 4
ADIABATIC = 5.0 / 3.0
TIME_STEP = 0.02
RATE_LOW = 0.02
RATE_SPAN = 0.14
GELU_A = 0.7978845608
GELU_B = 0.7978845608 * 0.044715
F32 = jnp.float32
BF16 = jnp.bfloat16
LANES = 128
NZ = 32
CX = 16
HID = 128
PLANE = NZ * CX
KIN = 80
KHID = HID + 16
VMEM_LIMIT = 48 << 20


def iota(shape, dim):
    return lax.broadcasted_iota(jnp.int32, shape, dim)


def take(values, index):
    return jnp.take_along_axis(values, index, axis=1, mode="promise_in_bounds")


def next_row(v):
    return pltpu.roll(v, v.shape[0] - 1, 0)


def prev_row(v):
    return pltpu.roll(v, 1, 0)


def next_lane(v):
    return pltpu.roll(v, v.shape[1] - 1, 1)


def prev_lane(v):
    return pltpu.roll(v, 1, 1)


def derive(p):
    rho, pr = p[0], p[7]
    v, b = p[1:4], p[4:7]
    m = [rho * c for c in v]
    b2 = b[0] * b[0] + b[1] * b[1] + b[2] * b[2]
    v2 = v[0] * v[0] + v[1] * v[1] + v[2] * v[2]
    vb = v[0] * b[0] + v[1] * b[1] + v[2] * b[2]
    pt = pr + 0.5 * b2
    en = 1.5 * pr + 0.5 * (rho * v2 + b2)
    fast = jnp.sqrt((ADIABATIC * pr + b2) / rho)
    ep = en + pt
    tens = {(i, j): m[i] * v[j] - b[i] * b[j] for i in range(3) for j in range(i, 3)}
    elec = {(i, j): v[i] * b[j] - b[i] * v[j] for i in range(3) for j in range(i + 1, 3)}
    fluxes = []
    for d in range(3):
        rows = [m[d]]
        for c in range(3):
            t = tens[(min(c, d), max(c, d))]
            rows.append(t + pt if c == d else t)
        for c in range(3):
            rows.append(None if c == d else (elec[(d, c)] if d < c else -elec[(c, d)]))
        rows.append(ep * v[d] - b[d] * vb)
        fluxes.append(rows)
    speeds = [jnp.abs(c) + fast for c in v]
    return [rho] + m + list(b) + [en], fluxes, speeds


def face(rows, u, un, f, fn, s, sn):
    a = 0.5 * jnp.maximum(s, sn)
    out = {}
    for c in rows:
        diss = a * (un[c] - u[c])
        out[c] = -diss if f[c] is None else 0.5 * (f[c] + fn[c]) - diss
    return out


def gelu_twice(u):
    u = u.astype(BF16)
    t = jnp.tanh(u * (jnp.asarray(GELU_A, BF16) + jnp.asarray(GELU_B, BF16) * (u * u)))
    return u + u * t


def closure_rates(first, w1, w2, wo):
    us = first
    for w in (w1, w2):
        hs = [jnp.concatenate([gelu_twice(u), bias_rows(u.shape[1]).astype(BF16)], axis=0) for u in us]
        us = [jnp.dot(w, h, preferred_element_type=F32) for h in hs]
    hs = [gelu_twice(u) for u in us]
    scores = [jnp.dot(wo, h, preferred_element_type=F32) for h in hs]
    return [(RATE_LOW + 0.5 * RATE_SPAN) + (0.5 * RATE_SPAN) * jnp.tanh(0.5 * s) for s in scores]


def features(load, z, patch_x=None, patch_y=None):
    zn, zp = lax.rem(z + 1, NZ), lax.rem(z + NZ - 1, NZ)
    row, lane = iota((CX, LANES), 0), iota((CX, LANES), 1)

    def dx(f, v):
        up, dn = next_row(v), prev_row(v)
        if patch_x is not None:
            lo, hi = patch_x(f, z)
            up = jnp.where(row == CX - 1, hi, up)
            dn = jnp.where(row == 0, lo, dn)
        return 0.5 * (up - dn)

    def dy(f, v):
        up, dn = next_lane(v), prev_lane(v)
        if patch_y is not None:
            edge = patch_y(f, z)
            up = jnp.where(lane == LANES - 1, edge, up)
            dn = jnp.where(lane == 0, edge, dn)
        return 0.5 * (up - dn)

    def dz(f):
        return 0.5 * (load(f, zn) - load(f, zp))

    rho, vx, vy, vz, bx, by, bz, pr = [load(f, z) for f in range(8)]
    jx = dy(6, bz) - dz(5)
    jy = dz(4) - dx(6, bz)
    jz = dx(5, by) - dy(4, bx)
    div = dx(1, vx) + dy(2, vy) + dz(3)
    return [jx, jy, jz, div, rho, pr, bx * bx + by * by + bz * bz, vx * vx + vy * vy + vz * vz]


def bias_rows(n):
    return jnp.where(iota((16, n), 0) < 3, 1.0, 0.0)


def plane_at(f, z):
    return pl.ds(pl.multiple_of((f * NZ + z) * CX, CX), CX)


def plane_loader(prim_ref):
    def load(f, z):
        return prim_ref[plane_at(f, z), :]

    return load


def pack_kernel(prim_ref, lo_ref, hi_ref, py_ref):
    lane = iota((8, LANES), 1)
    index = jnp.where(lane % 2 == 0, 0, LANES - 1)
    for f in range(8):
        lo_ref[pl.ds(f * NZ, NZ), :] = prim_ref[pl.ds(f * PLANE, NZ, stride=CX), :]
        hi_ref[pl.ds(f * NZ, NZ), :] = prim_ref[pl.ds(f * PLANE + CX - 1, NZ, stride=CX), :]
        acc = jnp.zeros((8, LANES), F32)
        for z in range(NZ):
            for o in range(2):
                v = prim_ref[pl.ds((f * NZ + z) * CX + o * 8, 8), :]
                acc = jnp.where(lane // 2 == o * NZ + z, take(v, index), acc)
        py_ref[pl.ds(f * 8, 8), :] = acc


def brick_rows(bricks_ref, count_ref):
    lane = iota((8, LANES), 1)
    slot, inner = lane // BRICK, lane % BRICK
    source = jnp.zeros((8, LANES), jnp.int32)
    half = jnp.zeros((8, LANES), jnp.int32)
    back = [jnp.full((8, LANES), -1, jnp.int32) for _ in range(2)]
    per_half = LANES // BRICK
    ends = [[0, 0], [0, 0]]
    for j in range(8):
        b = bricks_ref[0, j]
        bz, by = b // per_half, b % per_half
        source = jnp.where(slot == j, by * BRICK + inner, source)
        half = jnp.where(slot == j, bz, half)
        for h in range(2):
            use = jnp.logical_and(bz == h, j < count_ref[0, 0])
            want = jnp.where(use, by, -1)
            back[h] = jnp.where(slot == want, j * BRICK + inner, back[h])
            for side, end in enumerate((0, per_half - 1)):
                ends[h][side] = jnp.where(want == end, 1, ends[h][side])
    return source, half, back, ends


def mhd_bulk(rows, prim_ref, u_ref, fz_ref, sz_ref, ch_ref, out_ref, unroll):
    load = plane_loader(prim_ref)
    row, lane = iota((CX, LANES), 0), iota((CX, LANES), 1)
    slots = {c: k for k, c in enumerate(rows)}

    @pl.loop(0, NZ, unroll=unroll)
    def _(z):
        u, f, s = derive([load(k, z) for k in range(8)])

        def along(d, nxt, prv, last):
            un = {c: nxt(u[c]) for c in rows}
            fn = {c: None if f[d][c] is None else nxt(f[d][c]) for c in rows}
            fc = face(rows, u, un, f[d], fn, s[d], nxt(s[d]))
            out = {}
            for c in rows:
                inside = jnp.where(last, 0.0, fc[c])
                out[c] = inside - prv(inside)
            return out

        cx = along(0, next_row, prev_row, row == CX - 1)
        cy = along(1, next_lane, prev_lane, lane == LANES - 1)
        for c, k in slots.items():
            ch_ref[plane_at(k, z), :] = u[c] - TIME_STEP * (cx[c] + cy[c])
            u_ref[plane_at(k, z), :] = u[c]
            if f[2][c] is not None:
                fz_ref[plane_at(k, z), :] = f[2][c]
        sz_ref[plane_at(0, z), :] = s[2]

    def zface(z):
        zn = lax.rem(z + 1, NZ)
        u = {c: u_ref[plane_at(k, z), :] for c, k in slots.items()}
        un = {c: u_ref[plane_at(k, zn), :] for c, k in slots.items()}
        f = {c: None if c == 6 else fz_ref[plane_at(k, z), :] for c, k in slots.items()}
        fn = {c: None if c == 6 else fz_ref[plane_at(k, zn), :] for c, k in slots.items()}
        return face(rows, u, un, f, fn, sz_ref[plane_at(0, z), :], sz_ref[plane_at(0, zn), :])

    def finish(z, before):
        here = zface(z)
        for i, (c, k) in enumerate(slots.items()):
            out_ref[plane_at(place(rows, c), z), :] = (
                ch_ref[plane_at(k, z), :] - TIME_STEP * (here[c] - before[i]))
        return tuple(here[c] for c in rows)

    last = zface(NZ - 1)
    lax.fori_loop(0, NZ, finish, tuple(last[c] for c in rows), unroll=unroll)


FIELD_ROWS = (4, 5, 6)
OTHER_ROWS = (0, 1, 2, 3, 7)


def place(rows, c):
    return c - 4 if rows == FIELD_ROWS else c


def y_halo(f, yfl_ref, yfr_ref):
    at = pl.ds(f * 8, 8)
    side0 = iota((8, LANES), 1) % 2 == 0
    return jnp.where(side0, next_lane(yfl_ref[at, :]), prev_lane(yfr_ref[at, :]))


def mhd_ends(rows, prim_ref, py_ref, xlo_ref, xhi_ref, yfl_ref, yfr_ref, out_ref):
    lane8 = iota((8, LANES), 1)
    side0 = lane8 % 2 == 0
    last_lane = jnp.where(lane8 == LANES - 1, 1, 0)
    on_edge = jnp.logical_or(lane8 == 0, lane8 == LANES - 1)
    uh, fh, sh = derive([y_halo(f, yfl_ref, yfr_ref) for f in range(8)])
    uo, fo, so = derive([py_ref[pl.ds(f * 8, 8), :] for f in range(8)])

    def pair(a, b):
        return [None if p is None else jnp.where(side0, p, q) for p, q in zip(a, b)]

    fc = face(rows, pair(uh, uo), pair(uo, uh), pair(fh[1], fo[1]), pair(fo[1], fh[1]),
              jnp.where(side0, sh[1], so[1]), jnp.where(side0, so[1], sh[1]))
    for c in rows:
        delta = jnp.where(side0, TIME_STEP, -TIME_STEP) * fc[c]
        base = place(rows, c) * PLANE
        for z in range(NZ):
            for o in range(2):
                at = pl.ds(base + z * CX + o * 8, 8)
                g = take(delta, (o * NZ + z) * 2 + last_lane)
                out_ref[at, :] = out_ref[at, :] + jnp.where(on_edge, g, 0.0)

    for zs in range(0, NZ, 8):
        for lo in (True, False):
            start = zs * CX + (0 if lo else CX - 1)
            ref = xlo_ref if lo else xhi_ref
            uo, fo, so = derive([prim_ref[pl.ds(f * PLANE + start, 8, stride=CX), :] for f in range(8)])
            uh, fh, sh = derive([ref[pl.ds(f * NZ + zs, 8), :] for f in range(8)])
            if lo:
                fc = face(rows, uh, uo, fh[0], fo[0], sh[0], so[0])
            else:
                fc = face(rows, uo, uh, fo[0], fh[0], so[0], sh[0])
            for c in rows:
                at = pl.ds(place(rows, c) * PLANE + start, 8, stride=CX)
                step = TIME_STEP * fc[c]
                out_ref[at, :] = out_ref[at, :] + (step if lo else -step)


def field_kernel(prim_ref, win_ref, whid_ref, wout_ref, bias_ref,
                 adv_ref, wb_ref, w1_ref, w2_ref, wo_ref,
                 u_ref, fz_ref, sz_ref, ch_ref):
    def split(b):
        hi = b.astype(BF16)
        r = b - hi.astype(F32)
        mid = r.astype(BF16)
        return [hi.astype(F32), mid.astype(F32), r - mid.astype(F32)]

    cols = (((0,), (0,)), ((), ()))
    rows = iota((16, KIN), 0)
    col = iota((16, KIN), 1)
    first = jnp.concatenate(
        [win_ref[...].astype(F32)] + split(bias_ref[0:1, :]) + [jnp.zeros((5, HID), F32)], axis=0
    ).astype(BF16)
    for s in range(8):
        spot = jnp.where(rows < 8, rows * 8 + s, jnp.where(rows < 11, 64 + rows - 8, -1))
        pick = jnp.where(col == spot, 1.0, 0.0).astype(BF16)
        wb_ref[pl.ds(s * HID, HID), :] = lax.dot_general(
            first, pick, cols, preferred_element_type=F32).astype(BF16)
    eye = jnp.where(iota((HID, HID), 0) == iota((HID, HID), 1), 0.5, 0.0).astype(BF16)
    eye16 = jnp.where(iota((16, 16), 0) == iota((16, 16), 1), 1.0, 0.0).astype(BF16)
    for layer, ref in ((0, w1_ref), (1, w2_ref)):
        turned = lax.dot_general(whid_ref[pl.ds(layer * HID, HID), :], eye, cols,
                                 preferred_element_type=F32)
        brow = jnp.concatenate(
            split(bias_ref[layer + 1 : layer + 2, :]) + [jnp.zeros((13, HID), F32)], axis=0
        ).astype(BF16)
        bcol = lax.dot_general(brow, eye16, cols, preferred_element_type=F32)
        ref[...] = jnp.concatenate([turned, bcol], axis=1).astype(BF16)
    wo_ref[...] = jnp.broadcast_to(0.5 * wout_ref[...].astype(F32), (16, HID)).astype(BF16)

    mhd_bulk(FIELD_ROWS, prim_ref, u_ref, fz_ref, sz_ref, ch_ref, adv_ref, 2)


HALF = NZ // 2
WIDE = HALF * LANES


def edge_kernel(bricks_ref, count_ref, prim_ref, advin_ref, py_ref,
                xlo_ref, xhi_ref, yfl_ref, yfr_ref, wb_ref, w1_ref, w2_ref, wo_ref,
                adv_ref, x_ref, kape_ref, sy_ref, sxlo_ref, sxhi_ref,
                feat_ref, yh_ref):
    load = plane_loader(prim_ref)
    lane8 = iota((8, LANES), 1)
    last_lane = jnp.where(lane8 == LANES - 1, 1, 0)
    sub = iota((8, LANES), 0)
    adv_ref[...] = advin_ref[...]
    mhd_ends(FIELD_ROWS, prim_ref, py_ref, xlo_ref, xhi_ref, yfl_ref, yfr_ref, adv_ref)

    source, half, back, ends = brick_rows(bricks_ref, count_ref)
    tail = bias_rows(LANES)
    for f in range(8):
        yh_ref[pl.ds(f * 8, 8), :] = y_halo(f, yfl_ref, yfr_ref)

    def patch_x(f, z):
        return xlo_ref[pl.ds(f * NZ + z, 1), :], xhi_ref[pl.ds(f * NZ + z, 1), :]

    def patch_y(f, z):
        h = yh_ref[pl.ds(f * 8, 8), :]
        return jnp.concatenate([take(h, (o * NZ + z) * 2 + last_lane) for o in range(2)], axis=0)

    @pl.loop(0, HALF)
    def _(z):
        both = []
        for zz in (z, z + HALF):
            fs = features(load, zz, patch_x, patch_y)
            both.append(fs)
            for k in range(8):
                feat_ref[plane_at(k, zz), :] = fs[k]
        at = pl.ds(pl.multiple_of(z * LANES, LANES), LANES)
        for o in range(2):
            parts = []
            for a, b in zip(*both):
                a, b = a[o * 8 : o * 8 + 8], b[o * 8 : o * 8 + 8]
                parts.append(jnp.where(half == 1, take(b, source), take(a, source)))
            x_ref[pl.ds(o * KIN, KIN), at] = jnp.concatenate(parts + [tail], axis=0).astype(BF16)

    inner = lane8 % 8
    index = jnp.where(inner < 4, inner, LANES - 8 + inner)

    def y_pack(ref, base):
        out = {}
        for o in range(2):
            for h in range(2):
                acc = jnp.zeros((8, LANES), F32)
                for z in range(HALF):
                    v = ref[pl.ds(base + (h * HALF + z) * CX + o * 8, 8), :]
                    acc = jnp.where(lane8 // 8 == z, take(v, index), acc)
                out[o, h] = acc
        return out

    packs = [y_pack(feat_ref, k * PLANE) for k in range(8)]
    ycells = jnp.concatenate(
        [jnp.concatenate([p[o, h] for p in packs] + [tail], axis=0) for o in range(2) for h in range(2)],
        axis=1).astype(BF16)
    w1, w2, wo = w1_ref[...], w2_ref[...], wo_ref[...]
    us = []
    for o, s in ((0, 0), (0, 1), (0, 2), (1, 5), (1, 6), (1, 7)):
        us.append(jnp.dot(wb_ref[pl.ds(s * HID, HID), :], x_ref[pl.ds(o * KIN, KIN), :],
                          preferred_element_type=F32))
    uy = [jnp.dot(wb_ref[pl.ds(s * HID, HID), :], ycells, preferred_element_type=F32) for s in range(8)]
    for part in range(2):
        us.append(jnp.concatenate(uy[part * 4 : part * 4 + 4], axis=1))
    rates = closure_rates(us, w1, w2, wo)

    low = jnp.full((NZ, LANES), RATE_LOW, BF16)
    for e in range(6):
        packed = []
        for q in range(2):
            acc = jnp.zeros((8, LANES), F32)
            for k in range(8):
                z = q * 8 + k
                acc = jnp.where(sub == k, rates[e][:8, z * LANES : (z + 1) * LANES], acc)
            packed.append(acc)
            kape_ref[pl.ds(e * HALF + q * 8, 8), :] = acc
        full = []
        for h in range(2):
            listed = back[h] >= 0
            for q in range(2):
                full.append(jnp.where(listed, take(packed[q], jnp.maximum(back[h], 0)), RATE_LOW))
        full = jnp.concatenate(full, axis=0).astype(BF16)
        if e < 3:
            sxlo_ref[pl.ds((12 + e) * NZ, NZ), :] = full
        else:
            sxhi_ref[pl.ds((12 + e - 2) * NZ, NZ), :] = full
    sxlo_ref[pl.ds(15 * NZ, NZ), :] = low
    sxhi_ref[pl.ds(12 * NZ, NZ), :] = low
    for o in range(2):
        for h in range(2):
            acc = jnp.zeros((8, LANES), F32)
            for s in range(8):
                at = (s % 4) * 512 + (o * 2 + h) * LANES
                acc = jnp.where(sub == s, rates[6 + s // 4][:8, at : at + LANES], acc)
            use = jnp.where(inner < 4, ends[h][0], ends[h][1])
            packs[0][o, h] = jnp.where(use == 1, acc, RATE_LOW)
    rate_pack = packs[0]

    for f in range(4):
        got = rate_pack if f == 3 else y_pack(adv_ref, f * PLANE)
        for h in range(2):
            sy_ref[pl.ds((f * 2 + h) * CX, CX), :] = jnp.concatenate(
                [got[0, h], got[1, h]], axis=0).astype(BF16)
        if f < 3:
            for r in range(4):
                at = pl.ds((f * 4 + r) * NZ, NZ)
                sxlo_ref[at, :] = adv_ref[pl.ds(f * PLANE + r, NZ, stride=CX), :].astype(BF16)
                sxhi_ref[at, :] = adv_ref[pl.ds(f * PLANE + CX - 4 + r, NZ, stride=CX), :].astype(BF16)


def inner_kernel(bricks_ref, count_ref, x_ref, kape_ref, wb_ref, w1_ref, w2_ref, wo_ref,
                 kap_ref, kp_ref):
    w1, w2, wo = w1_ref[...], w2_ref[...], wo_ref[...]
    sub = iota((8, LANES), 0)
    _, _, back, _ = brick_rows(bricks_ref, count_ref)
    for o in range(2):
        which = range(3, 8) if o == 0 else range(5)
        us = [jnp.dot(wb_ref[pl.ds(s * HID, HID), :], x_ref[pl.ds(o * KIN, KIN), :],
                      preferred_element_type=F32) for s in which]
        rates = closure_rates(us, w1, w2, wo)
        for z in range(HALF):
            acc = jnp.zeros((8, LANES), F32)
            for s, r in zip(which, rates):
                acc = jnp.where(sub == s, r[:8, z * LANES : (z + 1) * LANES], acc)
            kp_ref[pl.ds(z * CX + o * 8, 8), :] = acc
    for e in range(6):
        x = e if e < 3 else CX - 6 + e
        kp_ref[pl.ds(x, HALF, stride=CX), :] = kape_ref[pl.ds(e * HALF, HALF), :]
    for h in range(2):
        listed = back[h] >= 0
        index = jnp.maximum(back[h], 0)
        for z in range(HALF):
            for o in range(2):
                k = kp_ref[pl.ds(z * CX + o * 8, 8), :]
                kap_ref[pl.ds((h * HALF + z) * CX + o * 8, 8), :] = jnp.where(
                    listed, take(k, index), RATE_LOW)


def corner_kernel(yfl_ref, yfr_ref, sxlo_ref, sxhi_ref, yh_ref, dlo_ref, dhi_ref):
    upper = iota((4 * 2 * CX, LANES), 1) % 8 < 4
    merged = jnp.where(upper, yfr_ref[...].astype(F32), yfl_ref[...].astype(F32))
    yh_ref[...] = merged
    rows = 16 * NZ
    dlo_ref[pl.ds(0, rows), :] = sxlo_ref[...]
    dhi_ref[pl.ds(0, rows), :] = sxhi_ref[...]
    firsts = [merged[k * CX : k * CX + 8] for k in range(8)]
    lasts = [merged[k * CX + 8 : k * CX + 16] for k in range(8)]
    dlo_ref[pl.ds(rows, 64), :] = jnp.concatenate(firsts, axis=0).astype(BF16)
    dhi_ref[pl.ds(rows, 64), :] = jnp.concatenate(lasts, axis=0).astype(BF16)


def others_kernel(prim_ref, py_ref, xlo_ref, xhi_ref, yfl_ref, yfr_ref, out_ref,
                  u_ref, fz_ref, sz_ref, ch_ref):
    mhd_bulk(OTHER_ROWS, prim_ref, u_ref, fz_ref, sz_ref, ch_ref, out_ref, 2)
    mhd_ends(OTHER_ROWS, prim_ref, py_ref, xlo_ref, xhi_ref, yfl_ref, yfr_ref, out_ref)


DEEP = CX + 8
YG = NZ // 4


def diffuse_kernel(out_in_ref, adv_ref, kap_ref, xlo_ref, xhi_ref, yh_ref, out_ref,
                   m0, m1, km, y0, y1, ky, xl, xh):
    comp = pl.program_id(0)
    lane = iota((8, LANES), 1)
    sub = iota((8, LANES), 0)
    window = lane % 32
    block = lane // 32
    own_index = jnp.maximum(jnp.where(window < 16, window - 4, window + 100), 0)
    own_index = jnp.minimum(own_index, LANES - 1)
    on_halo = jnp.logical_or(window < 4, window >= 28)
    halo_index = (block % 2) * 64 + jnp.where(window < 4, 4 + window, window - 28)
    halo_index = jnp.where(on_halo, halo_index, 0)

    def build(field, own_ref, main, edge):
        base = field * (4 * NZ)
        for z in range(NZ):
            main[pl.ds(z * DEEP, CX), :] = own_ref[pl.ds(z * CX, CX), :]
        for r in range(4):
            at = pl.ds(pl.multiple_of(base + r * NZ, 8), NZ)
            main[pl.ds(CX + r, NZ, stride=DEEP), :] = xh[at, :]
            main[pl.ds(CX + 4 + r, NZ, stride=DEEP), :] = xl[at, :]
        for o in range(3):
            halves = []
            for h in range(2):
                if o < 2:
                    at = pl.ds(pl.multiple_of((field * 2 + h) * CX + o * 8, 8), 8)
                    halves.append(yh_ref[at, :])
                else:
                    at = pl.ds(pl.multiple_of(16 * NZ + (field * 2 + h) * 8, 8), 8)
                    halves.append(jnp.where(sub < 4, xh[at, :], xl[at, :]))
            for g in range(YG):
                v = jnp.zeros((8, LANES), F32)
                for b in range(4):
                    piece = main[pl.ds((b * YG + g) * DEEP + o * 8, 8), :]
                    v = jnp.where(block == b, take(piece, own_index), v)
                index = jnp.where(on_halo, halo_index + g * 8, 0)
                got = jnp.where(block < 2, take(halves[0], index), take(halves[1], index))
                edge[pl.ds(g * DEEP + o * 8, 8), :] = jnp.where(on_halo, got, v)

    @pl.when(comp == 0)
    def _():
        xl[...] = xlo_ref[...].astype(F32)
        xh[...] = xhi_ref[...].astype(F32)
        build(3, kap_ref, km, ky)

    build(comp, adv_ref, m0, y0)

    def relax(c, up, dn, k):
        total = next_row(c) + prev_row(c) + next_lane(c) + prev_lane(c) + (up + dn)
        return c + k * (total - 6.0 * c)

    mains, edges = (m0, m1), (y0, y1)
    for step in range(SUB):
        a, b = mains[step % 2], mains[1 - step % 2]
        ea, eb = edges[step % 2], edges[1 - step % 2]

        def at(z):
            return pl.ds(z * DEEP, DEEP)

        dn, c = a[at(NZ - 1), :], a[at(0), :]
        for z in range(NZ):
            up = a[at((z + 1) % NZ), :]
            b[at(z), :] = relax(c, up, dn, km[at(z), :])
            dn, c = c, up

        for g in range(YG):
            up = ea[at(g + 1), :] if g + 1 < YG else pltpu.roll(ea[at(0), :], LANES - 32, 1)
            dn = ea[at(g - 1), :] if g > 0 else pltpu.roll(ea[at(YG - 1), :], 32, 1)
            eb[at(g), :] = relax(ea[at(g), :], up, dn, ky[at(g), :])

    main, edge = mains[SUB % 2], edges[SUB % 2]
    on_edge = jnp.logical_or(lane < 4, lane >= LANES - 4)
    for z in range(NZ):
        b, g = z // YG, z % YG
        index = jnp.where(lane < 4, b * 32 + 4 + lane, b * 32 + 24 + lane - (LANES - 4))
        index = jnp.minimum(jnp.maximum(index, 0), LANES - 1)
        for o in range(2):
            e = take(edge[pl.ds(g * DEEP + o * 8, 8), :], index)
            out_ref[pl.ds(z * CX + o * 8, 8), :] = jnp.where(
                on_edge, e, main[pl.ds(z * DEEP + o * 8, 8), :])


def struct(shape, dtype=F32):
    return jax.ShapeDtypeStruct(shape, dtype)


def params():
    return pltpu.CompilerParams(vmem_limit_bytes=VMEM_LIMIT)


def cost(us):
    return pl.CostEstimate(flops=us * 500_000_000, bytes_accessed=us << 20, transcendentals=0)


VSPEC = pl.BlockSpec(memory_space=pltpu.VMEM)
SSPEC = pl.BlockSpec(memory_space=pltpu.SMEM)


def step_up(axis):
    n = lax.axis_size(axis)
    return [(i, (i + 1) % n) for i in range(n)]


def step_down(axis):
    n = lax.axis_size(axis)
    return [((i + 1) % n, i) for i in range(n)]


def shards(primitive, current_sheet_bricks, brick_count, w_in, w_hid, w_out, b_hid):
    shape = primitive.shape
    prim = primitive.reshape(8 * PLANE, LANES)
    bricks = current_sheet_bricks.reshape(1, -1)
    count = brick_count.reshape(1, 1)

    lo, hi, py = pl.pallas_call(
        pack_kernel,
        out_shape=[struct((8 * NZ, LANES)), struct((8 * NZ, LANES)), struct((64, LANES))],
        compiler_params=params(),
        name="pack",
    )(prim)
    yfl = lax.ppermute(py, "row", step_up("row"))
    yfr = lax.ppermute(py, "row", step_down("row"))
    xlo = lax.ppermute(hi, "col", step_up("col"))
    xhi = lax.ppermute(lo, "col", step_down("col"))

    weights = [struct((8 * HID, KIN), BF16), struct((HID, KHID), BF16), struct((HID, KHID), BF16),
               struct((16, HID), BF16)]

    def mhd_scratch(rows):
        many = pltpu.VMEM((len(rows) * PLANE, LANES), F32)
        return [many, many, pltpu.VMEM((PLANE, LANES), F32), many]

    badv, wb, w1, w2, wo = pl.pallas_call(
        field_kernel,
        out_shape=[struct((3 * PLANE, LANES))] + weights,
        scratch_shapes=mhd_scratch(FIELD_ROWS),
        compiler_params=params(),
        cost_estimate=cost(4),
        name="field",
    )(prim, w_in, w_hid.reshape(2 * HID, HID), w_out.reshape(1, HID), b_hid)

    halos = (py, xlo, xhi, yfl, yfr)
    badv, xcells, kape, sy, sxlo, sxhi = pl.pallas_call(
        edge_kernel,
        in_specs=[SSPEC, SSPEC] + [VSPEC] * 11,
        out_shape=[struct((3 * PLANE, LANES)), struct((2 * KIN, WIDE), BF16), struct((6 * HALF, LANES)),
                   struct((8 * CX, LANES), BF16),
                   struct((16 * NZ, LANES), BF16), struct((16 * NZ, LANES), BF16)],
        scratch_shapes=[pltpu.VMEM((8 * PLANE, LANES), F32), pltpu.VMEM((64, LANES), F32)],
        compiler_params=params(),
        cost_estimate=cost(8),
        name="edges",
    )(bricks, count, prim, badv, *halos, wb, w1, w2, wo)

    hlo = lax.ppermute(sy, "row", step_up("row"))
    hhi = lax.ppermute(sy, "row", step_down("row"))

    kap = pl.pallas_call(
        inner_kernel,
        in_specs=[SSPEC, SSPEC] + [VSPEC] * 6,
        out_shape=struct((PLANE, LANES)),
        scratch_shapes=[pltpu.VMEM((HALF * CX, LANES), F32)],
        compiler_params=params(),
        cost_estimate=cost(6),
        name="inner",
    )(bricks, count, xcells, kape, wb, w1, w2, wo)

    xrows = 16 * NZ + 64
    yh, dlo, dhi = pl.pallas_call(
        corner_kernel,
        out_shape=[struct((8 * CX, LANES)), struct((xrows, LANES), BF16), struct((xrows, LANES), BF16)],
        compiler_params=params(),
        name="corners",
    )(hlo, hhi, sxlo, sxhi)
    gothi = lax.ppermute(dlo, "col", step_down("col"))
    gotlo = lax.ppermute(dhi, "col", step_up("col"))

    rest = pl.pallas_call(
        others_kernel,
        out_shape=struct((8 * PLANE, LANES)),
        scratch_shapes=mhd_scratch(OTHER_ROWS),
        compiler_params=params(),
        cost_estimate=cost(6),
        name="others",
    )(prim, *halos)

    full = lambda rows: pl.BlockSpec((rows, LANES), lambda c: (0, 0))
    out = pl.pallas_call(
        diffuse_kernel,
        grid=(3,),
        in_specs=[pl.BlockSpec(memory_space=pl.ANY), pl.BlockSpec((PLANE, LANES), lambda c: (c, 0)),
                  full(PLANE), full(xrows), full(xrows), full(8 * CX)],
        out_specs=pl.BlockSpec((PLANE, LANES), lambda c: (4 + c, 0)),
        out_shape=struct((8 * PLANE, LANES)),
        input_output_aliases={0: 0},
        scratch_shapes=[pltpu.VMEM((NZ * DEEP, LANES), F32)] * 3
        + [pltpu.VMEM((YG * DEEP, LANES), F32)] * 3
        + [pltpu.VMEM((xrows, LANES), F32)] * 2,
        compiler_params=params(),
        name="diffuse",
    )(rest, badv, kap, gotlo, gothi, yh)
    return out.reshape(shape)


def solution(mesh):
    return jax.shard_map(
        shards,
        mesh=mesh,
        in_specs=(
            P(None, None, "col", "row"),
            P("row", "col", None),
            P("row", "col"),
            P(),
            P(),
            P(),
            P(),
        ),
        out_specs=P(None, None, "col", "row"),
        check_vma=False,
    )
```

time: 86.9 us -> 48.1 us (0.55)
  Pallas kernels: 63.6 us -> 31.2 us
  waiting for transfers between devices: 4.99 us -> 0.02 us
    pallas_call x3 -> x6, Pallas kernels: 62.9 us -> 30.6 us  [the longest x1 9.33 us: shards(): pl.pallas_call(edge_kernel, in_specs=[SSPEC, SSPEC] + [VSPEC] * 11, out_s...]
    ppermute x4, waiting for transfers between devices: 4.98 us -> 0.01 us  [the longest x1 0.01 us: shards(): hhi = lax.ppermute(sy, 'row', step_down('row'))]
  transfers between devices with their start and end apart: 8 -> 8, of which waited for: 2 -> 0; matrix products, arithmetic and copies ran while one was open for 0% -> 0% of each run, Pallas kernels for 22% -> 32%
where the time goes in v1:
time: 48.1 us; the launch traced here: 48 us
  Pallas kernels  31.2 us (65%)
  starting transfers between devices  14.3 us (30%)
  local copies, waits for them, and re-layouts  1.63 us (3%)
  between operations  0.76 us (2%)
    pallas_call x1, Pallas kernels, shards(): pl.pallas_call(edge_kernel, in_specs=[SSPEC, SSPEC] + [VSPEC] * 11, out_s...  9.33 us
    pallas_call x1, Pallas kernels, shards(): pl.pallas_call(others_kernel, out_shape=struct((8 * PLANE, LANES)), scrat...  6.2 us
    pallas_call x1, Pallas kernels, shards(): pl.pallas_call(inner_kernel, in_specs=[SSPEC, SSPEC] + [VSPEC] * 6, out_s...  5.76 us
    pallas_call x1, Pallas kernels, shards(): pl.pallas_call(diffuse_kernel, grid=(3,), in_specs=[pl.BlockSpec(memory_s...  5.75 us
    ppermute x1, starting transfers between devices, shards(): yfr = lax.ppermute(py, 'row', step_down('row'))  5.1 us
    ppermute x1, starting transfers between devices, shards(): hhi = lax.ppermute(sy, 'row', step_down('row'))  3.87 us
    pallas_call x1, Pallas kernels, shards(): pl.pallas_call(field_kernel, out_shape=[struct((3 * PLANE, LANES))] + wei...  3.56 us
    ppermute x1, starting transfers between devices, shards(): xhi = lax.ppermute(lo, 'col', step_down('col'))  2.64 us
  transfers between devices with their start and end apart: 8, of which 0 were waited for; matrix products, arithmetic and copies ran while one was open for 0% of the time, Pallas kernels for 32%

profile of v1, /device:TPU:0, one launch (start us, length us, event | category | flops | bytes accessed | tf_op | source)
XLA Modules:
  0.0 48.0 jit_solution(8822958916674757515)
XLA Ops:
  0.0 1.6 %copy-done = f32[8,32,16,128]{3,2,1,0:T(8,128)S(1)} copy-done((f32[8,32,16,128]{3,2,1,0:T(8,128)S(1)}, f32[8,32,16,128]{3,2,1,0:T(8,128)}, u32[]{:S(2)}) %copy-start) | copy-done | bytes 2097176
  1.6 0.6 %pack.1 = (f32[256,128]{1,0:T(8,128)S(1)}, f32[256,128]{1,0:T(8,128)S(1)}, f32[64,128]{1,0:T(8,128)S(1)}) custom-call(f32[4096,128]{1,0:T(8,128)S(1)} %bitcast.5), custom_call_target="tpu_custom_call" | custom-call | tf_op jit(solution)/shard_map/pack/pallas_call | solution.py:600
  2.2 5.1 %collective-permute-start.3 = (f32[64,128]{1,0:T(8,128)S(1)}, f32[64,128]{1,0:T(8,128)S(1)}, u32[]{:S(2)}, u32[]{:S(2)}) collective-permute-start(f32[64,128]{1,0:T(8,128)S(1)} %get-tuple-element.22.py_ref), channel_id=1, source_target_pairs={{8,0},{16,8},{24,16},{0,24},{9,1},{17,9},{25,17},{1,25},{10,2},{18... | collective-permute-start | bytes 98312 | tf_op jit(solution)/shard_map/ppermute | solution.py:607
  7.3 0.0 collective-permute-start.2
  7.3 0.0 collective-permute-start
  7.3 2.6 %collective-permute-start.1 = (f32[256,128]{1,0:T(8,128)S(1)}, f32[256,128]{1,0:T(8,128)S(1)}, u32[]{:S(2)}, u32[]{:S(2)}) collective-permute-start(f32[256,128]{1,0:T(8,128)S(1)} %get-tuple-element.24), channel_id=1, source_target_pairs={{1,0},{2,1},{3,2},{4,3},{5,4},{6,5},{7,6},{0,7},{9,8},{10,9},{11,1... | collective-permute-start | bytes 393224 | tf_op jit(solution)/shard_map/ppermute | solution.py:609
  10.0 0.0 copy-start.6
  10.0 3.6 %field.1 = (f32[1536,128]{1,0:T(8,128)S(1)}, bf16[1024,80]{1,0:T(8,128)(2,1)S(1)}, bf16[128,144]{1,0:T(8,128)(2,1)S(1)}, bf16[128,144]{1,0:T(8,128)(2,1)S(1)}, bf16[16,128]{1,0:T(8,128)(2,1)S(1)}) custom-call(f32[4096,128]{1,0:T(8,128)S(1)} %bitcast.6, bf16[8,128]{1,0:T(8,128)(2,1)S(1)} %copy-done.3, bf16[256,128]{1,0:T(8,128)(2,1)S(1)} %bitcast.9, ...), custom_call_target="tpu_custom_call" | custom-call | flops 2000000000 | bytes 4194304 | tf_op jit(solution)/shard_map/field/pallas_call | solution.py:618
  14.2 0.0 collective-permute-done.3.yfr_ref
  14.2 0.0 collective-permute-done.2.yfl_ref
  14.2 0.0 collective-permute-done.xlo_ref
  14.3 0.0 collective-permute-done.1.xhi_ref
  14.3 9.3 %edges.1 = (f32[1536,128]{1,0:T(8,128)S(1)}, bf16[160,2048]{1,0:T(8,128)(2,1)S(1)}, f32[96,128]{1,0:T(8,128)S(1)}, bf16[128,128]{1,0:T(8,128)(2,1)S(1)}, bf16[51...) custom-call(s32[1,8]{1,0:T(1,128)S(1)} %bitcast.11, s32[1,1]{1,0:T(1,128)S(6)} %copy.10.count_ref, ...), custom_call_target="tpu_custom_call" | custom-call | flops 4000000000 | bytes 8388608 | tf_op jit(solution)/shard_map/edges/pallas_call | solution.py:628
  23.6 3.9 %collective-permute-start.5 = (bf16[128,128]{1,0:T(8,128)(2,1)S(1)}, bf16[128,128]{1,0:T(8,128)(2,1)S(1)}, u32[]{:S(2)}, u32[]{:S(2)}) collective-permute-start(bf16[128,128]{1,0:T(8,128)(2,1)S(1)} %get-tuple-element.33), channel_id=1, source_target_pairs={{8,0},{16,8},{24,16},{0,24},{9,1},{17,9},{25,17},{1,25},{10,2},{18... | collective-permute-start | bytes 98312 | tf_op jit(solution)/shard_map/ppermute | solution.py:641
  27.5 0.0 collective-permute-start.4
  27.5 5.8 %inner.1.kap_ref = f32[512,128]{1,0:T(8,128)S(1)} custom-call(s32[1,8]{1,0:T(1,128)S(1)} %bitcast.12, s32[1,1]{1,0:T(1,128)S(6)} %copy.10.count_ref, bf16[160,2048]{1,0:T(8,128)(2,1)S(1)} %get-tuple-element.31.x_ref, f32[96,128]{1,0:T(8,128)S(1)} %get-tuple-element.32.kape_ref, bf16[1024,80]{1,0:T(8,128)(2,1)S(1)} %get-tuple-element.26.wb_ref, ...), custom_call_target="tpu_custom_call" | custom-call | flops 3000000000 | bytes 6291456 | tf_op jit(solution)/shard_map/inner/pallas_call | solution.py:643
  33.3 0.0 collective-permute-done.5.yfr_ref
  33.3 0.0 collective-permute-done.4.yfl_ref
  33.3 0.1 collective-permute-start.6
  33.4 2.6 %collective-permute-start.7 = (bf16[576,128]{1,0:T(8,128)(2,1)S(1)}, bf16[576,128]{1,0:T(8,128)(2,1)S(1)}, u32[]{:S(2)}, u32[]{:S(2)}) collective-permute-start(bf16[576,128]{1,0:T(8,128)(2,1)S(1)} %get-tuple-element.37), channel_id=1, source_target_pairs={{1,0},{2,1},{3,2},{4,3},{5,4},{6,5},{7,6},{0,7},{9,8},{10,9},{11,1... | collective-permute-start | bytes 442376 | tf_op jit(solution)/shard_map/ppermute | solution.py:660
  36.0 6.2 %others.1.out_in_ref = f32[4096,128]{1,0:T(8,128)} custom-call(f32[4096,128]{1,0:T(8,128)S(1)} %bitcast.8, f32[64,128]{1,0:T(8,128)S(1)} %get-tuple-element.22.py_ref, f32[256,128]{1,0:T(8,128)S(1)} %collective-permute-done.xlo_ref, f32[256,128]{1,0:T(8,128)S(1)} %collective-permute-done.1.xhi_ref, f32[64,128]{1,0:T(8,128)S(1)} %collective-permute-done.2.yfl_ref, ...), custom_call_target="tpu_custom_call" | custom-call | flops 3000000000 | bytes 6291456 | tf_op jit(solution)/shard_map/others/pallas_call | solution.py:663
  42.2 0.0 collective-permute-done.6.xlo_ref
  42.2 0.0 collective-permute-done.7.xhi_ref
  42.2 5.7 %diffuse.1 = f32[4096,128]{1,0:T(8,128)} custom-call(f32[4096,128]{1,0:T(8,128)} %others.1.out_in_ref, f32[1536,128]{1,0:T(8,128)S(1)} %get-tuple-element.30.adv_ref, f32[512,128]{1,0:T(8,128)S(1)} %inner.1.kap_ref, bf16[576,128]{1,0:T(8,128)(2,1)S(1)} %collective-permute-done.6.xlo_ref, ...), custom_call_target="tpu_custom_call", output_to_operand_aliasing={{}: (0, {})} | custom-call | tf_op jit(solution)/shard_map/diffuse/pallas_call | solution.py:673
  (13 shorter events, 0.1 us)
Async XLA Ops:
  0.0 10.0 %copy-start.5 = (bf16[128]{0:T(256)(128)(2,1)S(1)}, bf16[128]{0:T(256)(128)(2,1)}, u32[]{:S(2)}) copy-start(bf16[128]{0:T(256)(128)(2,1)} %param.12) | copy-start | bytes 772
  0.0 1.6 %copy-start = (f32[8,32,16,128]{3,2,1,0:T(8,128)S(1)}, f32[8,32,16,128]{3,2,1,0:T(8,128)}, u32[]{:S(2)}) copy-start(f32[8,32,16,128]{3,2,1,0:T(8,128)} %param.7) | copy-start | bytes 6291460
  1.6 8.4 %copy-start.2 = (bf16[2,128,128]{2,1,0:T(8,128)(2,1)S(1)}, bf16[2,128,128]{2,1,0:T(8,128)(2,1)}, u32[]{:S(2)}) copy-start(bf16[2,128,128]{2,1,0:T(8,128)(2,1)} %param.11) | copy-start | bytes 196612
  1.6 8.4 %copy-start.3 = (bf16[8,128]{1,0:T(8,128)(2,1)S(1)}, bf16[8,128]{1,0:T(8,128)(2,1)}, u32[]{:S(2)}) copy-start(bf16[8,128]{1,0:T(8,128)(2,1)} %win_ref.1) | copy-start | bytes 6148
  1.6 8.4 %copy-start.4 = (f32[3,128]{1,0:T(4,128)S(1)}, f32[3,128]{1,0:T(4,128)}, u32[]{:S(2)}) copy-start(f32[3,128]{1,0:T(4,128)} %bias_ref.1) | copy-start | bytes 4612
  2.2 12.0 %collective-permute-start.3 = (f32[64,128]{1,0:T(8,128)S(1)}, f32[64,128]{1,0:T(8,128)S(1)}, u32[]{:S(2)}, u32[]{:S(2)}) collective-permute-start(f32[64,128]{1,0:T(8,128)S(1)} %get-tuple-element.22.py_ref), channel_id=1, source_target_pairs={{8,0},{16,8},{24,16},{0,24},{9,1},{17,9},{25,17},{1,25},{10,2},{18... | collective-permute-start | bytes 98312 | tf_op jit(solution)/shard_map/ppermute | solution.py:607
  7.3 6.9 %collective-permute-start.2 = (f32[64,128]{1,0:T(8,128)S(1)}, f32[64,128]{1,0:T(8,128)S(1)}, u32[]{:S(2)}, u32[]{:S(2)}) collective-permute-start(f32[64,128]{1,0:T(8,128)S(1)} %get-tuple-element.22.py_ref), channel_id=1, source_target_pairs={{0,8},{8,16},{16,24},{24,0},{1,9},{9,17},{17,25},{25,1},{2,10},{10... | collective-permute-start | bytes 98312 | tf_op jit(solution)/shard_map/ppermute | solution.py:606
  7.3 6.9 %collective-permute-start = (f32[256,128]{1,0:T(8,128)S(1)}, f32[256,128]{1,0:T(8,128)S(1)}, u32[]{:S(2)}, u32[]{:S(2)}) collective-permute-start(f32[256,128]{1,0:T(8,128)S(1)} %get-tuple-element.23), channel_id=1, source_target_pairs={{0,1},{1,2},{2,3},{3,4},{4,5},{5,6},{6,7},{7,0},{8,9},{9,10},{10,1... | collective-permute-start | bytes 393224 | tf_op jit(solution)/shard_map/ppermute | solution.py:608
  7.3 6.9 %collective-permute-start.1 = (f32[256,128]{1,0:T(8,128)S(1)}, f32[256,128]{1,0:T(8,128)S(1)}, u32[]{:S(2)}, u32[]{:S(2)}) collective-permute-start(f32[256,128]{1,0:T(8,128)S(1)} %get-tuple-element.24), channel_id=1, source_target_pairs={{1,0},{2,1},{3,2},{4,3},{5,4},{6,5},{7,6},{0,7},{9,8},{10,9},{11,1... | collective-permute-start | bytes 393224 | tf_op jit(solution)/shard_map/ppermute | solution.py:609
  10.0 4.3 %copy-start.6 = (s32[1,1,8]{2,1,0:T(1,128)S(1)}, s32[1,1,8]{2,1,0:T(1,128)}, u32[]{:S(2)}) copy-start(s32[1,1,8]{2,1,0:T(1,128)} %param.8) | copy-start | bytes 100
  23.6 9.6 %collective-permute-start.5 = (bf16[128,128]{1,0:T(8,128)(2,1)S(1)}, bf16[128,128]{1,0:T(8,128)(2,1)S(1)}, u32[]{:S(2)}, u32[]{:S(2)}) collective-permute-start(bf16[128,128]{1,0:T(8,128)(2,1)S(1)} %get-tuple-element.33), channel_id=1, source_target_pairs={{8,0},{16,8},{24,16},{0,24},{9,1},{17,9},{25,17},{1,25},{10,2},{18... | collective-permute-start | bytes 98312 | tf_op jit(solution)/shard_map/ppermute | solution.py:641
  27.5 5.8 %collective-permute-start.4 = (bf16[128,128]{1,0:T(8,128)(2,1)S(1)}, bf16[128,128]{1,0:T(8,128)(2,1)S(1)}, u32[]{:S(2)}, u32[]{:S(2)}) collective-permute-start(bf16[128,128]{1,0:T(8,128)(2,1)S(1)} %get-tuple-element.33), channel_id=1, source_target_pairs={{0,8},{8,16},{16,24},{24,0},{1,9},{9,17},{17,25},{25,1},{2,10},{10... | collective-permute-start | bytes 98312 | tf_op jit(solution)/shard_map/ppermute | solution.py:640
  27.5 8.5 %copy-start.1 = (f32[8,32,16,128]{3,2,1,0:T(8,128)S(1)}, f32[8,32,16,128]{3,2,1,0:T(8,128)}, u32[]{:S(2)}) copy-start(f32[8,32,16,128]{3,2,1,0:T(8,128)} %param.7) | copy-start | bytes 6291460
  33.3 8.9 %collective-permute-start.6 = (bf16[576,128]{1,0:T(8,128)(2,1)S(1)}, bf16[576,128]{1,0:T(8,128)(2,1)S(1)}, u32[]{:S(2)}, u32[]{:S(2)}) collective-permute-start(bf16[576,128]{1,0:T(8,128)(2,1)S(1)} %get-tuple-element.36), channel_id=1, source_target_pairs={{0,1},{1,2},{2,3},{3,4},{4,5},{5,6},{6,7},{7,0},{8,9},{9,10},{10,1... | collective-permute-start | bytes 442376 | tf_op jit(solution)/shard_map/ppermute | solution.py:661
  33.4 8.8 %collective-permute-start.7 = (bf16[576,128]{1,0:T(8,128)(2,1)S(1)}, bf16[576,128]{1,0:T(8,128)(2,1)S(1)}, u32[]{:S(2)}, u32[]{:S(2)}) collective-permute-start(bf16[576,128]{1,0:T(8,128)(2,1)S(1)} %get-tuple-element.37), channel_id=1, source_target_pairs={{1,0},{2,1},{3,2},{4,3},{5,4},{6,5},{7,6},{0,7},{9,8},{10,9},{11,1... | collective-permute-start | bytes 442376 | tf_op jit(solution)/shard_map/ppermute | solution.py:660

commit v2 on v1

v2 whole, which is shorter than its diff:
```python
import jax
import jax.numpy as jnp
from jax import lax
from jax.experimental import pallas as pl
from jax.experimental.pallas import tpu as pltpu
from jax.sharding import PartitionSpec as P

BRICK = 16
SUB = 4
ADIABATIC = 5.0 / 3.0
TIME_STEP = 0.02
RATE_LOW = 0.02
RATE_SPAN = 0.14
GELU_A = 0.7978845608
GELU_B = 0.7978845608 * 0.044715
F32 = jnp.float32
BF16 = jnp.bfloat16
LANES = 128
NZ = 32
CX = 16
HID = 128
PLANE = NZ * CX
KIN = 80
KHID = HID + 16
VMEM_LIMIT = 48 << 20


def iota(shape, dim):
    return lax.broadcasted_iota(jnp.int32, shape, dim)


def take(values, index):
    return jnp.take_along_axis(values, index, axis=1, mode="promise_in_bounds")


def next_row(v):
    return pltpu.roll(v, v.shape[0] - 1, 0)


def prev_row(v):
    return pltpu.roll(v, 1, 0)


def next_lane(v):
    return pltpu.roll(v, v.shape[1] - 1, 1)


def prev_lane(v):
    return pltpu.roll(v, 1, 1)


def derive(p):
    rho, pr = p[0], p[7]
    v, b = p[1:4], p[4:7]
    m = [rho * c for c in v]
    b2 = b[0] * b[0] + b[1] * b[1] + b[2] * b[2]
    v2 = v[0] * v[0] + v[1] * v[1] + v[2] * v[2]
    vb = v[0] * b[0] + v[1] * b[1] + v[2] * b[2]
    pt = pr + 0.5 * b2
    en = 1.5 * pr + 0.5 * (rho * v2 + b2)
    wave = ADIABATIC * pr + b2
    fast = wave * lax.rsqrt(wave * rho)
    ep = en + pt
    tens = {(i, j): m[i] * v[j] - b[i] * b[j] for i in range(3) for j in range(i, 3)}
    elec = {(i, j): v[i] * b[j] - b[i] * v[j] for i in range(3) for j in range(i + 1, 3)}
    fluxes = []
    for d in range(3):
        rows = [m[d]]
        for c in range(3):
            t = tens[(min(c, d), max(c, d))]
            rows.append(t + pt if c == d else t)
        for c in range(3):
            rows.append(None if c == d else (elec[(d, c)] if d < c else -elec[(c, d)]))
        rows.append(ep * v[d] - b[d] * vb)
        fluxes.append(rows)
    speeds = [jnp.abs(c) + fast for c in v]
    return [rho] + m + list(b) + [en], fluxes, speeds


def face(rows, u, un, f, fn, s, sn):
    a = 0.5 * jnp.maximum(s, sn)
    out = {}
    for c in rows:
        diss = a * (un[c] - u[c])
        out[c] = -diss if f[c] is None else 0.5 * (f[c] + fn[c]) - diss
    return out


def gelu_twice(u):
    u = u.astype(BF16)
    t = jnp.tanh(u * (jnp.asarray(GELU_A, BF16) + jnp.asarray(GELU_B, BF16) * (u * u)))
    return u + u * t


def closure_rates(first, w1, w2, wo):
    us = first
    for w in (w1, w2):
        hs = [jnp.concatenate([gelu_twice(u), bias_rows(u.shape[1]).astype(BF16)], axis=0) for u in us]
        us = [jnp.dot(w, h, preferred_element_type=F32) for h in hs]
    hs = [gelu_twice(u) for u in us]
    scores = [jnp.dot(wo, h, preferred_element_type=F32) for h in hs]
    return [(RATE_LOW + 0.5 * RATE_SPAN) + (0.5 * RATE_SPAN) * jnp.tanh(0.5 * s) for s in scores]


def features(load, z, up_of, dn_of, patch_x=None):
    row = iota((CX, LANES), 0)

    def dx(f, v):
        up, dn = next_row(v), prev_row(v)
        if patch_x is not None:
            lo, hi = patch_x(f, z)
            up = jnp.where(row == CX - 1, hi, up)
            dn = jnp.where(row == 0, lo, dn)
        return 0.5 * (up - dn)

    def dy(v):
        return 0.5 * (next_lane(v) - prev_lane(v))

    def dz(f):
        return 0.5 * (up_of(f, z) - dn_of(f, z))

    rho, vx, vy, vz, bx, by, bz, pr = [load(f, z) for f in range(8)]
    return feature_list(rho, (vx, vy, vz), (bx, by, bz), pr, lambda f, v: dx(f, v), dy, dz)


def feature_list(rho, v, b, pr, dx, dy, dz):
    jx = dy(b[2]) - dz(5)
    jy = dz(4) - dx(6, b[2])
    jz = dx(5, b[1]) - dy(b[0])
    div = dx(1, v[0]) + dy(v[1]) + dz(3)
    return [jx, jy, jz, div, rho, pr, b[0] * b[0] + b[1] * b[1] + b[2] * b[2],
            v[0] * v[0] + v[1] * v[1] + v[2] * v[2]]


def bias_rows(n):
    return jnp.where(iota((16, n), 0) < 3, 1.0, 0.0)


def plane_at(f, z):
    return pl.ds(pl.multiple_of((f * NZ + z) * CX, CX), CX)


def plane_loader(prim_ref):
    def load(f, z):
        return prim_ref[plane_at(f, z), :]

    return load


HALF = NZ // 2
WIDE = HALF * LANES
YG = NZ // 4
YPLANE = YG * CX
ENDS = 8
YROWS = 8 * 2 * CX


def pack_kernel(bricks_ref, count_ref, prim_ref, lo_ref, hi_ref):
    lane = iota((8, LANES), 1)
    spot = lane % ENDS
    for f in range(8):
        for h in range(2):
            los, his = [], []
            for o in range(2):
                lo = jnp.zeros((8, LANES), F32)
                hi = jnp.zeros((8, LANES), F32)
                for z in range(HALF):
                    v = prim_ref[pl.ds((f * NZ + h * HALF + z) * CX + o * 8, 8), :]
                    mine = lane // ENDS == z
                    lo = jnp.where(mine, take(v, spot), lo)
                    hi = jnp.where(mine, take(v, spot + (LANES - ENDS)), hi)
                los.append(lo)
                his.append(hi)
            at = pl.ds((f * 2 + h) * CX, CX)
            lo_ref[at, :] = jnp.concatenate(los, axis=0).astype(BF16)
            hi_ref[at, :] = jnp.concatenate(his, axis=0).astype(BF16)
    _, _, _, ends = brick_rows(bricks_ref, count_ref)
    second = iota((16, LANES), 1) >= LANES // 2
    for ref, side in ((lo_ref, 0), (hi_ref, 1)):
        flag = jnp.where(second, ends[1][side], ends[0][side])
        ref[pl.ds(YROWS, 16), :] = flag.astype(F32).astype(BF16)


def brick_rows(bricks_ref, count_ref):
    lane = iota((8, LANES), 1)
    slot, inner = lane // BRICK, lane % BRICK
    source = jnp.zeros((8, LANES), jnp.int32)
    half = jnp.zeros((8, LANES), jnp.int32)
    back = [jnp.full((8, LANES), -1, jnp.int32) for _ in range(2)]
    per_half = LANES // BRICK
    ends = [[0, 0], [0, 0]]
    for j in range(8):
        b = bricks_ref[0, j]
        bz, by = b // per_half, b % per_half
        source = jnp.where(slot == j, by * BRICK + inner, source)
        half = jnp.where(slot == j, bz, half)
        for h in range(2):
            use = jnp.logical_and(bz == h, j < count_ref[0, 0])
            want = jnp.where(use, by, -1)
            back[h] = jnp.where(slot == want, j * BRICK + inner, back[h])
            for side, end in enumerate((0, per_half - 1)):
                ends[h][side] = jnp.where(want == end, 1, ends[h][side])
    return source, half, back, ends


def mhd_bulk(count, prim_ref, u_ref, fz_ref, sz_ref, ch_ref, out_ref, unroll, windows):
    rows = range(8)
    row, lane = iota((CX, LANES), 0), iota((CX, LANES), 1)

    def at(f, z):
        return pl.ds(pl.multiple_of((f * count + z) * CX, CX), CX)

    @pl.loop(0, count, unroll=unroll)
    def _(z):
        u, f, s = derive([prim_ref[at(k, z), :] for k in rows])

        def along(d, nxt, prv, last):
            un = {c: nxt(u[c]) for c in rows}
            fn = {c: None if f[d][c] is None else nxt(f[d][c]) for c in rows}
            fc = face(rows, u, un, f[d], fn, s[d], nxt(s[d]))
            out = {}
            for c in rows:
                inside = fc[c] if last is None else jnp.where(last, 0.0, fc[c])
                out[c] = inside - prv(inside)
            return out

        cx = along(0, next_row, prev_row, row == CX - 1)
        cy = along(1, next_lane, prev_lane, None if windows else lane == LANES - 1)
        for c in rows:
            ch_ref[at(c, z), :] = u[c] - TIME_STEP * (cx[c] + cy[c])
            u_ref[at(c, z), :] = u[c]
            if f[2][c] is not None:
                fz_ref[at(c, z), :] = f[2][c]
        sz_ref[at(0, z), :] = s[2]

    def zface(z, zn, turn):
        u = {c: u_ref[at(c, z), :] for c in rows}
        un = {c: turn(u_ref[at(c, zn), :]) for c in rows}
        f = {c: None if c == 6 else fz_ref[at(c, z), :] for c in rows}
        fn = {c: None if c == 6 else turn(fz_ref[at(c, zn), :]) for c in rows}
        return face(rows, u, un, f, fn, sz_ref[at(0, z), :], turn(sz_ref[at(0, zn), :]))

    def finish(z, before, here):
        for c in rows:
            out_ref[at(c, z), :] = ch_ref[at(c, z), :] - TIME_STEP * (here[c] - before[c])
        return tuple(here[c] for c in rows)

    if windows:
        last = zface(count - 1, 0, lambda v: pltpu.roll(v, LANES - 32, 1))
        before = tuple(pltpu.roll(last[c], 32, 1) for c in rows)
        for z in range(count):
            here = last if z == count - 1 else zface(z, z + 1, lambda v: v)
            before = finish(z, before, here)
    else:
        def step(z, before):
            return finish(z, before, zface(z, lax.rem(z + 1, count), lambda v: v))

        last = zface(count - 1, 0, lambda v: v)
        lax.fori_loop(0, count, step, tuple(last[c] for c in rows), unroll=unroll)


def x_ends(own_of, halo_of, lo, add):
    rows = range(8)
    uo, fo, so = derive([own_of(f) for f in rows])
    uh, fh, sh = derive([halo_of(f) for f in rows])
    if lo:
        fc = face(rows, uh, uo, fh[0], fo[0], sh[0], so[0])
    else:
        fc = face(rows, uo, uh, fo[0], fh[0], so[0], sh[0])
    for c in rows:
        step = TIME_STEP * fc[c]
        add(c, step if lo else -step)


def bulk_kernel(prim_ref, adv_ref, xlo_ref, xhi_ref, u_ref, fz_ref, sz_ref, ch_ref):
    mhd_bulk(NZ, prim_ref, u_ref, fz_ref, sz_ref, ch_ref, adv_ref, 4, False)
    for f in range(8):
        at = pl.ds(f * NZ, NZ)
        xlo_ref[at, :] = prim_ref[pl.ds(f * PLANE, NZ, stride=CX), :].astype(BF16)
        xhi_ref[at, :] = prim_ref[pl.ds(f * PLANE + CX - 1, NZ, stride=CX), :].astype(BF16)


def window_kernel(prim_ref, yfl_ref, yfr_ref, xlo_ref, xhi_ref, yp_ref, sxlo_ref, sxhi_ref,
                  left_ref, right_ref):
    lane = iota((8, LANES), 1)
    window, block = lane % 32, lane // 32
    own = jnp.where(window < 16, window - 6, LANES - 26 + window)
    own = jnp.minimum(jnp.maximum(own, 0), LANES - 1)
    spot = (block % 2) * 64 + jnp.where(window < 16, jnp.minimum(window + 2, 7), jnp.maximum(window - 26, 0))
    left_ref[...] = yfl_ref[pl.ds(0, YROWS), :].astype(F32)
    right_ref[...] = yfr_ref[pl.ds(0, YROWS), :].astype(F32)
    low, high, first = window < 6, window >= 26, block < 2
    for f in range(8):
        for o in range(2):
            here = [[ref[pl.ds((f * 2 + h) * CX + o * 8, 8), :] for h in range(2)]
                    for ref in (left_ref, right_ref)]
            for g in range(YG):
                v = None
                for b in range(4):
                    piece = take(prim_ref[pl.ds((f * NZ + b * YG + g) * CX + o * 8, 8), :], own)
                    v = piece if v is None else jnp.where(block == b, piece, v)
                index = spot + g * ENDS
                for side, where in ((0, low), (1, high)):
                    got = jnp.where(first, take(here[side][0], index), take(here[side][1], index))
                    v = jnp.where(where, got, v)
                yp_ref[pl.ds((f * YG + g) * CX + o * 8, 8), :] = v
    rows = 8 * NZ
    sxlo_ref[pl.ds(0, rows), :] = xlo_ref[...]
    sxhi_ref[pl.ds(0, rows), :] = xhi_ref[...]
    for f in range(0, 8, 2):
        for ref, start in ((sxlo_ref, 0), (sxhi_ref, CX - 1)):
            ref[pl.ds(rows + f * YG, 2 * YG), :] = yp_ref[
                pl.ds(f * YPLANE + start, 2 * YG, stride=CX), :].astype(BF16)


def ready_kernel(bricks_ref, count_ref, prim_ref, yp_ref, win_ref, whid_ref, wout_ref, bias_ref,
                 yadv_ref, x_ref, wb_ref, w1_ref, w2_ref, wo_ref,
                 u_ref, fz_ref, sz_ref, ch_ref):
    def split(b):
        hi = b.astype(BF16)
        r = b - hi.astype(F32)
        mid = r.astype(BF16)
        return [hi.astype(F32), mid.astype(F32), r - mid.astype(F32)]

    cols = (((0,), (0,)), ((), ()))
    rows = iota((16, KIN), 0)
    col = iota((16, KIN), 1)
    first = jnp.concatenate(
        [win_ref[...].astype(F32)] + split(bias_ref[0:1, :]) + [jnp.zeros((5, HID), F32)], axis=0
    ).astype(BF16)
    for s in range(8):
        spot = jnp.where(rows < 8, rows * 8 + s, jnp.where(rows < 11, 64 + rows - 8, -1))
        pick = jnp.where(col == spot, 1.0, 0.0).astype(BF16)
        wb_ref[pl.ds(s * HID, HID), :] = lax.dot_general(
            first, pick, cols, preferred_element_type=F32).astype(BF16)
    eye = jnp.where(iota((HID, HID), 0) == iota((HID, HID), 1), 0.5, 0.0).astype(BF16)
    eye16 = jnp.where(iota((16, 16), 0) == iota((16, 16), 1), 1.0, 0.0).astype(BF16)
    for layer, ref in ((0, w1_ref), (1, w2_ref)):
        turned = lax.dot_general(whid_ref[pl.ds(layer * HID, HID), :], eye, cols,
                                 preferred_element_type=F32)
        brow = jnp.concatenate(
            split(bias_ref[layer + 1 : layer + 2, :]) + [jnp.zeros((13, HID), F32)], axis=0
        ).astype(BF16)
        bcol = lax.dot_general(brow, eye16, cols, preferred_element_type=F32)
        ref[...] = jnp.concatenate([turned, bcol], axis=1).astype(BF16)
    wo_ref[...] = jnp.broadcast_to(0.5 * wout_ref[...].astype(F32), (16, HID)).astype(BF16)

    mhd_bulk(YG, yp_ref, u_ref, fz_ref, sz_ref, ch_ref, yadv_ref, 4, True)

    source, half, _, _ = brick_rows(bricks_ref, count_ref)
    tail = bias_rows(LANES)
    load = plane_loader(prim_ref)

    def up_of(f, z):
        return load(f, lax.rem(z + 1, NZ))

    def dn_of(f, z):
        return load(f, lax.rem(z + NZ - 1, NZ))

    @pl.loop(0, HALF, unroll=4)
    def _(z):
        both = [features(load, zz, up_of, dn_of) for zz in (z, z + HALF)]
        at = pl.ds(pl.multiple_of(z * LANES, LANES), LANES)
        for o in range(2):
            parts = []
            for a, b in zip(*both):
                a, b = a[o * 8 : o * 8 + 8], b[o * 8 : o * 8 + 8]
                parts.append(jnp.where(half == 1, take(b, source), take(a, source)))
            x_ref[pl.ds(o * KIN, KIN), at] = jnp.concatenate(parts + [tail], axis=0).astype(BF16)


def edge_kernel(bricks_ref, count_ref, prim_ref, bulk_ref, yp_ref, ybulk_ref, x_ref,
                xlo_ref, xhi_ref, yfl_ref, yfr_ref, wb_ref, w1_ref, w2_ref, wo_ref,
                rest_ref, badv_ref, yb_ref, ky_ref, kape_ref, sxlo_ref, sxhi_ref,
                lo_ref, hi_ref, yadv_ref):
    lane8 = iota((8, LANES), 1)
    sub = iota((8, LANES), 0)
    lo_ref[...] = xlo_ref[...].astype(F32)
    hi_ref[...] = xhi_ref[...].astype(F32)
    yrows = 8 * NZ

    yadv_ref[...] = ybulk_ref[...]
    badv_ref[...] = bulk_ref[pl.ds(4 * PLANE, 3 * PLANE), :]
    for lo in (True, False):
        start = 0 if lo else CX - 1
        ref = lo_ref if lo else hi_ref

        def add_window(c, step):
            at = pl.ds(c * YPLANE + start, YG, stride=CX)
            yadv_ref[at, :] = yadv_ref[at, :] + step

        x_ends(lambda f: yp_ref[pl.ds(f * YPLANE + start, YG, stride=CX), :],
               lambda f: ref[pl.ds(yrows + f * YG, YG), :], lo, add_window)
    yb_ref[...] = yadv_ref[pl.ds(4 * YPLANE, 3 * YPLANE), :]
    on_edge = jnp.logical_or(lane8 == 0, lane8 == LANES - 1)
    for c in (0, 1, 2, 3, 7):
        for z in range(NZ):
            b, g = z // YG, z % YG
            index = b * 32 + jnp.where(lane8 == LANES - 1, 25, 6)
            for o in range(2):
                at = pl.ds(c * PLANE + z * CX + o * 8, 8)
                edge = take(yadv_ref[pl.ds(c * YPLANE + g * CX + o * 8, 8), :], index)
                rest_ref[at, :] = jnp.where(on_edge, edge, bulk_ref[at, :])
    at_end = jnp.logical_or(lane8 == 0, lane8 == LANES - 1)
    for zs in range(0, NZ, 8):
        for lo in (True, False):
            start = zs * CX + (0 if lo else CX - 1)
            ref = lo_ref if lo else hi_ref

            def add_block(c, step):
                if 4 <= c < 7:
                    at = pl.ds((c - 4) * PLANE + start, 8, stride=CX)
                    badv_ref[at, :] = badv_ref[at, :] + step
                else:
                    at = pl.ds(c * PLANE + start, 8, stride=CX)
                    rest_ref[at, :] = rest_ref[at, :] + jnp.where(at_end, 0.0, step)

            x_ends(lambda f: prim_ref[pl.ds(f * PLANE + start, 8, stride=CX), :],
                   lambda f: ref[pl.ds(f * NZ + zs, 8), :], lo, add_block)

    source, half, back, ends = brick_rows(bricks_ref, count_ref)
    tail = bias_rows(LANES)
    parts = []
    for lo in (True, False):
        start = 0 if lo else CX - 1
        ref = lo_ref if lo else hi_ref

        def row_of(f, x=start):
            return prim_ref[pl.ds(f * PLANE + x, NZ, stride=CX), :]

        def dx(f, v):
            beyond = ref[pl.ds(f * NZ, NZ), :]
            within = row_of(f, start + (1 if lo else -1))
            return 0.5 * (within - beyond) if lo else 0.5 * (beyond - within)

        def dy(v):
            return 0.5 * (next_lane(v) - prev_lane(v))

        p = [row_of(f) for f in range(8)]

        def dz(f):
            return 0.5 * (next_row(p[f]) - prev_row(p[f]))

        fs = feature_list(p[0], p[1:4], p[4:7], p[7], dx, dy, dz)
        for q in range(2):
            packed = [jnp.where(half == 1, take(v[HALF + q * 8 : HALF + q * 8 + 8], source),
                                take(v[q * 8 : q * 8 + 8], source)) for v in fs]
            parts.append(jnp.concatenate(packed + [tail], axis=0))
    xend = jnp.concatenate(parts, axis=1).astype(BF16)

    def yload(f, z):
        return yp_ref[pl.ds((f * YG + z) * CX, CX), :]

    def yup(f, z):
        return yload(f, z + 1) if z + 1 < YG else pltpu.roll(yload(f, 0), LANES - 32, 1)

    def ydn(f, z):
        return yload(f, z - 1) if z > 0 else pltpu.roll(yload(f, YG - 1), 32, 1)

    def patch_x(f, z):
        at = pl.ds(yrows + f * YG + z, 1)
        return lo_ref[at, :], hi_ref[at, :]

    window, block = lane8 % 32, lane8 // 32
    inner = window % 8
    from_window = block * 32 + jnp.where(inner < 4, inner + 3, inner + 21)
    ycells = {(o, q): [jnp.zeros((8, LANES), F32)] * 8 for o in range(2) for q in range(2)}
    for g in range(YG):
        fs = features(yload, g, yup, ydn, patch_x)
        mine = window // 8 == g % 4
        for o in range(2):
            ycells[o, g // 4] = [jnp.where(mine, take(v[o * 8 : o * 8 + 8], from_window), a)
                                 for v, a in zip(fs, ycells[o, g // 4])]
    yend = jnp.concatenate([jnp.concatenate(ycells[o, q] + [tail], axis=0)
                            for o in range(2) for q in range(2)], axis=1).astype(BF16)

    us = []
    for o, s in ((0, 1), (0, 2), (1, 5), (1, 6)):
        us.append(jnp.dot(wb_ref[pl.ds(s * HID, HID), :], x_ref[pl.ds(o * KIN, KIN), :],
                          preferred_element_type=F32))
    for cells in (xend, yend):
        ue = [jnp.dot(wb_ref[pl.ds(s * HID, HID), :], cells, preferred_element_type=F32) for s in range(8)]
        for part in range(2):
            us.append(jnp.concatenate(ue[part * 4 : part * 4 + 4], axis=1))
    rates = closure_rates(us, w1_ref[...], w2_ref[...], wo_ref[...])

    def by_row(first, k):
        acc = jnp.zeros((8, LANES), F32)
        for s in range(8):
            at = (s % 4) * 512 + k * LANES
            acc = jnp.where(sub == s, rates[first + s // 4][:8, at : at + LANES], acc)
        return acc

    low = jnp.full((NZ, LANES), RATE_LOW, BF16)
    for e in range(6):
        packed = []
        for q in range(2):
            if e in (0, 5):
                acc = by_row(4, (0 if e == 0 else 2) + q)
            else:
                acc = jnp.zeros((8, LANES), F32)
                for k in range(8):
                    z = q * 8 + k
                    acc = jnp.where(sub == k, rates[e - 1][:8, z * LANES : (z + 1) * LANES], acc)
            packed.append(acc)
            kape_ref[pl.ds(e * HALF + q * 8, 8), :] = acc
        full = []
        for h in range(2):
            listed = back[h] >= 0
            for q in range(2):
                full.append(jnp.where(listed, take(packed[q], jnp.maximum(back[h], 0)), RATE_LOW))
        full = jnp.concatenate(full, axis=0).astype(BF16)
        if e < 3:
            sxlo_ref[pl.ds((12 + e) * NZ, NZ), :] = full
        else:
            sxhi_ref[pl.ds((12 + e - 2) * NZ, NZ), :] = full
    sxlo_ref[pl.ds(15 * NZ, NZ), :] = low
    sxhi_ref[pl.ds(12 * NZ, NZ), :] = low

    second = lane8 >= LANES // 2
    mine = jnp.where(window < 16, jnp.where(second, ends[1][0], ends[0][0]),
                     jnp.where(second, ends[1][1], ends[0][1]))
    left = yfl_ref[pl.ds(YROWS, 16), :].astype(F32)[:8]
    right = yfr_ref[pl.ds(YROWS, 16), :].astype(F32)[:8]
    listed = jnp.where(window < 6, left, jnp.where(window >= 26, right, mine.astype(F32))) > 0.5
    known = jnp.where(window < 16, window - 3, window - 21)
    known = jnp.minimum(jnp.maximum(known, 0), 7)
    for o in range(2):
        for q in range(2):
            got = by_row(6, o * 2 + q)
            for g in range(4):
                k = take(got, block * 32 + g * 8 + known)
                ky_ref[pl.ds((q * 4 + g) * CX + o * 8, 8), :] = jnp.where(listed, k, RATE_LOW)

    for f in range(3):
        for r in range(4):
            at = pl.ds((f * 4 + r) * NZ, NZ)
            sxlo_ref[at, :] = badv_ref[pl.ds(f * PLANE + r, NZ, stride=CX), :].astype(BF16)
            sxhi_ref[at, :] = badv_ref[pl.ds(f * PLANE + CX - 4 + r, NZ, stride=CX), :].astype(BF16)
    for f in range(4):
        ref, base = (yb_ref, f * YPLANE) if f < 3 else (ky_ref, 0)
        for dst, start in ((sxlo_ref, 0), (sxhi_ref, CX - 4)):
            for r in range(0, 4, 2):
                pair = [ref[pl.ds(base + start + r + k, YG, stride=CX), :] for k in range(2)]
                dst[pl.ds(16 * NZ + (f * 4 + r) * YG, 2 * YG), :] = jnp.concatenate(pair, axis=0).astype(BF16)


def inner_rates(o, x_ref, wb_ref, w1_ref, w2_ref, wo_ref, kp_ref):
    sub = iota((8, LANES), 0)
    which = range(3, 8) if o == 0 else range(5)
    us = [jnp.dot(wb_ref[pl.ds(s * HID, HID), :], x_ref[pl.ds(o * KIN, KIN), :],
                  preferred_element_type=F32) for s in which]
    rates = closure_rates(us, w1_ref[...], w2_ref[...], wo_ref[...])
    for z in range(HALF):
        acc = jnp.zeros((8, LANES), F32)
        for s, r in zip(which, rates):
            acc = jnp.where(sub == s, r[:8, z * LANES : (z + 1) * LANES], acc)
        kp_ref[pl.ds(z * 8, 8), :] = acc


def inner_kernel(bricks_ref, count_ref, x_ref, kape_ref, wb_ref, w1_ref, w2_ref, wo_ref,
                 kap_ref, kp_ref):
    rows = HALF * 8
    for o in range(2):
        inner_rates(o, x_ref, wb_ref, w1_ref, w2_ref, wo_ref, kp_ref.at[pl.ds(o * rows, rows), :])
    _, _, back, _ = brick_rows(bricks_ref, count_ref)
    for e in range(6):
        x = e if e < 3 else rows + 2 + e
        kp_ref[pl.ds(x, HALF, stride=8), :] = kape_ref[pl.ds(e * HALF, HALF), :]
    for h in range(2):
        listed = back[h] >= 0
        index = jnp.maximum(back[h], 0)
        for z in range(HALF):
            for o in range(2):
                k = kp_ref[pl.ds(o * rows + z * 8, 8), :]
                kap_ref[pl.ds((h * HALF + z) * CX + o * 8, 8), :] = jnp.where(
                    listed, take(k, index), RATE_LOW)


DEEP = CX + 8


def diffuse_kernel(rest_ref, b_ref, kap_ref, yb_ref, kapy_ref, xlo_ref, xhi_ref, out_ref,
                   m0, m1, km, y0, y1, ky, xl, xh):
    comp = pl.program_id(0)
    lane = iota((8, LANES), 1)
    window, block = lane % 32, lane // 32

    def build(field, own_ref, yown_ref, main, edge):
        for z in range(NZ):
            main[pl.ds(z * DEEP, CX), :] = own_ref[pl.ds(z * CX, CX), :]
        for g in range(YG):
            edge[pl.ds(g * DEEP, CX), :] = yown_ref[pl.ds(g * CX, CX), :]
        for r in range(4):
            for src, row in ((xh, CX + r), (xl, CX + 4 + r)):
                at = pl.ds(pl.multiple_of((field * 4 + r) * NZ, 8), NZ)
                main[pl.ds(row, NZ, stride=DEEP), :] = src[at, :]
                at = pl.ds(pl.multiple_of(16 * NZ + (field * 4 + r) * YG, 8), YG)
                edge[pl.ds(row, YG, stride=DEEP), :] = src[at, :]

    @pl.when(comp == 0)
    def _():
        xl[...] = xlo_ref[...].astype(F32)
        xh[...] = xhi_ref[...].astype(F32)
        build(3, kap_ref, kapy_ref, km, ky)
        own = jnp.where(window < 16, window - 6, LANES - 26 + window)
        own = jnp.minimum(jnp.maximum(own, 0), LANES - 1)
        made = jnp.logical_or(window < 7, window >= 25)
        for g in range(YG):
            for o in range(3):
                v = None
                for b in range(4):
                    piece = take(km[pl.ds((b * YG + g) * DEEP + o * 8, 8), :], own)
                    v = piece if v is None else jnp.where(block == b, piece, v)
                at = pl.ds(g * DEEP + o * 8, 8)
                ky[at, :] = jnp.where(made, ky[at, :], v)

    build(comp, b_ref, yb_ref, m0, y0)

    def relax(c, up, dn, k):
        total = next_row(c) + prev_row(c) + next_lane(c) + prev_lane(c) + (up + dn)
        return c + k * (total - 6.0 * c)

    def at(z):
        return pl.ds(z * DEEP, DEEP)

    on_edge = jnp.logical_or(lane < 5, lane >= LANES - 5)
    mains, edges = (m0, m1), (y0, y1)
    for step in range(SUB):
        a, b = mains[step % 2], mains[1 - step % 2]
        ea, eb = edges[step % 2], edges[1 - step % 2]
        for g in range(YG):
            up = ea[at(g + 1), :] if g + 1 < YG else pltpu.roll(ea[at(0), :], LANES - 32, 1)
            dn = ea[at(g - 1), :] if g > 0 else pltpu.roll(ea[at(YG - 1), :], 32, 1)
            eb[at(g), :] = relax(ea[at(g), :], up, dn, ky[at(g), :])
        dn, c = a[at(NZ - 1), :], a[at(0), :]
        for z in range(NZ):
            up = a[at((z + 1) % NZ), :]
            new = relax(c, up, dn, km[at(z), :])
            dn, c = c, up
            if step < SUB - 1:
                b[at(z), :] = new
                continue
            k, g = z // YG, z % YG
            index = k * 32 + jnp.where(lane < 5, 6 + lane, lane - (LANES - 26))
            index = jnp.minimum(jnp.maximum(index, 0), LANES - 1)
            for o in range(2):
                e = take(eb[pl.ds(g * DEEP + o * 8, 8), :], index)
                out_ref[pl.ds(z * CX + o * 8, 8), :] = jnp.where(on_edge, e, new[o * 8 : o * 8 + 8])


def struct(shape, dtype=F32):
    return jax.ShapeDtypeStruct(shape, dtype)


def params():
    return pltpu.CompilerParams(vmem_limit_bytes=VMEM_LIMIT)


def cost(us):
    return pl.CostEstimate(flops=us * 500_000_000, bytes_accessed=us << 20, transcendentals=0)


VSPEC = pl.BlockSpec(memory_space=pltpu.VMEM)
SSPEC = pl.BlockSpec(memory_space=pltpu.SMEM)


def step_up(axis):
    n = lax.axis_size(axis)
    return [(i, (i + 1) % n) for i in range(n)]


def step_down(axis):
    n = lax.axis_size(axis)
    return [((i + 1) % n, i) for i in range(n)]


def shards(primitive, current_sheet_bricks, brick_count, w_in, w_hid, w_out, b_hid):
    shape = primitive.shape
    prim = primitive.reshape(8 * PLANE, LANES)
    bricks = current_sheet_bricks.reshape(1, -1)
    count = brick_count.reshape(1, 1)

    blo, bhi = pl.pallas_call(
        pack_kernel,
        in_specs=[SSPEC, SSPEC, VSPEC],
        out_shape=[struct((YROWS + 16, LANES), BF16)] * 2,
        compiler_params=params(),
        name="pack",
    )(bricks, count, prim)
    yfl = lax.ppermute(bhi, "row", step_up("row"))
    yfr = lax.ppermute(blo, "row", step_down("row"))

    def mhd_scratch(planes):
        many = pltpu.VMEM((8 * planes * CX, LANES), F32)
        return [many, many, pltpu.VMEM((planes * CX, LANES), F32), many]

    adv, xmlo, xmhi = pl.pallas_call(
        bulk_kernel,
        out_shape=[struct((8 * PLANE, LANES))] + [struct((8 * NZ, LANES), BF16)] * 2,
        scratch_shapes=mhd_scratch(NZ),
        compiler_params=params(),
        cost_estimate=cost(4),
        name="bulk",
    )(prim)

    sxrows = 8 * NZ + 8 * YG
    yp, slo, shi = pl.pallas_call(
        window_kernel,
        out_shape=[struct((8 * YPLANE, LANES))] + [struct((sxrows, LANES), BF16)] * 2,
        scratch_shapes=[pltpu.VMEM((YROWS, LANES), F32)] * 2,
        compiler_params=params(),
        cost_estimate=cost(1),
        name="windows",
    )(prim, yfl, yfr, xmlo, xmhi)
    xlo = lax.ppermute(shi, "col", step_up("col"))
    xhi = lax.ppermute(slo, "col", step_down("col"))

    weights = [struct((8 * HID, KIN), BF16), struct((HID, KHID), BF16), struct((HID, KHID), BF16),
               struct((16, HID), BF16)]
    yadv, xcells, *closure = pl.pallas_call(
        ready_kernel,
        in_specs=[SSPEC, SSPEC] + [VSPEC] * 6,
        out_shape=[struct((8 * YPLANE, LANES)), struct((2 * KIN, WIDE), BF16)] + weights,
        scratch_shapes=mhd_scratch(YG),
        compiler_params=params(),
        cost_estimate=cost(4),
        name="ready",
    )(bricks, count, prim, yp, w_in, w_hid.reshape(2 * HID, HID), w_out.reshape(1, HID), b_hid)

    xrows = 16 * NZ + 16 * YG
    rest, badv, yb, ky, kape, sxlo, sxhi = pl.pallas_call(
        edge_kernel,
        in_specs=[SSPEC, SSPEC] + [VSPEC] * 13,
        out_shape=[struct((8 * PLANE, LANES)), struct((3 * PLANE, LANES)), struct((3 * YPLANE, LANES)),
                   struct((YPLANE, LANES)), struct((6 * HALF, LANES)),
                   struct((xrows, LANES), BF16), struct((xrows, LANES), BF16)],
        scratch_shapes=[pltpu.VMEM((sxrows, LANES), F32)] * 2 + [pltpu.VMEM((8 * YPLANE, LANES), F32)],
        compiler_params=params(),
        cost_estimate=cost(8),
        name="edges",
    )(bricks, count, prim, adv, yp, yadv, xcells, xlo, xhi, yfl, yfr, *closure)

    gothi = lax.ppermute(sxlo, "col", step_down("col"))
    gotlo = lax.ppermute(sxhi, "col", step_up("col"))

    kap = pl.pallas_call(
        inner_kernel,
        in_specs=[SSPEC, SSPEC] + [VSPEC] * 6,
        out_shape=struct((PLANE, LANES)),
        scratch_shapes=[pltpu.VMEM((HALF * CX, LANES), F32)],
        compiler_params=params(),
        cost_estimate=cost(6),
        name="inner",
    )(bricks, count, xcells, kape, *closure)

    full = lambda rows: pl.BlockSpec((rows, LANES), lambda c: (0, 0))
    part = lambda rows: pl.BlockSpec((rows, LANES), lambda c: (c, 0))
    out = pl.pallas_call(
        diffuse_kernel,
        grid=(3,),
        in_specs=[pl.BlockSpec(memory_space=pl.ANY), part(PLANE), full(PLANE), part(YPLANE), full(YPLANE),
                  full(xrows), full(xrows)],
        out_specs=pl.BlockSpec((PLANE, LANES), lambda c: (4 + c, 0)),
        out_shape=struct((8 * PLANE, LANES)),
        input_output_aliases={0: 0},
        scratch_shapes=[pltpu.VMEM((NZ * DEEP, LANES), F32)] * 3
        + [pltpu.VMEM((YG * DEEP, LANES), F32)] * 3
        + [pltpu.VMEM((xrows, LANES), F32)] * 2,
        compiler_params=params(),
        name="diffuse",
    )(rest, badv, kap, yb, ky, gotlo, gothi)
    return out.reshape(shape)


def solution(mesh):
    return jax.shard_map(
        shards,
        mesh=mesh,
        in_specs=(
            P(None, None, "col", "row"),
            P("row", "col", None),
            P("row", "col"),
            P(),
            P(),
            P(),
            P(),
        ),
        out_specs=P(None, None, "col", "row"),
        check_vma=False,
    )
```

time: 48.1 us -> 44 us (0.915)
  starting transfers between devices: 14.3 us -> 10.5 us
  Pallas kernels: 31.2 us -> 28.9 us
  local copies, waits for them, and re-layouts: 1.63 us -> 3.59 us
    ppermute x8 -> x6, starting transfers between devices: 14.3 us -> 10.5 us  [the longest x1 3.08 us: shards(): yfl = lax.ppermute(bhi, 'row', step_up('row'))]
    unnamed x14 -> x16, local copies, waits for them, and re-layouts: 1.63 us -> 3.59 us
    pallas_call x5, Pallas kernels: 19.7 us -> 18.6 us  [the longest x1 8.53 us: shards(): pl.pallas_call(edge_kernel, in_specs=[SSPEC, SSPEC] + [VSPEC] * 13, out_s...]
    pallas_call x1, Pallas kernels: 5.75 us -> 4.58 us  [shards(): pl.pallas_call(diffuse_kernel, grid=(3,), in_specs=[pl.BlockSpec(memory_s...]
  transfers between devices with their start and end apart: 8 -> 6, of which waited for: 0 -> 0; matrix products, arithmetic and copies ran while one was open for 0% -> 0% of each run, Pallas kernels for 32% -> 29%
where the time goes in v2:
time: 44 us; the launch traced here: 43.8 us
  Pallas kernels  28.9 us (66%)
  starting transfers between devices  10.5 us (24%)
  local copies, waits for them, and re-layouts  3.59 us (8%)
  between operations  0.78 us (2%)
    pallas_call x1, Pallas kernels, shards(): pl.pallas_call(edge_kernel, in_specs=[SSPEC, SSPEC] + [VSPEC] * 13, out_s...  8.53 us
    pallas_call x1, Pallas kernels, shards(): pl.pallas_call(inner_kernel, in_specs=[SSPEC, SSPEC] + [VSPEC] * 6, out_s...  5.76 us
    pallas_call x1, Pallas kernels, shards(): pl.pallas_call(diffuse_kernel, grid=(3,), in_specs=[pl.BlockSpec(memory_s...  4.58 us
    pallas_call x1, Pallas kernels, shards(): pl.pallas_call(bulk_kernel, out_shape=[struct((8 * PLANE, LANES))] + [str...  3.68 us
    unnamed x16, local copies, waits for them, and re-layouts  3.59 us
    pallas_call x1, Pallas kernels, shards(): pl.pallas_call(ready_kernel, in_specs=[SSPEC, SSPEC] + [VSPEC] * 6, out_s...  3.47 us
    ppermute x1, starting transfers between devices, shards(): yfl = lax.ppermute(bhi, 'row', step_up('row'))  3.08 us
    ppermute x1, starting transfers between devices, shards(): gothi = lax.ppermute(sxlo, 'col', step_down('col'))  2.64 us
  transfers between devices with their start and end apart: 6, of which 0 were waited for; matrix products, arithmetic and copies ran while one was open for 0% of the time, Pallas kernels for 29%

profile of v2, /device:TPU:0, one launch (start us, length us, event | category | flops | bytes accessed | tf_op | source)
XLA Modules:
  0.0 43.8 jit_solution(5027657161749417889)
XLA Ops:
  0.7 0.0 copy-start
  0.7 1.6 %copy-done = f32[8,32,16,128]{3,2,1,0:T(8,128)S(1)} copy-done((f32[8,32,16,128]{3,2,1,0:T(8,128)S(1)}, f32[8,32,16,128]{3,2,1,0:T(8,128)}, u32[]{:S(2)}) %copy-start) | copy-done | bytes 2097176
  2.2 0.7 %copy-done.1 = s32[1,1,8]{2,1,0:T(1,128)S(1)} copy-done((s32[1,1,8]{2,1,0:T(1,128)S(1)}, s32[1,1,8]{2,1,0:T(1,128)}, u32[]{:S(2)}) %copy-start.1) | copy-done | bytes 56
  2.9 1.2 %pack.1 = (bf16[272,128]{1,0:T(8,128)(2,1)S(1)}, bf16[272,128]{1,0:T(8,128)(2,1)S(1)}) custom-call(s32[1,8]{1,0:T(1,128)S(1)} %bitcast.10, s32[1,1]{1,0:T(1,128)S(6)} %copy.10.count_ref, f32[4096,128]{1,0:T(8,128)S(1)} %bitcast.5), custom_call_target="tpu_custom_call" | custom-call | tf_op jit(solution)/shard_map/pack/pallas_call | solution.py:684
  4.1 3.1 %collective-permute-start = (bf16[272,128]{1,0:T(8,128)(2,1)S(1)}, bf16[272,128]{1,0:T(8,128)(2,1)S(1)}, u32[]{:S(2)}, u32[]{:S(2)}) collective-permute-start(bf16[272,128]{1,0:T(8,128)(2,1)S(1)} %get-tuple-element.27), channel_id=1, source_target_pairs={{0,8},{8,16},{16,24},{24,0},{1,9},{9,17},{17,25},{25,1},{2,10},{10... | collective-permute-start | bytes 208904 | tf_op jit(solution)/shard_map/ppermute | solution.py:691
  7.1 2.1 %collective-permute-start.1 = (bf16[272,128]{1,0:T(8,128)(2,1)S(1)}, bf16[272,128]{1,0:T(8,128)(2,1)S(1)}, u32[]{:S(2)}, u32[]{:S(2)}) collective-permute-start(bf16[272,128]{1,0:T(8,128)(2,1)S(1)} %get-tuple-element.28), channel_id=1, source_target_pairs={{8,0},{16,8},{24,16},{0,24},{9,1},{17,9},{25,17},{1,25},{10,2},{18... | collective-permute-start | bytes 208904 | tf_op jit(solution)/shard_map/ppermute | solution.py:692
  9.2 3.7 %bulk.1 = (f32[4096,128]{1,0:T(8,128)S(1)}, bf16[256,128]{1,0:T(8,128)(2,1)S(1)}, bf16[256,128]{1,0:T(8,128)(2,1)S(1)}) custom-call(f32[4096,128]{1,0:T(8,128)S(1)} %bitcast.6), custom_call_target="tpu_custom_call" | custom-call | flops 2000000000 | bytes 4194304 | tf_op jit(solution)/shard_map/bulk/pallas_call | solution.py:698
  12.9 1.3 %copy-done.7 = f32[4096,128]{1,0:T(8,128)} copy-done((f32[4096,128]{1,0:T(8,128)}, f32[4096,128]{1,0:T(8,128)S(1)}, u32[]{:S(2)}) %copy-start.7) | copy-done | bytes 2097176
  14.3 0.0 copy-start.6
  14.3 0.0 collective-permute-done.yfl_ref
  14.3 0.0 collective-permute-done.1.yfr_ref
  14.3 1.7 %windows.1 = (f32[1024,128]{1,0:T(8,128)S(1)}, bf16[320,128]{1,0:T(8,128)(2,1)S(1)}, bf16[320,128]{1,0:T(8,128)(2,1)S(1)}) custom-call(f32[4096,128]{1,0:T(8,128)S(1)} %bitcast.7, bf16[272,128]{1,0:T(8,128)(2,1)S(1)} %collective-permute-done.yfl_ref, bf16[272,128]{1,0:T(8,128)(2,1)S(1)} %collective-permute-done.1.yfr_ref, ...), custom_call_target="tpu_custom_call" | custom-call | flops 500000000 | bytes 1048576 | tf_op jit(solution)/shard_map/windows/pallas_call | solution.py:708
  16.0 0.1 collective-permute-start.2
  16.1 2.6 %collective-permute-start.3 = (bf16[320,128]{1,0:T(8,128)(2,1)S(1)}, bf16[320,128]{1,0:T(8,128)(2,1)S(1)}, u32[]{:S(2)}, u32[]{:S(2)}) collective-permute-start(bf16[320,128]{1,0:T(8,128)(2,1)S(1)} %get-tuple-element.35), channel_id=1, source_target_pairs={{1,0},{2,1},{3,2},{4,3},{5,4},{6,5},{7,6},{0,7},{9,8},{10,9},{11,1... | collective-permute-start | bytes 245768 | tf_op jit(solution)/shard_map/ppermute | solution.py:717
  18.7 3.5 %ready.1 = (f32[1024,128]{1,0:T(8,128)S(1)}, bf16[160,2048]{1,0:T(8,128)(2,1)S(1)}, bf16[1024,80]{1,0:T(8,128)(2,1)S(1)}, bf16[128,144]{1,0:T(8,128)(2,1)S(1)}, ...) custom-call(s32[1,8]{1,0:T(1,128)S(1)} %bitcast.11, s32[1,1]{1,0:T(1,128)S(6)} %copy.10.count_ref, ...), custom_call_target="tpu_custom_call" | custom-call | flops 2000000000 | bytes 4194304 | tf_op jit(solution)/shard_map/ready/pallas_call | solution.py:721
  22.2 0.0 collective-permute-done.2.xlo_ref
  22.2 0.0 collective-permute-done.3.xhi_ref
  22.2 8.5 %edges.1 = (f32[4096,128]{1,0:T(8,128)}, f32[1536,128]{1,0:T(8,128)S(1)}, f32[384,128]{1,0:T(8,128)S(1)}, f32[128,128]{1,0:T(8,128)S(1)}, f32[96,128]{1,0:T(8,12...) custom-call(s32[1,8]{1,0:T(1,128)S(1)} %bitcast.12, s32[1,1]{1,0:T(1,128)S(6)} %copy.10.count_ref, ...), custom_call_target="tpu_custom_call" | custom-call | flops 4000000000 | bytes 8388608 | tf_op jit(solution)/shard_map/edges/pallas_call | solution.py:732
  30.8 0.0 collective-permute-start.4
  30.8 2.6 %collective-permute-start.5 = (bf16[640,128]{1,0:T(8,128)(2,1)S(1)}, bf16[640,128]{1,0:T(8,128)(2,1)S(1)}, u32[]{:S(2)}, u32[]{:S(2)}) collective-permute-start(bf16[640,128]{1,0:T(8,128)(2,1)S(1)} %get-tuple-element.46), channel_id=1, source_target_pairs={{1,0},{2,1},{3,2},{4,3},{5,4},{6,5},{7,6},{0,7},{9,8},{10,9},{11,1... | collective-permute-start | bytes 491528 | tf_op jit(solution)/shard_map/ppermute | solution.py:744
  33.4 5.8 %inner.1.kap_ref = f32[512,128]{1,0:T(8,128)S(1)} custom-call(s32[1,8]{1,0:T(1,128)S(1)} %bitcast.13, s32[1,1]{1,0:T(1,128)S(6)} %copy.10.count_ref, bf16[160,2048]{1,0:T(8,128)(2,1)S(1)} %get-tuple-element.33.x_ref, f32[96,128]{1,0:T(8,128)S(1)} %get-tuple-element.42.kape_ref, bf16[1024,80]{1,0:T(8,128)(2,1)S(1)} %get-tuple-element.36.wb_ref, ...), custom_call_target="tpu_custom_call" | custom-call | flops 3000000000 | bytes 6291456 | tf_op jit(solution)/shard_map/inner/pallas_call | solution.py:747
  39.2 0.0 collective-permute-done.4.xlo_ref
  39.2 0.0 collective-permute-done.5.xhi_ref
  39.2 4.6 %diffuse.1 = f32[4096,128]{1,0:T(8,128)} custom-call(f32[4096,128]{1,0:T(8,128)} %get-tuple-element.40.rest_ref, f32[1536,128]{1,0:T(8,128)S(1)} %get-tuple-element.41.b_ref, f32[512,128]{1,0:T(8,128)S(1)} %inner.1.kap_ref, f32[384,128]{1,0:T(8,128)S(1)} %get-tuple-element.43.yb_ref, ...), custom_call_target="tpu_custom_call", output_to_operand_aliasing={{}: (0, {})} | custom-call | tf_op jit(solution)/shard_map/diffuse/pallas_call | solution.py:759
  (11 shorter events, 0.0 us)
Async XLA Ops:
  0.7 1.6 %copy-start = (f32[8,32,16,128]{3,2,1,0:T(8,128)S(1)}, f32[8,32,16,128]{3,2,1,0:T(8,128)}, u32[]{:S(2)}) copy-start(f32[8,32,16,128]{3,2,1,0:T(8,128)} %param.7) | copy-start | bytes 6291460
  2.2 0.7 %copy-start.1 = (s32[1,1,8]{2,1,0:T(1,128)S(1)}, s32[1,1,8]{2,1,0:T(1,128)}, u32[]{:S(2)}) copy-start(s32[1,1,8]{2,1,0:T(1,128)} %param.8) | copy-start | bytes 100
  4.1 10.2 %collective-permute-start = (bf16[272,128]{1,0:T(8,128)(2,1)S(1)}, bf16[272,128]{1,0:T(8,128)(2,1)S(1)}, u32[]{:S(2)}, u32[]{:S(2)}) collective-permute-start(bf16[272,128]{1,0:T(8,128)(2,1)S(1)} %get-tuple-element.27), channel_id=1, source_target_pairs={{0,8},{8,16},{16,24},{24,0},{1,9},{9,17},{17,25},{25,1},{2,10},{10... | collective-permute-start | bytes 208904 | tf_op jit(solution)/shard_map/ppermute | solution.py:691
  7.1 7.2 %collective-permute-start.1 = (bf16[272,128]{1,0:T(8,128)(2,1)S(1)}, bf16[272,128]{1,0:T(8,128)(2,1)S(1)}, u32[]{:S(2)}, u32[]{:S(2)}) collective-permute-start(bf16[272,128]{1,0:T(8,128)(2,1)S(1)} %get-tuple-element.28), channel_id=1, source_target_pairs={{8,0},{16,8},{24,16},{0,24},{9,1},{17,9},{25,17},{1,25},{10,2},{18... | collective-permute-start | bytes 208904 | tf_op jit(solution)/shard_map/ppermute | solution.py:692
  12.9 1.3 %copy-start.7 = (f32[4096,128]{1,0:T(8,128)}, f32[4096,128]{1,0:T(8,128)S(1)}, u32[]{:S(2)}) copy-start(f32[4096,128]{1,0:T(8,128)S(1)} %get-tuple-element.26.bulk_ref) | copy-start | bytes 6291460
  14.3 4.5 %copy-start.2 = (s32[1,1,8]{2,1,0:T(1,128)S(1)}, s32[1,1,8]{2,1,0:T(1,128)}, u32[]{:S(2)}) copy-start(s32[1,1,8]{2,1,0:T(1,128)} %param.8) | copy-start | bytes 100
  14.3 4.5 %copy-start.3 = (bf16[2,128,128]{2,1,0:T(8,128)(2,1)S(1)}, bf16[2,128,128]{2,1,0:T(8,128)(2,1)}, u32[]{:S(2)}) copy-start(bf16[2,128,128]{2,1,0:T(8,128)(2,1)} %param.11) | copy-start | bytes 196612
  14.3 4.5 %copy-start.4 = (bf16[8,128]{1,0:T(8,128)(2,1)S(1)}, bf16[8,128]{1,0:T(8,128)(2,1)}, u32[]{:S(2)}) copy-start(bf16[8,128]{1,0:T(8,128)(2,1)} %win_ref.1) | copy-start | bytes 6148
  14.3 4.5 %copy-start.5 = (f32[3,128]{1,0:T(4,128)S(1)}, f32[3,128]{1,0:T(4,128)}, u32[]{:S(2)}) copy-start(f32[3,128]{1,0:T(4,128)} %bias_ref.1) | copy-start | bytes 4612
  14.3 4.5 %copy-start.6 = (bf16[128]{0:T(256)(128)(2,1)S(1)}, bf16[128]{0:T(256)(128)(2,1)}, u32[]{:S(2)}) copy-start(bf16[128]{0:T(256)(128)(2,1)} %param.12) | copy-start | bytes 772
  16.0 6.2 %collective-permute-start.2 = (bf16[320,128]{1,0:T(8,128)(2,1)S(1)}, bf16[320,128]{1,0:T(8,128)(2,1)S(1)}, u32[]{:S(2)}, u32[]{:S(2)}) collective-permute-start(bf16[320,128]{1,0:T(8,128)(2,1)S(1)} %get-tuple-element.34), channel_id=1, source_target_pairs={{0,1},{1,2},{2,3},{3,4},{4,5},{5,6},{6,7},{7,0},{8,9},{9,10},{10,1... | collective-permute-start | bytes 245768 | tf_op jit(solution)/shard_map/ppermute | solution.py:716
  16.1 6.1 %collective-permute-start.3 = (bf16[320,128]{1,0:T(8,128)(2,1)S(1)}, bf16[320,128]{1,0:T(8,128)(2,1)S(1)}, u32[]{:S(2)}, u32[]{:S(2)}) collective-permute-start(bf16[320,128]{1,0:T(8,128)(2,1)S(1)} %get-tuple-element.35), channel_id=1, source_target_pairs={{1,0},{2,1},{3,2},{4,3},{5,4},{6,5},{7,6},{0,7},{9,8},{10,9},{11,1... | collective-permute-start | bytes 245768 | tf_op jit(solution)/shard_map/ppermute | solution.py:717
  30.8 8.4 %collective-permute-start.4 = (bf16[640,128]{1,0:T(8,128)(2,1)S(1)}, bf16[640,128]{1,0:T(8,128)(2,1)S(1)}, u32[]{:S(2)}, u32[]{:S(2)}) collective-permute-start(bf16[640,128]{1,0:T(8,128)(2,1)S(1)} %get-tuple-element.45), channel_id=1, source_target_pairs={{0,1},{1,2},{2,3},{3,4},{4,5},{5,6},{6,7},{7,0},{8,9},{9,10},{10,1... | collective-permute-start | bytes 491528 | tf_op jit(solution)/shard_map/ppermute | solution.py:745
  30.8 8.4 %collective-permute-start.5 = (bf16[640,128]{1,0:T(8,128)(2,1)S(1)}, bf16[640,128]{1,0:T(8,128)(2,1)S(1)}, u32[]{:S(2)}, u32[]{:S(2)}) collective-permute-start(bf16[640,128]{1,0:T(8,128)(2,1)S(1)} %get-tuple-element.46), channel_id=1, source_target_pairs={{1,0},{2,1},{3,2},{4,3},{5,4},{6,5},{7,6},{0,7},{9,8},{10,9},{11,1... | collective-permute-start | bytes 491528 | tf_op jit(solution)/shard_map/ppermute | solution.py:744

commit v3 on v2

--- a/solution.py
+++ b/solution.py
@@ -22,7 +22,6 @@
 PLANE = NZ * CX
 KIN = 80
 KHID = HID + 16
-VMEM_LIMIT = 48 << 20
 
 
 def iota(shape, dim):
@@ -155,10 +154,22 @@
 YROWS = 8 * 2 * CX
 
 
-def pack_kernel(bricks_ref, count_ref, prim_ref, lo_ref, hi_ref):
+def pack_kernel(bricks_hbm, count_hbm, hbm_ref, lo_ref, hi_ref, maps_ref, prim_ref, bricks_ref, count_ref, sems):
     lane = iota((8, LANES), 1)
     spot = lane % ENDS
+
+    def fetch(f):
+        at = pl.ds(f * PLANE, PLANE)
+        return pltpu.make_async_copy(hbm_ref.at[at, :], prim_ref.at[at, :], sems.at[f])
+
     for f in range(8):
+        fetch(f).start()
+    lists = [pltpu.make_async_copy(bricks_hbm, bricks_ref, sems.at[8]),
+             pltpu.make_async_copy(count_hbm, count_ref, sems.at[9])]
+    for copy in lists:
+        copy.start()
+    for f in range(8):
+        fetch(f).wait()
         for h in range(2):
             los, his = [], []
             for o in range(2):
@@ -174,11 +185,15 @@
             at = pl.ds((f * 2 + h) * CX, CX)
             lo_ref[at, :] = jnp.concatenate(los, axis=0).astype(BF16)
             hi_ref[at, :] = jnp.concatenate(his, axis=0).astype(BF16)
-    _, _, _, ends = brick_rows(bricks_ref, count_ref)
-    second = iota((16, LANES), 1) >= LANES // 2
-    for ref, side in ((lo_ref, 0), (hi_ref, 1)):
-        flag = jnp.where(second, ends[1][side], ends[0][side])
-        ref[pl.ds(YROWS, 16), :] = flag.astype(F32).astype(BF16)
+    for copy in lists:
+        copy.wait()
+    source, half, back, ends = brick_rows(bricks_ref, count_ref)
+    second = lane >= LANES // 2
+    listed = [jnp.where(second, ends[1][side], ends[0][side]) for side in range(2)]
+    for k, v in enumerate([source, half] + back + listed):
+        maps_ref[pl.ds(k * 8, 8), :] = v
+    for ref, flag in ((lo_ref, listed[0]), (hi_ref, listed[1])):
+        ref[pl.ds(YROWS, 16), :] = jnp.concatenate([flag, flag], axis=0).astype(F32).astype(BF16)
 
 
 def brick_rows(bricks_ref, count_ref):
@@ -201,6 +216,11 @@
             for side, end in enumerate((0, per_half - 1)):
                 ends[h][side] = jnp.where(want == end, 1, ends[h][side])
     return source, half, back, ends
+
+
+def read_maps(maps_ref):
+    source, half, back0, back1, low, high = [maps_ref[pl.ds(k * 8, 8), :] for k in range(6)]
+    return source, half, [back0, back1], [low, high]
 
 
 def mhd_bulk(count, prim_ref, u_ref, fz_ref, sz_ref, ch_ref, out_ref, unroll, windows):
@@ -313,7 +333,7 @@
                 pl.ds(f * YPLANE + start, 2 * YG, stride=CX), :].astype(BF16)
 
 
-def ready_kernel(bricks_ref, count_ref, prim_ref, yp_ref, win_ref, whid_ref, wout_ref, bias_ref,
+def ready_kernel(maps_ref, prim_ref, yp_ref, win_ref, whid_ref, wout_ref, bias_ref,
                  yadv_ref, x_ref, wb_ref, w1_ref, w2_ref, wo_ref,
                  u_ref, fz_ref, sz_ref, ch_ref):
     def split(b):
@@ -347,7 +367,7 @@
 
     mhd_bulk(YG, yp_ref, u_ref, fz_ref, sz_ref, ch_ref, yadv_ref, 4, True)
 
-    source, half, _, _ = brick_rows(bricks_ref, count_ref)
+    source, half, _, _ = read_maps(maps_ref)
     tail = bias_rows(LANES)
     load = plane_loader(prim_ref)
 
@@ -369,7 +389,7 @@
             x_ref[pl.ds(o * KIN, KIN), at] = jnp.concatenate(parts + [tail], axis=0).astype(BF16)
 
 
-def edge_kernel(bricks_ref, count_ref, prim_ref, bulk_ref, yp_ref, ybulk_ref, x_ref,
+def edge_kernel(maps_ref, prim_ref, bulk_ref, yp_ref, ybulk_ref, x_ref,
                 xlo_ref, xhi_ref, yfl_ref, yfr_ref, wb_ref, w1_ref, w2_ref, wo_ref,
                 rest_ref, badv_ref, yb_ref, ky_ref, kape_ref, sxlo_ref, sxhi_ref,
                 lo_ref, hi_ref, yadv_ref):
@@ -394,13 +414,15 @@
     yb_ref[...] = yadv_ref[pl.ds(4 * YPLANE, 3 * YPLANE), :]
     on_edge = jnp.logical_or(lane8 == 0, lane8 == LANES - 1)
     for c in (0, 1, 2, 3, 7):
+        k = c if c < 4 else 4
         for z in range(NZ):
             b, g = z // YG, z % YG
             index = b * 32 + jnp.where(lane8 == LANES - 1, 25, 6)
             for o in range(2):
                 at = pl.ds(c * PLANE + z * CX + o * 8, 8)
                 edge = take(yadv_ref[pl.ds(c * YPLANE + g * CX + o * 8, 8), :], index)
-                rest_ref[at, :] = jnp.where(on_edge, edge, bulk_ref[at, :])
+                to = pl.ds(k * PLANE + z * CX + o * 8, 8)
+                rest_ref[to, :] = jnp.where(on_edge, edge, bulk_ref[at, :])
     at_end = jnp.logical_or(lane8 == 0, lane8 == LANES - 1)
     for zs in range(0, NZ, 8):
         for lo in (True, False):
@@ -412,13 +434,13 @@
                     at = pl.ds((c - 4) * PLANE + start, 8, stride=CX)
                     badv_ref[at, :] = badv_ref[at, :] + step
                 else:
-                    at = pl.ds(c * PLANE + start, 8, stride=CX)
+                    at = pl.ds(min(c, 4) * PLANE + start, 8, stride=CX)
                     rest_ref[at, :] = rest_ref[at, :] + jnp.where(at_end, 0.0, step)
 
             x_ends(lambda f: prim_ref[pl.ds(f * PLANE + start, 8, stride=CX), :],
                    lambda f: ref[pl.ds(f * NZ + zs, 8), :], lo, add_block)
 
-    source, half, back, ends = brick_rows(bricks_ref, count_ref)
+    source, half, back, ends = read_maps(maps_ref)
     tail = bias_rows(LANES)
     parts = []
     for lo in (True, False):
@@ -517,9 +539,7 @@
     sxlo_ref[pl.ds(15 * NZ, NZ), :] = low
     sxhi_ref[pl.ds(12 * NZ, NZ), :] = low
 
-    second = lane8 >= LANES // 2
-    mine = jnp.where(window < 16, jnp.where(second, ends[1][0], ends[0][0]),
-                     jnp.where(second, ends[1][1], ends[0][1]))
+    mine = jnp.where(window < 16, ends[0], ends[1])
     left = yfl_ref[pl.ds(YROWS, 16), :].astype(F32)[:8]
     right = yfr_ref[pl.ds(YROWS, 16), :].astype(F32)[:8]
     listed = jnp.where(window < 6, left, jnp.where(window >= 26, right, mine.astype(F32))) > 0.5
@@ -558,12 +578,12 @@
         kp_ref[pl.ds(z * 8, 8), :] = acc
 
 
-def inner_kernel(bricks_ref, count_ref, x_ref, kape_ref, wb_ref, w1_ref, w2_ref, wo_ref,
+def inner_kernel(maps_ref, x_ref, kape_ref, wb_ref, w1_ref, w2_ref, wo_ref,
                  kap_ref, kp_ref):
     rows = HALF * 8
     for o in range(2):
         inner_rates(o, x_ref, wb_ref, w1_ref, w2_ref, wo_ref, kp_ref.at[pl.ds(o * rows, rows), :])
-    _, _, back, _ = brick_rows(bricks_ref, count_ref)
+    _, _, back, _ = read_maps(maps_ref)
     for e in range(6):
         x = e if e < 3 else rows + 2 + e
         kp_ref[pl.ds(x, HALF, stride=8), :] = kape_ref[pl.ds(e * HALF, HALF), :]
@@ -581,41 +601,42 @@
 
 
 def diffuse_kernel(rest_ref, b_ref, kap_ref, yb_ref, kapy_ref, xlo_ref, xhi_ref, out_ref,
-                   m0, m1, km, y0, y1, ky, xl, xh):
-    comp = pl.program_id(0)
+                   m0, m1, km, y0, y1, ky, xl, xh, done, sems):
+    copies = [pltpu.make_async_copy(rest_ref.at[pl.ds(0, 4 * PLANE), :],
+                                    out_ref.at[pl.ds(0, 4 * PLANE), :], sems.at[0]),
+              pltpu.make_async_copy(rest_ref.at[pl.ds(4 * PLANE, PLANE), :],
+                                    out_ref.at[pl.ds(7 * PLANE, PLANE), :], sems.at[1])]
+    for copy in copies:
+        copy.start()
     lane = iota((8, LANES), 1)
     window, block = lane % 32, lane // 32
 
-    def build(field, own_ref, yown_ref, main, edge):
+    def build(field, own_ref, own_at, yown_ref, yown_at, main, edge):
         for z in range(NZ):
-            main[pl.ds(z * DEEP, CX), :] = own_ref[pl.ds(z * CX, CX), :]
+            main[pl.ds(z * DEEP, CX), :] = own_ref[pl.ds(own_at + z * CX, CX), :]
         for g in range(YG):
-            edge[pl.ds(g * DEEP, CX), :] = yown_ref[pl.ds(g * CX, CX), :]
+            edge[pl.ds(g * DEEP, CX), :] = yown_ref[pl.ds(yown_at + g * CX, CX), :]
         for r in range(4):
             for src, row in ((xh, CX + r), (xl, CX + 4 + r)):
-                at = pl.ds(pl.multiple_of((field * 4 + r) * NZ, 8), NZ)
+                at = pl.ds((field * 4 + r) * NZ, NZ)
                 main[pl.ds(row, NZ, stride=DEEP), :] = src[at, :]
-                at = pl.ds(pl.multiple_of(16 * NZ + (field * 4 + r) * YG, 8), YG)
+                at = pl.ds(16 * NZ + (field * 4 + r) * YG, YG)
                 edge[pl.ds(row, YG, stride=DEEP), :] = src[at, :]
 
-    @pl.when(comp == 0)
-    def _():
-        xl[...] = xlo_ref[...].astype(F32)
-        xh[...] = xhi_ref[...].astype(F32)
-        build(3, kap_ref, kapy_ref, km, ky)
-        own = jnp.where(window < 16, window - 6, LANES - 26 + window)
-        own = jnp.minimum(jnp.maximum(own, 0), LANES - 1)
-        made = jnp.logical_or(window < 7, window >= 25)
-        for g in range(YG):
-            for o in range(3):
-                v = None
-                for b in range(4):
-                    piece = take(km[pl.ds((b * YG + g) * DEEP + o * 8, 8), :], own)
-                    v = piece if v is None else jnp.where(block == b, piece, v)
-                at = pl.ds(g * DEEP + o * 8, 8)
-                ky[at, :] = jnp.where(made, ky[at, :], v)
-
-    build(comp, b_ref, yb_ref, m0, y0)
+    xl[...] = xlo_ref[...].astype(F32)
+    xh[...] = xhi_ref[...].astype(F32)
+    build(3, kap_ref, 0, kapy_ref, 0, km, ky)
+    own = jnp.where(window < 16, window - 6, LANES - 26 + window)
+    own = jnp.minimum(jnp.maximum(own, 0), LANES - 1)
+    made = jnp.logical_or(window < 7, window >= 25)
+    for g in range(YG):
+        for o in range(3):
+            v = None
+            for b in range(4):
+                piece = take(km[pl.ds((b * YG + g) * DEEP + o * 8, 8), :], own)
+                v = piece if v is None else jnp.where(block == b, piece, v)
+            at = pl.ds(g * DEEP + o * 8, 8)
+            ky[at, :] = jnp.where(made, ky[at, :], v)
 
     def relax(c, up, dn, k):
         total = next_row(c) + prev_row(c) + next_lane(c) + prev_lane(c) + (up + dn)
@@ -625,36 +646,44 @@
         return pl.ds(z * DEEP, DEEP)
 
     on_edge = jnp.logical_or(lane < 5, lane >= LANES - 5)
-    mains, edges = (m0, m1), (y0, y1)
-    for step in range(SUB):
-        a, b = mains[step % 2], mains[1 - step % 2]
-        ea, eb = edges[step % 2], edges[1 - step % 2]
-        for g in range(YG):
-            up = ea[at(g + 1), :] if g + 1 < YG else pltpu.roll(ea[at(0), :], LANES - 32, 1)
-            dn = ea[at(g - 1), :] if g > 0 else pltpu.roll(ea[at(YG - 1), :], 32, 1)
-            eb[at(g), :] = relax(ea[at(g), :], up, dn, ky[at(g), :])
-        dn, c = a[at(NZ - 1), :], a[at(0), :]
-        for z in range(NZ):
-            up = a[at((z + 1) % NZ), :]
-            new = relax(c, up, dn, km[at(z), :])
-            dn, c = c, up
-            if step < SUB - 1:
-                b[at(z), :] = new
-                continue
-            k, g = z // YG, z % YG
-            index = k * 32 + jnp.where(lane < 5, 6 + lane, lane - (LANES - 26))
-            index = jnp.minimum(jnp.maximum(index, 0), LANES - 1)
-            for o in range(2):
-                e = take(eb[pl.ds(g * DEEP + o * 8, 8), :], index)
-                out_ref[pl.ds(z * CX + o * 8, 8), :] = jnp.where(on_edge, e, new[o * 8 : o * 8 + 8])
+    for comp in range(3):
+        build(comp, b_ref, comp * PLANE, yb_ref, comp * YPLANE, m0, y0)
+        mains, edges = (m0, m1), (y0, y1)
+        for step in range(SUB):
+            a, b = mains[step % 2], mains[1 - step % 2]
+            ea, eb = edges[step % 2], edges[1 - step % 2]
+            for g in range(YG):
+                up = ea[at(g + 1), :] if g + 1 < YG else pltpu.roll(ea[at(0), :], LANES - 32, 1)
+                dn = ea[at(g - 1), :] if g > 0 else pltpu.roll(ea[at(YG - 1), :], 32, 1)
+                eb[at(g), :] = relax(ea[at(g), :], up, dn, ky[at(g), :])
+            dn, c = a[at(NZ - 1), :], a[at(0), :]
+            for z in range(NZ):
+                up = a[at((z + 1) % NZ), :]
+                new = relax(c, up, dn, km[at(z), :])
+                dn, c = c, up
+                if step < SUB - 1:
+                    b[at(z), :] = new
+                    continue
+                k, g = z // YG, z % YG
+                index = k * 32 + jnp.where(lane < 5, 6 + lane, lane - (LANES - 26))
+                index = jnp.minimum(jnp.maximum(index, 0), LANES - 1)
+                for o in range(2):
+                    e = take(eb[pl.ds(g * DEEP + o * 8, 8), :], index)
+                    done[pl.ds(comp * PLANE + z * CX + o * 8, 8), :] = jnp.where(on_edge, e, new[o * 8 : o * 8 + 8])
+        copy = pltpu.make_async_copy(done.at[pl.ds(comp * PLANE, PLANE), :],
+                                     out_ref.at[pl.ds((4 + comp) * PLANE, PLANE), :], sems.at[2 + comp])
+        copy.start()
+        copies.append(copy)
+    for copy in copies:
+        copy.wait()
 
 
 def struct(shape, dtype=F32):
     return jax.ShapeDtypeStruct(shape, dtype)
 
 
-def params():
-    return pltpu.CompilerParams(vmem_limit_bytes=VMEM_LIMIT)
+def params(mib):
+    return pltpu.CompilerParams(vmem_limit_bytes=mib << 20)
 
 
 def cost(us):
@@ -662,7 +691,6 @@
 
 
 VSPEC = pl.BlockSpec(memory_space=pltpu.VMEM)
-SSPEC = pl.BlockSpec(memory_space=pltpu.SMEM)
 
 
 def step_up(axis):
@@ -681,11 +709,13 @@
     bricks = current_sheet_bricks.reshape(1, -1)
     count = brick_count.reshape(1, 1)
 
-    blo, bhi = pl.pallas_call(
+    blo, bhi, maps = pl.pallas_call(
         pack_kernel,
-        in_specs=[SSPEC, SSPEC, VSPEC],
-        out_shape=[struct((YROWS + 16, LANES), BF16)] * 2,
-        compiler_params=params(),
+        in_specs=[pl.BlockSpec(memory_space=pltpu.HBM)] * 3,
+        out_shape=[struct((YROWS + 16, LANES), BF16)] * 2 + [struct((48, LANES), jnp.int32)],
+        scratch_shapes=[pltpu.VMEM((8 * PLANE, LANES), F32), pltpu.SMEM((1, 8), jnp.int32),
+                        pltpu.SMEM((1, 1), jnp.int32), pltpu.SemaphoreType.DMA((10,))],
+        compiler_params=params(60),
         name="pack",
     )(bricks, count, prim)
     yfl = lax.ppermute(bhi, "row", step_up("row"))
@@ -699,7 +729,7 @@
         bulk_kernel,
         out_shape=[struct((8 * PLANE, LANES))] + [struct((8 * NZ, LANES), BF16)] * 2,
         scratch_shapes=mhd_scratch(NZ),
-        compiler_params=params(),
+        compiler_params=params(20),
         cost_estimate=cost(4),
         name="bulk",
     )(prim)
@@ -709,7 +739,7 @@
         window_kernel,
         out_shape=[struct((8 * YPLANE, LANES))] + [struct((sxrows, LANES), BF16)] * 2,
         scratch_shapes=[pltpu.VMEM((YROWS, LANES), F32)] * 2,
-        compiler_params=params(),
+        compiler_params=params(12),
         cost_estimate=cost(1),
         name="windows",
     )(prim, yfl, yfr, xmlo, xmhi)
@@ -720,54 +750,49 @@
                struct((16, HID), BF16)]
     yadv, xcells, *closure = pl.pallas_call(
         ready_kernel,
-        in_specs=[SSPEC, SSPEC] + [VSPEC] * 6,
+        in_specs=[VSPEC] * 7,
         out_shape=[struct((8 * YPLANE, LANES)), struct((2 * KIN, WIDE), BF16)] + weights,
         scratch_shapes=mhd_scratch(YG),
-        compiler_params=params(),
+        compiler_params=params(16),
         cost_estimate=cost(4),
         name="ready",
-    )(bricks, count, prim, yp, w_in, w_hid.reshape(2 * HID, HID), w_out.reshape(1, HID), b_hid)
+    )(maps, prim, yp, w_in, w_hid.reshape(2 * HID, HID), w_out.reshape(1, HID), b_hid)
 
     xrows = 16 * NZ + 16 * YG
     rest, badv, yb, ky, kape, sxlo, sxhi = pl.pallas_call(
         edge_kernel,
-        in_specs=[SSPEC, SSPEC] + [VSPEC] * 13,
-        out_shape=[struct((8 * PLANE, LANES)), struct((3 * PLANE, LANES)), struct((3 * YPLANE, LANES)),
+        in_specs=[VSPEC] * 14,
+        out_shape=[struct((5 * PLANE, LANES)), struct((3 * PLANE, LANES)), struct((3 * YPLANE, LANES)),
                    struct((YPLANE, LANES)), struct((6 * HALF, LANES)),
                    struct((xrows, LANES), BF16), struct((xrows, LANES), BF16)],
         scratch_shapes=[pltpu.VMEM((sxrows, LANES), F32)] * 2 + [pltpu.VMEM((8 * YPLANE, LANES), F32)],
-        compiler_params=params(),
+        compiler_params=params(32),
         cost_estimate=cost(8),
         name="edges",
-    )(bricks, count, prim, adv, yp, yadv, xcells, xlo, xhi, yfl, yfr, *closure)
+    )(maps, prim, adv, yp, yadv, xcells, xlo, xhi, yfl, yfr, *closure)
 
     gothi = lax.ppermute(sxlo, "col", step_down("col"))
     gotlo = lax.ppermute(sxhi, "col", step_up("col"))
 
     kap = pl.pallas_call(
         inner_kernel,
-        in_specs=[SSPEC, SSPEC] + [VSPEC] * 6,
+        in_specs=[VSPEC] * 7,
         out_shape=struct((PLANE, LANES)),
         scratch_shapes=[pltpu.VMEM((HALF * CX, LANES), F32)],
-        compiler_params=params(),
+        compiler_params=params(24),
         cost_estimate=cost(6),
         name="inner",
-    )(bricks, count, xcells, kape, *closure)
-
-    full = lambda rows: pl.BlockSpec((rows, LANES), lambda c: (0, 0))
-    part = lambda rows: pl.BlockSpec((rows, LANES), lambda c: (c, 0))
+    )(maps, xcells, kape, *closure)
+
     out = pl.pallas_call(
         diffuse_kernel,
-        grid=(3,),
-        in_specs=[pl.BlockSpec(memory_space=pl.ANY), part(PLANE), full(PLANE), part(YPLANE), full(YPLANE),
-                  full(xrows), full(xrows)],
-        out_specs=pl.BlockSpec((PLANE, LANES), lambda c: (4 + c, 0)),
+        out_specs=pl.BlockSpec(memory_space=pltpu.HBM),
         out_shape=struct((8 * PLANE, LANES)),
-        input_output_aliases={0: 0},
         scratch_shapes=[pltpu.VMEM((NZ * DEEP, LANES), F32)] * 3
         + [pltpu.VMEM((YG * DEEP, LANES), F32)] * 3
-        + [pltpu.VMEM((xrows, LANES), F32)] * 2,
-        compiler_params=params(),
+        + [pltpu.VMEM((xrows, LANES), F32)] * 2
+        + [pltpu.VMEM((3 * PLANE, LANES), F32), pltpu.SemaphoreType.DMA((5,))],
+        compiler_params=params(16),
         name="diffuse",
     )(rest, badv, kap, yb, ky, gotlo, gothi)
     return out.reshape(shape)

time: 44 us -> 38.9 us (0.88)
  local copies, waits for them, and re-layouts: 3.59 us -> 0.03 us
  Pallas kernels: 28.9 us -> 27.1 us
    unnamed x16 -> x12, local copies, waits for them, and re-layouts: 3.59 us -> 0.03 us
    pallas_call x5, Pallas kernels: 23.5 us -> 21.7 us  [the longest x1 5.89 us: shards(): pl.pallas_call(edge_kernel, in_specs=[VSPEC] * 14, out_shape=[struct((5 *...]
  transfers between devices with their start and end apart: 6 -> 6, of which waited for: 0 -> 0; matrix products, arithmetic and copies ran while one was open for 0% -> 0% of each run, Pallas kernels for 29% -> 31%
where the time goes in v3:
time: 38.9 us; the launch traced here: 38.8 us
  Pallas kernels  27.1 us (70%)
  starting transfers between devices  10.6 us (27%)
  between operations  1.11 us (3%)
    pallas_call x1, Pallas kernels, shards(): pl.pallas_call(edge_kernel, in_specs=[VSPEC] * 14, out_shape=[struct((5 *...  5.89 us
    pallas_call x1, Pallas kernels, shards(): pl.pallas_call(inner_kernel, in_specs=[VSPEC] * 7, out_shape=struct((PLAN...  5.22 us
    pallas_call x1, Pallas kernels, shards(): pl.pallas_call(diffuse_kernel, out_specs=pl.BlockSpec(memory_space=pltpu....  4.65 us
    pallas_call x1, Pallas kernels, shards(): pl.pallas_call(bulk_kernel, out_shape=[struct((8 * PLANE, LANES))] + [str...  3.68 us
    ppermute x1, starting transfers between devices, shards(): yfl = lax.ppermute(bhi, 'row', step_up('row'))  3.08 us
    pallas_call x1, Pallas kernels, shards(): pl.pallas_call(pack_kernel, in_specs=[pl.BlockSpec(memory_space=pltpu.HBM...  2.97 us
    pallas_call x1, Pallas kernels, shards(): pl.pallas_call(ready_kernel, in_specs=[VSPEC] * 7, out_shape=[struct((8 *...  2.94 us
    ppermute x1, starting transfers between devices, shards(): xhi = lax.ppermute(slo, 'col', step_down('col'))  2.63 us
  transfers between devices with their start and end apart: 6, of which 0 were waited for; matrix products, arithmetic and copies ran while one was open for 0% of the time, Pallas kernels for 31%

profile of v3, /device:TPU:0, one launch (start us, length us, event | category | flops | bytes accessed | tf_op | source)
XLA Modules:
  0.0 38.8 jit_solution(1765619584252175088)
XLA Ops:
  0.8 3.0 %pack.1 = (bf16[272,128]{1,0:T(8,128)(2,1)}, bf16[272,128]{1,0:T(8,128)(2,1)}, s32[48,128]{1,0:T(8,128)}) custom-call(s32[1,8]{1,0:T(1,128)} %bitcast.12, s32[1,1]{1,0:T(1,128)S(6)} %copy.8.count_hbm, f32[4096,128]{1,0:T(8,128)} %bitcast.5), custom_call_target="tpu_custom_call" | custom-call | tf_op jit(solution)/shard_map/pack/pallas_call | solution.py:712
  3.8 3.1 %collective-permute-start = (bf16[272,128]{1,0:T(8,128)(2,1)}, bf16[272,128]{1,0:T(8,128)(2,1)S(1)}, u32[]{:S(2)}, u32[]{:S(2)}) collective-permute-start(bf16[272,128]{1,0:T(8,128)(2,1)} %get-tuple-element.29), channel_id=1, source_target_pairs={{0,8},{8,16},{16,24},{24,0},{1,9},{9,17},{17,25},{25,1},{2,10},{10... | collective-permute-start | bytes 208904 | tf_op jit(solution)/shard_map/ppermute | solution.py:721
  6.9 2.1 %collective-permute-start.1 = (bf16[272,128]{1,0:T(8,128)(2,1)}, bf16[272,128]{1,0:T(8,128)(2,1)S(1)}, u32[]{:S(2)}, u32[]{:S(2)}) collective-permute-start(bf16[272,128]{1,0:T(8,128)(2,1)} %get-tuple-element.30), channel_id=1, source_target_pairs={{8,0},{16,8},{24,16},{0,24},{9,1},{17,9},{25,17},{1,25},{10,2},{18... | collective-permute-start | bytes 208904 | tf_op jit(solution)/shard_map/ppermute | solution.py:722
  8.9 3.7 %bulk.1 = (f32[4096,128]{1,0:T(8,128)S(1)}, bf16[256,128]{1,0:T(8,128)(2,1)S(1)}, bf16[256,128]{1,0:T(8,128)(2,1)S(1)}) custom-call(f32[4096,128]{1,0:T(8,128)S(1)} %bitcast.6), custom_call_target="tpu_custom_call" | custom-call | flops 2000000000 | bytes 4194304 | tf_op jit(solution)/shard_map/bulk/pallas_call | solution.py:728
  12.6 0.0 copy-start.1
  12.7 0.0 copy-start.2
  12.7 0.0 copy-start.3
  12.7 0.0 copy-start.4
  12.7 0.0 copy-start.5
  12.7 0.0 collective-permute-done.yfl_ref
  12.7 0.0 collective-permute-done.1.yfr_ref
  12.7 1.7 %windows.1 = (f32[1024,128]{1,0:T(8,128)S(1)}, bf16[320,128]{1,0:T(8,128)(2,1)S(1)}, bf16[320,128]{1,0:T(8,128)(2,1)S(1)}) custom-call(f32[4096,128]{1,0:T(8,128)S(1)} %bitcast.7, bf16[272,128]{1,0:T(8,128)(2,1)S(1)} %collective-permute-done.yfl_ref, bf16[272,128]{1,0:T(8,128)(2,1)S(1)} %collective-permute-done.1.yfr_ref, ...), custom_call_target="tpu_custom_call" | custom-call | flops 500000000 | bytes 1048576 | tf_op jit(solution)/shard_map/windows/pallas_call | solution.py:738
  14.4 0.1 collective-permute-start.2
  14.5 2.6 %collective-permute-start.3 = (bf16[320,128]{1,0:T(8,128)(2,1)S(1)}, bf16[320,128]{1,0:T(8,128)(2,1)S(1)}, u32[]{:S(2)}, u32[]{:S(2)}) collective-permute-start(bf16[320,128]{1,0:T(8,128)(2,1)S(1)} %get-tuple-element.37), channel_id=1, source_target_pairs={{1,0},{2,1},{3,2},{4,3},{5,4},{6,5},{7,6},{0,7},{9,8},{10,9},{11,1... | collective-permute-start | bytes 245768 | tf_op jit(solution)/shard_map/ppermute | solution.py:747
  17.2 2.9 %ready.1 = (f32[1024,128]{1,0:T(8,128)S(1)}, bf16[160,2048]{1,0:T(8,128)(2,1)S(1)}, bf16[1024,80]{1,0:T(8,128)(2,1)S(1)}, bf16[128,144]{1,0:T(8,128)(2,1)S(1)}, ...) custom-call(s32[48,128]{1,0:T(8,128)S(1)} %copy-done.2, f32[4096,128]{1,0:T(8,128)S(1)} %bitcast.8, ...), custom_call_target="tpu_custom_call" | custom-call | flops 2000000000 | bytes 4194304 | tf_op jit(solution)/shard_map/ready/pallas_call | solution.py:751
  20.1 0.0 collective-permute-done.2.xlo_ref
  20.1 0.0 collective-permute-done.3.xhi_ref
  20.1 5.9 %edges.1 = (f32[2560,128]{1,0:T(8,128)S(1)}, f32[1536,128]{1,0:T(8,128)S(1)}, f32[384,128]{1,0:T(8,128)S(1)}, f32[128,128]{1,0:T(8,128)S(1)}, f32[96,128]{1,0:T(...) custom-call(s32[48,128]{1,0:T(8,128)S(1)} %copy-done.2, f32[4096,128]{1,0:T(8,128)S(1)} %bitcast.9, ...), custom_call_target="tpu_custom_call" | custom-call | flops 4000000000 | bytes 8388608 | tf_op jit(solution)/shard_map/edges/pallas_call | solution.py:762
  26.0 0.1 collective-permute-start.4
  26.1 2.6 %collective-permute-start.5 = (bf16[640,128]{1,0:T(8,128)(2,1)S(1)}, bf16[640,128]{1,0:T(8,128)(2,1)S(1)}, u32[]{:S(2)}, u32[]{:S(2)}) collective-permute-start(bf16[640,128]{1,0:T(8,128)(2,1)S(1)} %get-tuple-element.48), channel_id=1, source_target_pairs={{1,0},{2,1},{3,2},{4,3},{5,4},{6,5},{7,6},{0,7},{9,8},{10,9},{11,1... | collective-permute-start | bytes 491528 | tf_op jit(solution)/shard_map/ppermute | solution.py:774
  28.7 5.2 %inner.1.kap_ref = f32[512,128]{1,0:T(8,128)S(1)} custom-call(s32[48,128]{1,0:T(8,128)S(1)} %copy-done.2, bf16[160,2048]{1,0:T(8,128)(2,1)S(1)} %get-tuple-element.35.x_ref, f32[96,128]{1,0:T(8,128)S(1)} %get-tuple-element.44.kape_ref, bf16[1024,80]{1,0:T(8,128)(2,1)S(1)} %get-tuple-element.38.wb_ref, bf16[128,144]{1,0:T(8,128)(2,1)S(1)} %get-tuple-element.39.w1_ref, ...), custom_call_target="tpu_custom_call" | custom-call | flops 3000000000 | bytes 6291456 | tf_op jit(solution)/shard_map/inner/pallas_call | solution.py:777
  33.9 0.0 collective-permute-done.4.xlo_ref
  34.0 0.0 collective-permute-done.5.xhi_ref
  34.0 4.6 %diffuse.1 = f32[4096,128]{1,0:T(8,128)} custom-call(f32[2560,128]{1,0:T(8,128)S(1)} %get-tuple-element.42.rest_ref, f32[1536,128]{1,0:T(8,128)S(1)} %get-tuple-element.43.b_ref, f32[512,128]{1,0:T(8,128)S(1)} %inner.1.kap_ref, f32[384,128]{1,0:T(8,128)S(1)} %get-tuple-element.45.yb_ref, f32[128,128]{1,0:T(8,128)S(1)} %get-tuple-element.46.kapy_ref, ...), custom_call_target="tpu_custom_call" | custom-call | tf_op jit(solution)/shard_map/diffuse/pallas_call | solution.py:787
  (7 shorter events, 0.0 us)
Async XLA Ops:
  0.0 8.9 %copy-start = (f32[8,32,16,128]{3,2,1,0:T(8,128)S(1)}, f32[8,32,16,128]{3,2,1,0:T(8,128)}, u32[]{:S(2)}) copy-start(f32[8,32,16,128]{3,2,1,0:T(8,128)} %param.7) | copy-start | bytes 6291460
  3.8 8.9 %collective-permute-start = (bf16[272,128]{1,0:T(8,128)(2,1)}, bf16[272,128]{1,0:T(8,128)(2,1)S(1)}, u32[]{:S(2)}, u32[]{:S(2)}) collective-permute-start(bf16[272,128]{1,0:T(8,128)(2,1)} %get-tuple-element.29), channel_id=1, source_target_pairs={{0,8},{8,16},{16,24},{24,0},{1,9},{9,17},{17,25},{25,1},{2,10},{10... | collective-permute-start | bytes 208904 | tf_op jit(solution)/shard_map/ppermute | solution.py:721
  6.9 5.9 %collective-permute-start.1 = (bf16[272,128]{1,0:T(8,128)(2,1)}, bf16[272,128]{1,0:T(8,128)(2,1)S(1)}, u32[]{:S(2)}, u32[]{:S(2)}) collective-permute-start(bf16[272,128]{1,0:T(8,128)(2,1)} %get-tuple-element.30), channel_id=1, source_target_pairs={{8,0},{16,8},{24,16},{0,24},{9,1},{17,9},{25,17},{1,25},{10,2},{18... | collective-permute-start | bytes 208904 | tf_op jit(solution)/shard_map/ppermute | solution.py:722
  12.6 4.5 %copy-start.1 = (bf16[2,128,128]{2,1,0:T(8,128)(2,1)S(1)}, bf16[2,128,128]{2,1,0:T(8,128)(2,1)}, u32[]{:S(2)}) copy-start(bf16[2,128,128]{2,1,0:T(8,128)(2,1)} %param.11) | copy-start | bytes 196612
  12.7 4.5 %copy-start.2 = (s32[48,128]{1,0:T(8,128)S(1)}, s32[48,128]{1,0:T(8,128)}, u32[]{:S(2)}) copy-start(s32[48,128]{1,0:T(8,128)} %get-tuple-element.27.maps_ref) | copy-start | bytes 73732
  12.7 4.5 %copy-start.3 = (bf16[8,128]{1,0:T(8,128)(2,1)S(1)}, bf16[8,128]{1,0:T(8,128)(2,1)}, u32[]{:S(2)}) copy-start(bf16[8,128]{1,0:T(8,128)(2,1)} %win_ref.1) | copy-start | bytes 6148
  12.7 4.5 %copy-start.4 = (f32[3,128]{1,0:T(4,128)S(1)}, f32[3,128]{1,0:T(4,128)}, u32[]{:S(2)}) copy-start(f32[3,128]{1,0:T(4,128)} %bias_ref.1) | copy-start | bytes 4612
  12.7 4.5 %copy-start.5 = (bf16[128]{0:T(256)(128)(2,1)S(1)}, bf16[128]{0:T(256)(128)(2,1)}, u32[]{:S(2)}) copy-start(bf16[128]{0:T(256)(128)(2,1)} %param.12) | copy-start | bytes 772
  14.4 5.7 %collective-permute-start.2 = (bf16[320,128]{1,0:T(8,128)(2,1)S(1)}, bf16[320,128]{1,0:T(8,128)(2,1)S(1)}, u32[]{:S(2)}, u32[]{:S(2)}) collective-permute-start(bf16[320,128]{1,0:T(8,128)(2,1)S(1)} %get-tuple-element.36), channel_id=1, source_target_pairs={{0,1},{1,2},{2,3},{3,4},{4,5},{5,6},{6,7},{7,0},{8,9},{9,10},{10,1... | collective-permute-start | bytes 245768 | tf_op jit(solution)/shard_map/ppermute | solution.py:746
  14.5 5.6 %collective-permute-start.3 = (bf16[320,128]{1,0:T(8,128)(2,1)S(1)}, bf16[320,128]{1,0:T(8,128)(2,1)S(1)}, u32[]{:S(2)}, u32[]{:S(2)}) collective-permute-start(bf16[320,128]{1,0:T(8,128)(2,1)S(1)} %get-tuple-element.37), channel_id=1, source_target_pairs={{1,0},{2,1},{3,2},{4,3},{5,4},{6,5},{7,6},{0,7},{9,8},{10,9},{11,1... | collective-permute-start | bytes 245768 | tf_op jit(solution)/shard_map/ppermute | solution.py:747
  26.0 7.9 %collective-permute-start.4 = (bf16[640,128]{1,0:T(8,128)(2,1)S(1)}, bf16[640,128]{1,0:T(8,128)(2,1)S(1)}, u32[]{:S(2)}, u32[]{:S(2)}) collective-permute-start(bf16[640,128]{1,0:T(8,128)(2,1)S(1)} %get-tuple-element.47), channel_id=1, source_target_pairs={{0,1},{1,2},{2,3},{3,4},{4,5},{5,6},{6,7},{7,0},{8,9},{9,10},{10,1... | collective-permute-start | bytes 491528 | tf_op jit(solution)/shard_map/ppermute | solution.py:775
  26.1 7.9 %collective-permute-start.5 = (bf16[640,128]{1,0:T(8,128)(2,1)S(1)}, bf16[640,128]{1,0:T(8,128)(2,1)S(1)}, u32[]{:S(2)}, u32[]{:S(2)}) collective-permute-start(bf16[640,128]{1,0:T(8,128)(2,1)S(1)} %get-tuple-element.48), channel_id=1, source_target_pairs={{1,0},{2,1},{3,2},{4,3},{5,4},{6,5},{7,6},{0,7},{9,8},{10,9},{11,1... | collective-permute-start | bytes 491528 | tf_op jit(solution)/shard_map/ppermute | solution.py:774

commit v4 on v3

--- a/solution.py
+++ b/solution.py
@@ -175,9 +175,10 @@
             for o in range(2):
                 lo = jnp.zeros((8, LANES), F32)
                 hi = jnp.zeros((8, LANES), F32)
-                for z in range(HALF):
-                    v = prim_ref[pl.ds((f * NZ + h * HALF + z) * CX + o * 8, 8), :]
-                    mine = lane // ENDS == z
+                for spot_z in range(HALF):
+                    z = spot_z // 4 * YG + h * 4 + spot_z % 4
+                    v = prim_ref[pl.ds((f * NZ + z) * CX + o * 8, 8), :]
+                    mine = lane // ENDS == spot_z
                     lo = jnp.where(mine, take(v, spot), lo)
                     hi = jnp.where(mine, take(v, spot + (LANES - ENDS)), hi)
                 los.append(lo)
@@ -300,42 +301,7 @@
         xhi_ref[at, :] = prim_ref[pl.ds(f * PLANE + CX - 1, NZ, stride=CX), :].astype(BF16)
 
 
-def window_kernel(prim_ref, yfl_ref, yfr_ref, xlo_ref, xhi_ref, yp_ref, sxlo_ref, sxhi_ref,
-                  left_ref, right_ref):
-    lane = iota((8, LANES), 1)
-    window, block = lane % 32, lane // 32
-    own = jnp.where(window < 16, window - 6, LANES - 26 + window)
-    own = jnp.minimum(jnp.maximum(own, 0), LANES - 1)
-    spot = (block % 2) * 64 + jnp.where(window < 16, jnp.minimum(window + 2, 7), jnp.maximum(window - 26, 0))
-    left_ref[...] = yfl_ref[pl.ds(0, YROWS), :].astype(F32)
-    right_ref[...] = yfr_ref[pl.ds(0, YROWS), :].astype(F32)
-    low, high, first = window < 6, window >= 26, block < 2
-    for f in range(8):
-        for o in range(2):
-            here = [[ref[pl.ds((f * 2 + h) * CX + o * 8, 8), :] for h in range(2)]
-                    for ref in (left_ref, right_ref)]
-            for g in range(YG):
-                v = None
-                for b in range(4):
-                    piece = take(prim_ref[pl.ds((f * NZ + b * YG + g) * CX + o * 8, 8), :], own)
-                    v = piece if v is None else jnp.where(block == b, piece, v)
-                index = spot + g * ENDS
-                for side, where in ((0, low), (1, high)):
-                    got = jnp.where(first, take(here[side][0], index), take(here[side][1], index))
-                    v = jnp.where(where, got, v)
-                yp_ref[pl.ds((f * YG + g) * CX + o * 8, 8), :] = v
-    rows = 8 * NZ
-    sxlo_ref[pl.ds(0, rows), :] = xlo_ref[...]
-    sxhi_ref[pl.ds(0, rows), :] = xhi_ref[...]
-    for f in range(0, 8, 2):
-        for ref, start in ((sxlo_ref, 0), (sxhi_ref, CX - 1)):
-            ref[pl.ds(rows + f * YG, 2 * YG), :] = yp_ref[
-                pl.ds(f * YPLANE + start, 2 * YG, stride=CX), :].astype(BF16)
-
-
-def ready_kernel(maps_ref, prim_ref, yp_ref, win_ref, whid_ref, wout_ref, bias_ref,
-                 yadv_ref, x_ref, wb_ref, w1_ref, w2_ref, wo_ref,
-                 u_ref, fz_ref, sz_ref, ch_ref):
+def prepare_weights(win_ref, whid_ref, wout_ref, bias_ref, wb_ref, w1_ref, w2_ref, wo_ref):
     def split(b):
         hi = b.astype(BF16)
         r = b - hi.astype(F32)
@@ -365,6 +331,41 @@
         ref[...] = jnp.concatenate([turned, bcol], axis=1).astype(BF16)
     wo_ref[...] = jnp.broadcast_to(0.5 * wout_ref[...].astype(F32), (16, HID)).astype(BF16)
 
+
+def window_kernel(prim_ref, yfl_ref, yfr_ref, xlo_ref, xhi_ref, win_ref, whid_ref, wout_ref, bias_ref,
+                  yp_ref, sxlo_ref, sxhi_ref, wb_ref, w1_ref, w2_ref, wo_ref, left_ref, right_ref):
+    prepare_weights(win_ref, whid_ref, wout_ref, bias_ref, wb_ref, w1_ref, w2_ref, wo_ref)
+    lane = iota((8, LANES), 1)
+    window, block = lane % 32, lane // 32
+    own = jnp.where(window < 16, window - 6, LANES - 26 + window)
+    own = jnp.minimum(jnp.maximum(own, 0), LANES - 1)
+    spot = block * 32 + jnp.where(window < 16, jnp.minimum(window + 2, 7), jnp.maximum(window - 26, 0))
+    left_ref[...] = yfl_ref[pl.ds(0, YROWS), :].astype(F32)
+    right_ref[...] = yfr_ref[pl.ds(0, YROWS), :].astype(F32)
+    low, high = window < 6, window >= 26
+    for f in range(8):
+        for o in range(2):
+            here = [[ref[pl.ds((f * 2 + h) * CX + o * 8, 8), :] for h in range(2)]
+                    for ref in (left_ref, right_ref)]
+            for g in range(YG):
+                v = None
+                for b in range(4):
+                    piece = take(prim_ref[pl.ds((f * NZ + b * YG + g) * CX + o * 8, 8), :], own)
+                    v = piece if v is None else jnp.where(block == b, piece, v)
+                index = spot + g % 4 * ENDS
+                for side, where in ((0, low), (1, high)):
+                    v = jnp.where(where, take(here[side][g // 4], index), v)
+                yp_ref[pl.ds((f * YG + g) * CX + o * 8, 8), :] = v
+    rows = 8 * NZ
+    sxlo_ref[pl.ds(0, rows), :] = xlo_ref[...]
+    sxhi_ref[pl.ds(0, rows), :] = xhi_ref[...]
+    for f in range(0, 8, 2):
+        for ref, start in ((sxlo_ref, 0), (sxhi_ref, CX - 1)):
+            ref[pl.ds(rows + f * YG, 2 * YG), :] = yp_ref[
+                pl.ds(f * YPLANE + start, 2 * YG, stride=CX), :].astype(BF16)
+
+
+def ready_kernel(maps_ref, prim_ref, yp_ref, yadv_ref, x_ref, u_ref, fz_ref, sz_ref, ch_ref):
     mhd_bulk(YG, yp_ref, u_ref, fz_ref, sz_ref, ch_ref, yadv_ref, 4, True)
 
     source, half, _, _ = read_maps(maps_ref)
@@ -735,28 +736,27 @@
     )(prim)
 
     sxrows = 8 * NZ + 8 * YG
-    yp, slo, shi = pl.pallas_call(
+    weights = [struct((8 * HID, KIN), BF16), struct((HID, KHID), BF16), struct((HID, KHID), BF16),
+               struct((16, HID), BF16)]
+    yp, slo, shi, *closure = pl.pallas_call(
         window_kernel,
-        out_shape=[struct((8 * YPLANE, LANES))] + [struct((sxrows, LANES), BF16)] * 2,
+        out_shape=[struct((8 * YPLANE, LANES))] + [struct((sxrows, LANES), BF16)] * 2 + weights,
         scratch_shapes=[pltpu.VMEM((YROWS, LANES), F32)] * 2,
         compiler_params=params(12),
         cost_estimate=cost(1),
         name="windows",
-    )(prim, yfl, yfr, xmlo, xmhi)
+    )(prim, yfl, yfr, xmlo, xmhi, w_in, w_hid.reshape(2 * HID, HID), w_out.reshape(1, HID), b_hid)
     xlo = lax.ppermute(shi, "col", step_up("col"))
     xhi = lax.ppermute(slo, "col", step_down("col"))
 
-    weights = [struct((8 * HID, KIN), BF16), struct((HID, KHID), BF16), struct((HID, KHID), BF16),
-               struct((16, HID), BF16)]
-    yadv, xcells, *closure = pl.pallas_call(
+    yadv, xcells = pl.pallas_call(
         ready_kernel,
-        in_specs=[VSPEC] * 7,
-        out_shape=[struct((8 * YPLANE, LANES)), struct((2 * KIN, WIDE), BF16)] + weights,
+        out_shape=[struct((8 * YPLANE, LANES)), struct((2 * KIN, WIDE), BF16)],
         scratch_shapes=mhd_scratch(YG),
         compiler_params=params(16),
         cost_estimate=cost(4),
         name="ready",
-    )(maps, prim, yp, w_in, w_hid.reshape(2 * HID, HID), w_out.reshape(1, HID), b_hid)
+    )(maps, prim, yp)
 
     xrows = 16 * NZ + 16 * YG
     rest, badv, yb, ky, kape, sxlo, sxhi = pl.pallas_call(

time: 38.9 us -> 38.5 us (0.990)
  Pallas kernels: 27.1 us -> 26.6 us
    pallas_call x1, Pallas kernels: 1.71 us -> 1.28 us  [shards(): pl.pallas_call(window_kernel, out_shape=[struct((8 * YPLANE, LANES))] + [...]
  transfers between devices with their start and end apart: 6 -> 6, of which waited for: 0 -> 0; matrix products, arithmetic and copies ran while one was open for 0% -> 0% of each run, Pallas kernels for 31% -> 30%
where the time goes in v4:
time: 38.5 us; the launch traced here: 38.3 us
  Pallas kernels  26.6 us (69%)
  starting transfers between devices  10.6 us (28%)
  between operations  1.1 us (3%)
    pallas_call x1, Pallas kernels, shards(): pl.pallas_call(edge_kernel, in_specs=[VSPEC] * 14, out_shape=[struct((5 *...  6.07 us
    pallas_call x1, Pallas kernels, shards(): pl.pallas_call(inner_kernel, in_specs=[VSPEC] * 7, out_shape=struct((PLAN...  5.3 us
    pallas_call x1, Pallas kernels, shards(): pl.pallas_call(diffuse_kernel, out_specs=pl.BlockSpec(memory_space=pltpu....  4.65 us
    pallas_call x1, Pallas kernels, shards(): pl.pallas_call(bulk_kernel, out_shape=[struct((8 * PLANE, LANES))] + [str...  3.68 us
    ppermute x1, starting transfers between devices, shards(): yfl = lax.ppermute(bhi, 'row', step_up('row'))  3.08 us
    pallas_call x1, Pallas kernels, shards(): pl.pallas_call(pack_kernel, in_specs=[pl.BlockSpec(memory_space=pltpu.HBM...  2.97 us
    pallas_call x1, Pallas kernels, shards(): pl.pallas_call(ready_kernel, out_shape=[struct((8 * YPLANE, LANES)), stru...  2.63 us
    ppermute x1, starting transfers between devices, shards(): xhi = lax.ppermute(slo, 'col', step_down('col'))  2.63 us
  transfers between devices with their start and end apart: 6, of which 0 were waited for; matrix products, arithmetic and copies ran while one was open for 0% of the time, Pallas kernels for 30%

profile of v4, /device:TPU:0, one launch (start us, length us, event | category | flops | bytes accessed | tf_op | source)
XLA Modules:
  0.0 38.3 jit_solution(8426603352344933319)
XLA Ops:
  0.8 3.0 %pack.1 = (bf16[272,128]{1,0:T(8,128)(2,1)}, bf16[272,128]{1,0:T(8,128)(2,1)}, s32[48,128]{1,0:T(8,128)}) custom-call(s32[1,8]{1,0:T(1,128)} %bitcast.12, s32[1,1]{1,0:T(1,128)S(6)} %copy.8.count_hbm, f32[4096,128]{1,0:T(8,128)} %bitcast.5), custom_call_target="tpu_custom_call" | custom-call | tf_op jit(solution)/shard_map/pack/pallas_call | solution.py:713
  3.8 3.1 %collective-permute-start = (bf16[272,128]{1,0:T(8,128)(2,1)}, bf16[272,128]{1,0:T(8,128)(2,1)S(1)}, u32[]{:S(2)}, u32[]{:S(2)}) collective-permute-start(bf16[272,128]{1,0:T(8,128)(2,1)} %get-tuple-element.29), channel_id=1, source_target_pairs={{0,8},{8,16},{16,24},{24,0},{1,9},{9,17},{17,25},{25,1},{2,10},{10... | collective-permute-start | bytes 208904 | tf_op jit(solution)/shard_map/ppermute | solution.py:722
  6.9 2.1 %collective-permute-start.1 = (bf16[272,128]{1,0:T(8,128)(2,1)}, bf16[272,128]{1,0:T(8,128)(2,1)S(1)}, u32[]{:S(2)}, u32[]{:S(2)}) collective-permute-start(bf16[272,128]{1,0:T(8,128)(2,1)} %get-tuple-element.30), channel_id=1, source_target_pairs={{8,0},{16,8},{24,16},{0,24},{9,1},{17,9},{25,17},{1,25},{10,2},{18... | collective-permute-start | bytes 208904 | tf_op jit(solution)/shard_map/ppermute | solution.py:723
  9.0 0.0 copy-done
  9.0 3.7 %bulk.1 = (f32[4096,128]{1,0:T(8,128)S(1)}, bf16[256,128]{1,0:T(8,128)(2,1)S(1)}, bf16[256,128]{1,0:T(8,128)(2,1)S(1)}) custom-call(f32[4096,128]{1,0:T(8,128)S(1)} %bitcast.6), custom_call_target="tpu_custom_call" | custom-call | flops 2000000000 | bytes 4194304 | tf_op jit(solution)/shard_map/bulk/pallas_call | solution.py:729
  12.7 0.0 copy-start.5
  12.7 0.0 collective-permute-done.yfl_ref
  12.7 0.0 collective-permute-done.1.yfr_ref
  12.7 0.0 copy-done.1
  12.7 0.0 copy-done.2
  12.7 0.0 copy-done.3
  12.8 1.3 %windows.1 = (f32[1024,128]{1,0:T(8,128)S(1)}, bf16[320,128]{1,0:T(8,128)(2,1)S(1)}, bf16[320,128]{1,0:T(8,128)(2,1)S(1)}, bf16[1024,80]{1,0:T(8,128)(2,1)S(1)},...) custom-call(f32[4096,128]{1,0:T(8,128)S(1)} %bitcast.7, ...), custom_call_target="tpu_custom_call" | custom-call | flops 500000000 | bytes 1048576 | tf_op jit(solution)/shard_map/windows/pallas_call | solution.py:741
  14.0 0.1 collective-permute-start.2
  14.1 2.6 %collective-permute-start.3 = (bf16[320,128]{1,0:T(8,128)(2,1)S(1)}, bf16[320,128]{1,0:T(8,128)(2,1)S(1)}, u32[]{:S(2)}, u32[]{:S(2)}) collective-permute-start(bf16[320,128]{1,0:T(8,128)(2,1)S(1)} %get-tuple-element.37), channel_id=1, source_target_pairs={{1,0},{2,1},{3,2},{4,3},{5,4},{6,5},{7,6},{0,7},{9,8},{10,9},{11,1... | collective-permute-start | bytes 245768 | tf_op jit(solution)/shard_map/ppermute | solution.py:750
  16.7 2.6 %ready.1 = (f32[1024,128]{1,0:T(8,128)S(1)}, bf16[160,2048]{1,0:T(8,128)(2,1)S(1)}) custom-call(s32[48,128]{1,0:T(8,128)S(1)} %copy-done.5, f32[4096,128]{1,0:T(8,128)S(1)} %bitcast.8, f32[1024,128]{1,0:T(8,128)S(1)} %get-tuple-element.33.yp_ref), custom_call_target="tpu_custom_call" | custom-call | flops 2000000000 | bytes 4194304 | tf_op jit(solution)/shard_map/ready/pallas_call | solution.py:752
  19.4 0.0 collective-permute-done.2.xlo_ref
  19.4 0.0 collective-permute-done.3.xhi_ref
  19.4 6.1 %edges.1 = (f32[2560,128]{1,0:T(8,128)S(1)}, f32[1536,128]{1,0:T(8,128)S(1)}, f32[384,128]{1,0:T(8,128)S(1)}, f32[128,128]{1,0:T(8,128)S(1)}, f32[96,128]{1,0:T(...) custom-call(s32[48,128]{1,0:T(8,128)S(1)} %copy-done.5, f32[4096,128]{1,0:T(8,128)S(1)} %bitcast.9, ...), custom_call_target="tpu_custom_call" | custom-call | flops 4000000000 | bytes 8388608 | tf_op jit(solution)/shard_map/edges/pallas_call | solution.py:762
  25.5 0.4 %collective-permute-start.4 = (bf16[640,128]{1,0:T(8,128)(2,1)S(1)}, bf16[640,128]{1,0:T(8,128)(2,1)S(1)}, u32[]{:S(2)}, u32[]{:S(2)}) collective-permute-start(bf16[640,128]{1,0:T(8,128)(2,1)S(1)} %get-tuple-element.47), channel_id=1, source_target_pairs={{0,1},{1,2},{2,3},{3,4},{4,5},{5,6},{6,7},{7,0},{8,9},{9,10},{10,1... | collective-permute-start | bytes 491528 | tf_op jit(solution)/shard_map/ppermute | solution.py:775
  25.9 2.3 %collective-permute-start.5 = (bf16[640,128]{1,0:T(8,128)(2,1)S(1)}, bf16[640,128]{1,0:T(8,128)(2,1)S(1)}, u32[]{:S(2)}, u32[]{:S(2)}) collective-permute-start(bf16[640,128]{1,0:T(8,128)(2,1)S(1)} %get-tuple-element.48), channel_id=1, source_target_pairs={{1,0},{2,1},{3,2},{4,3},{5,4},{6,5},{7,6},{0,7},{9,8},{10,9},{11,1... | collective-permute-start | bytes 491528 | tf_op jit(solution)/shard_map/ppermute | solution.py:774
  28.2 5.3 %inner.1.kap_ref = f32[512,128]{1,0:T(8,128)S(1)} custom-call(s32[48,128]{1,0:T(8,128)S(1)} %copy-done.5, bf16[160,2048]{1,0:T(8,128)(2,1)S(1)} %get-tuple-element.35.x_ref, f32[96,128]{1,0:T(8,128)S(1)} %get-tuple-element.44.kape_ref, bf16[1024,80]{1,0:T(8,128)(2,1)S(1)} %get-tuple-element.38.wb_ref, bf16[128,144]{1,0:T(8,128)(2,1)S(1)} %get-tuple-element.39.w1_ref, ...), custom_call_target="tpu_custom_call" | custom-call | flops 3000000000 | bytes 6291456 | tf_op jit(solution)/shard_map/inner/pallas_call | solution.py:777
  33.5 0.0 collective-permute-done.4.xlo_ref
  33.5 0.0 collective-permute-done.5.xhi_ref
  33.5 4.6 %diffuse.1 = f32[4096,128]{1,0:T(8,128)} custom-call(f32[2560,128]{1,0:T(8,128)S(1)} %get-tuple-element.42.rest_ref, f32[1536,128]{1,0:T(8,128)S(1)} %get-tuple-element.43.b_ref, f32[512,128]{1,0:T(8,128)S(1)} %inner.1.kap_ref, f32[384,128]{1,0:T(8,128)S(1)} %get-tuple-element.45.yb_ref, f32[128,128]{1,0:T(8,128)S(1)} %get-tuple-element.46.kapy_ref, ...), custom_call_target="tpu_custom_call" | custom-call | tf_op jit(solution)/shard_map/diffuse/pallas_call | solution.py:787
  (7 shorter events, 0.0 us)
Async XLA Ops:
  0.0 9.0 %copy-start = (f32[8,32,16,128]{3,2,1,0:T(8,128)S(1)}, f32[8,32,16,128]{3,2,1,0:T(8,128)}, u32[]{:S(2)}) copy-start(f32[8,32,16,128]{3,2,1,0:T(8,128)} %param.7) | copy-start | bytes 6291460
  3.8 8.9 %collective-permute-start = (bf16[272,128]{1,0:T(8,128)(2,1)}, bf16[272,128]{1,0:T(8,128)(2,1)S(1)}, u32[]{:S(2)}, u32[]{:S(2)}) collective-permute-start(bf16[272,128]{1,0:T(8,128)(2,1)} %get-tuple-element.29), channel_id=1, source_target_pairs={{0,8},{8,16},{16,24},{24,0},{1,9},{9,17},{17,25},{25,1},{2,10},{10... | collective-permute-start | bytes 208904 | tf_op jit(solution)/shard_map/ppermute | solution.py:722
  6.9 5.9 %copy-start.1 = (bf16[2,128,128]{2,1,0:T(8,128)(2,1)S(1)}, bf16[2,128,128]{2,1,0:T(8,128)(2,1)}, u32[]{:S(2)}) copy-start(bf16[2,128,128]{2,1,0:T(8,128)(2,1)} %param.11) | copy-start | bytes 196612
  6.9 5.9 %copy-start.2 = (bf16[8,128]{1,0:T(8,128)(2,1)S(1)}, bf16[8,128]{1,0:T(8,128)(2,1)}, u32[]{:S(2)}) copy-start(bf16[8,128]{1,0:T(8,128)(2,1)} %win_ref.1) | copy-start | bytes 6148
  6.9 5.9 %copy-start.3 = (f32[3,128]{1,0:T(4,128)S(1)}, f32[3,128]{1,0:T(4,128)}, u32[]{:S(2)}) copy-start(f32[3,128]{1,0:T(4,128)} %bias_ref.1) | copy-start | bytes 4612
  6.9 5.9 %copy-start.4 = (bf16[128]{0:T(256)(128)(2,1)S(1)}, bf16[128]{0:T(256)(128)(2,1)}, u32[]{:S(2)}) copy-start(bf16[128]{0:T(256)(128)(2,1)} %param.12) | copy-start | bytes 772
  6.9 5.8 %collective-permute-start.1 = (bf16[272,128]{1,0:T(8,128)(2,1)}, bf16[272,128]{1,0:T(8,128)(2,1)S(1)}, u32[]{:S(2)}, u32[]{:S(2)}) collective-permute-start(bf16[272,128]{1,0:T(8,128)(2,1)} %get-tuple-element.30), channel_id=1, source_target_pairs={{8,0},{16,8},{24,16},{0,24},{9,1},{17,9},{25,17},{1,25},{10,2},{18... | collective-permute-start | bytes 208904 | tf_op jit(solution)/shard_map/ppermute | solution.py:723
  12.7 4.0 %copy-start.5 = (s32[48,128]{1,0:T(8,128)S(1)}, s32[48,128]{1,0:T(8,128)}, u32[]{:S(2)}) copy-start(s32[48,128]{1,0:T(8,128)} %get-tuple-element.27.maps_ref) | copy-start | bytes 73732
  14.0 5.3 %collective-permute-start.2 = (bf16[320,128]{1,0:T(8,128)(2,1)S(1)}, bf16[320,128]{1,0:T(8,128)(2,1)S(1)}, u32[]{:S(2)}, u32[]{:S(2)}) collective-permute-start(bf16[320,128]{1,0:T(8,128)(2,1)S(1)} %get-tuple-element.36), channel_id=1, source_target_pairs={{0,1},{1,2},{2,3},{3,4},{4,5},{5,6},{6,7},{7,0},{8,9},{9,10},{10,1... | collective-permute-start | bytes 245768 | tf_op jit(solution)/shard_map/ppermute | solution.py:749
  14.1 5.3 %collective-permute-start.3 = (bf16[320,128]{1,0:T(8,128)(2,1)S(1)}, bf16[320,128]{1,0:T(8,128)(2,1)S(1)}, u32[]{:S(2)}, u32[]{:S(2)}) collective-permute-start(bf16[320,128]{1,0:T(8,128)(2,1)S(1)} %get-tuple-element.37), channel_id=1, source_target_pairs={{1,0},{2,1},{3,2},{4,3},{5,4},{6,5},{7,6},{0,7},{9,8},{10,9},{11,1... | collective-permute-start | bytes 245768 | tf_op jit(solution)/shard_map/ppermute | solution.py:750
  25.5 8.0 %collective-permute-start.4 = (bf16[640,128]{1,0:T(8,128)(2,1)S(1)}, bf16[640,128]{1,0:T(8,128)(2,1)S(1)}, u32[]{:S(2)}, u32[]{:S(2)}) collective-permute-start(bf16[640,128]{1,0:T(8,128)(2,1)S(1)} %get-tuple-element.47), channel_id=1, source_target_pairs={{0,1},{1,2},{2,3},{3,4},{4,5},{5,6},{6,7},{7,0},{8,9},{9,10},{10,1... | collective-permute-start | bytes 491528 | tf_op jit(solution)/shard_map/ppermute | solution.py:775
  25.9 7.6 %collective-permute-start.5 = (bf16[640,128]{1,0:T(8,128)(2,1)S(1)}, bf16[640,128]{1,0:T(8,128)(2,1)S(1)}, u32[]{:S(2)}, u32[]{:S(2)}) collective-permute-start(bf16[640,128]{1,0:T(8,128)(2,1)S(1)} %get-tuple-element.48), channel_id=1, source_target_pairs={{1,0},{2,1},{3,2},{4,3},{5,4},{6,5},{7,6},{0,7},{9,8},{10,9},{11,1... | collective-permute-start | bytes 491528 | tf_op jit(solution)/shard_map/ppermute | solution.py:774

commit v5 on v4

--- a/solution.py
+++ b/solution.py
@@ -602,7 +602,7 @@
 
 
 def diffuse_kernel(rest_ref, b_ref, kap_ref, yb_ref, kapy_ref, xlo_ref, xhi_ref, out_ref,
-                   m0, m1, km, y0, y1, ky, xl, xh, done, sems):
+                   m0, m1, km, y0, y1, ky, xl, xh, done, kc, kyc, sems):
     copies = [pltpu.make_async_copy(rest_ref.at[pl.ds(0, 4 * PLANE), :],
                                     out_ref.at[pl.ds(0, 4 * PLANE), :], sems.at[0]),
               pltpu.make_async_copy(rest_ref.at[pl.ds(4 * PLANE, PLANE), :],
@@ -639,9 +639,12 @@
             at = pl.ds(g * DEEP + o * 8, 8)
             ky[at, :] = jnp.where(made, ky[at, :], v)
 
-    def relax(c, up, dn, k):
-        total = next_row(c) + prev_row(c) + next_lane(c) + prev_lane(c) + (up + dn)
-        return c + k * (total - 6.0 * c)
+    kc[...] = 1.0 - 6.0 * km[...]
+    kyc[...] = 1.0 - 6.0 * ky[...]
+
+    def relax(c, up, dn, k, own):
+        total = (next_row(c) + prev_row(c)) + (next_lane(c) + prev_lane(c)) + (up + dn)
+        return own * c + k * total
 
     def at(z):
         return pl.ds(z * DEEP, DEEP)
@@ -656,11 +659,11 @@
             for g in range(YG):
                 up = ea[at(g + 1), :] if g + 1 < YG else pltpu.roll(ea[at(0), :], LANES - 32, 1)
                 dn = ea[at(g - 1), :] if g > 0 else pltpu.roll(ea[at(YG - 1), :], 32, 1)
-                eb[at(g), :] = relax(ea[at(g), :], up, dn, ky[at(g), :])
+                eb[at(g), :] = relax(ea[at(g), :], up, dn, ky[at(g), :], kyc[at(g), :])
             dn, c = a[at(NZ - 1), :], a[at(0), :]
             for z in range(NZ):
                 up = a[at((z + 1) % NZ), :]
-                new = relax(c, up, dn, km[at(z), :])
+                new = relax(c, up, dn, km[at(z), :], kc[at(z), :])
                 dn, c = c, up
                 if step < SUB - 1:
                     b[at(z), :] = new
@@ -719,8 +722,8 @@
         compiler_params=params(60),
         name="pack",
     )(bricks, count, prim)
+    yfr = lax.ppermute(blo, "row", step_down("row"))
     yfl = lax.ppermute(bhi, "row", step_up("row"))
-    yfr = lax.ppermute(blo, "row", step_down("row"))
 
     def mhd_scratch(planes):
         many = pltpu.VMEM((8 * planes * CX, LANES), F32)
@@ -791,7 +794,8 @@
         scratch_shapes=[pltpu.VMEM((NZ * DEEP, LANES), F32)] * 3
         + [pltpu.VMEM((YG * DEEP, LANES), F32)] * 3
         + [pltpu.VMEM((xrows, LANES), F32)] * 2
-        + [pltpu.VMEM((3 * PLANE, LANES), F32), pltpu.SemaphoreType.DMA((5,))],
+        + [pltpu.VMEM((3 * PLANE, LANES), F32), pltpu.VMEM((NZ * DEEP, LANES), F32),
+           pltpu.VMEM((YG * DEEP, LANES), F32), pltpu.SemaphoreType.DMA((5,))],
         compiler_params=params(16),
         name="diffuse",
     )(rest, badv, kap, yb, ky, gotlo, gothi)

time: 38.5 us -> 38.4 us (level)
  no operation moved by 1% of the time
where the time goes in v5:
time: 38.4 us; the launch traced here: 38.2 us
  Pallas kernels  26.5 us (69%)
  starting transfers between devices  10.6 us (28%)
  between operations  1.1 us (3%)
    pallas_call x1, Pallas kernels, shards(): pl.pallas_call(edge_kernel, in_specs=[VSPEC] * 14, out_shape=[struct((5 *...  6.07 us
    pallas_call x1, Pallas kernels, shards(): pl.pallas_call(inner_kernel, in_specs=[VSPEC] * 7, out_shape=struct((PLAN...  5.3 us
    pallas_call x1, Pallas kernels, shards(): pl.pallas_call(diffuse_kernel, out_specs=pl.BlockSpec(memory_space=pltpu....  4.57 us
    pallas_call x1, Pallas kernels, shards(): pl.pallas_call(bulk_kernel, out_shape=[struct((8 * PLANE, LANES))] + [str...  3.68 us
    ppermute x1, starting transfers between devices, shards(): yfl = lax.ppermute(bhi, 'row', step_up('row'))  3.08 us
    pallas_call x1, Pallas kernels, shards(): pl.pallas_call(pack_kernel, in_specs=[pl.BlockSpec(memory_space=pltpu.HBM...  2.97 us
    pallas_call x1, Pallas kernels, shards(): pl.pallas_call(ready_kernel, out_shape=[struct((8 * YPLANE, LANES)), stru...  2.63 us
    ppermute x1, starting transfers between devices, shards(): xhi = lax.ppermute(slo, 'col', step_down('col'))  2.63 us
  transfers between devices with their start and end apart: 6, of which 0 were waited for; matrix products, arithmetic and copies ran while one was open for 0% of the time, Pallas kernels for 30%

profile of v5, /device:TPU:0, one launch (start us, length us, event | category | flops | bytes accessed | tf_op | source)
XLA Modules:
  0.0 38.2 jit_solution(4284249873694961773)
XLA Ops:
  0.8 3.0 %pack.1 = (bf16[272,128]{1,0:T(8,128)(2,1)}, bf16[272,128]{1,0:T(8,128)(2,1)}, s32[48,128]{1,0:T(8,128)}) custom-call(s32[1,8]{1,0:T(1,128)} %bitcast.12, s32[1,1]{1,0:T(1,128)S(6)} %copy.8.count_hbm, f32[4096,128]{1,0:T(8,128)} %bitcast.5), custom_call_target="tpu_custom_call" | custom-call | tf_op jit(solution)/shard_map/pack/pallas_call | solution.py:716
  3.8 3.1 %collective-permute-start = (bf16[272,128]{1,0:T(8,128)(2,1)}, bf16[272,128]{1,0:T(8,128)(2,1)S(1)}, u32[]{:S(2)}, u32[]{:S(2)}) collective-permute-start(bf16[272,128]{1,0:T(8,128)(2,1)} %get-tuple-element.29), channel_id=1, source_target_pairs={{0,8},{8,16},{16,24},{24,0},{1,9},{9,17},{17,25},{25,1},{2,10},{10... | collective-permute-start | bytes 208904 | tf_op jit(solution)/shard_map/ppermute | solution.py:726
  6.9 2.1 %collective-permute-start.1 = (bf16[272,128]{1,0:T(8,128)(2,1)}, bf16[272,128]{1,0:T(8,128)(2,1)S(1)}, u32[]{:S(2)}, u32[]{:S(2)}) collective-permute-start(bf16[272,128]{1,0:T(8,128)(2,1)} %get-tuple-element.30), channel_id=1, source_target_pairs={{8,0},{16,8},{24,16},{0,24},{9,1},{17,9},{25,17},{1,25},{10,2},{18... | collective-permute-start | bytes 208904 | tf_op jit(solution)/shard_map/ppermute | solution.py:725
  9.0 0.0 copy-done
  9.0 3.7 %bulk.1 = (f32[4096,128]{1,0:T(8,128)S(1)}, bf16[256,128]{1,0:T(8,128)(2,1)S(1)}, bf16[256,128]{1,0:T(8,128)(2,1)S(1)}) custom-call(f32[4096,128]{1,0:T(8,128)S(1)} %bitcast.6), custom_call_target="tpu_custom_call" | custom-call | flops 2000000000 | bytes 4194304 | tf_op jit(solution)/shard_map/bulk/pallas_call | solution.py:732
  12.7 0.0 copy-start.5
  12.7 0.0 collective-permute-done.yfl_ref
  12.7 0.0 collective-permute-done.1.yfr_ref
  12.7 0.0 copy-done.1
  12.7 0.0 copy-done.2
  12.7 0.0 copy-done.3
  12.8 1.3 %windows.1 = (f32[1024,128]{1,0:T(8,128)S(1)}, bf16[320,128]{1,0:T(8,128)(2,1)S(1)}, bf16[320,128]{1,0:T(8,128)(2,1)S(1)}, bf16[1024,80]{1,0:T(8,128)(2,1)S(1)},...) custom-call(f32[4096,128]{1,0:T(8,128)S(1)} %bitcast.7, ...), custom_call_target="tpu_custom_call" | custom-call | flops 500000000 | bytes 1048576 | tf_op jit(solution)/shard_map/windows/pallas_call | solution.py:744
  14.0 0.1 collective-permute-start.2
  14.1 2.6 %collective-permute-start.3 = (bf16[320,128]{1,0:T(8,128)(2,1)S(1)}, bf16[320,128]{1,0:T(8,128)(2,1)S(1)}, u32[]{:S(2)}, u32[]{:S(2)}) collective-permute-start(bf16[320,128]{1,0:T(8,128)(2,1)S(1)} %get-tuple-element.37), channel_id=1, source_target_pairs={{1,0},{2,1},{3,2},{4,3},{5,4},{6,5},{7,6},{0,7},{9,8},{10,9},{11,1... | collective-permute-start | bytes 245768 | tf_op jit(solution)/shard_map/ppermute | solution.py:753
  16.7 2.6 %ready.1 = (f32[1024,128]{1,0:T(8,128)S(1)}, bf16[160,2048]{1,0:T(8,128)(2,1)S(1)}) custom-call(s32[48,128]{1,0:T(8,128)S(1)} %copy-done.5, f32[4096,128]{1,0:T(8,128)S(1)} %bitcast.8, f32[1024,128]{1,0:T(8,128)S(1)} %get-tuple-element.33.yp_ref), custom_call_target="tpu_custom_call" | custom-call | flops 2000000000 | bytes 4194304 | tf_op jit(solution)/shard_map/ready/pallas_call | solution.py:755
  19.4 0.0 collective-permute-done.2.xlo_ref
  19.4 0.0 collective-permute-done.3.xhi_ref
  19.4 6.1 %edges.1 = (f32[2560,128]{1,0:T(8,128)S(1)}, f32[1536,128]{1,0:T(8,128)S(1)}, f32[384,128]{1,0:T(8,128)S(1)}, f32[128,128]{1,0:T(8,128)S(1)}, f32[96,128]{1,0:T(...) custom-call(s32[48,128]{1,0:T(8,128)S(1)} %copy-done.5, f32[4096,128]{1,0:T(8,128)S(1)} %bitcast.9, ...), custom_call_target="tpu_custom_call" | custom-call | flops 4000000000 | bytes 8388608 | tf_op jit(solution)/shard_map/edges/pallas_call | solution.py:765
  25.5 0.4 %collective-permute-start.4 = (bf16[640,128]{1,0:T(8,128)(2,1)S(1)}, bf16[640,128]{1,0:T(8,128)(2,1)S(1)}, u32[]{:S(2)}, u32[]{:S(2)}) collective-permute-start(bf16[640,128]{1,0:T(8,128)(2,1)S(1)} %get-tuple-element.47), channel_id=1, source_target_pairs={{0,1},{1,2},{2,3},{3,4},{4,5},{5,6},{6,7},{7,0},{8,9},{9,10},{10,1... | collective-permute-start | bytes 491528 | tf_op jit(solution)/shard_map/ppermute | solution.py:778
  25.9 2.3 %collective-permute-start.5 = (bf16[640,128]{1,0:T(8,128)(2,1)S(1)}, bf16[640,128]{1,0:T(8,128)(2,1)S(1)}, u32[]{:S(2)}, u32[]{:S(2)}) collective-permute-start(bf16[640,128]{1,0:T(8,128)(2,1)S(1)} %get-tuple-element.48), channel_id=1, source_target_pairs={{1,0},{2,1},{3,2},{4,3},{5,4},{6,5},{7,6},{0,7},{9,8},{10,9},{11,1... | collective-permute-start | bytes 491528 | tf_op jit(solution)/shard_map/ppermute | solution.py:777
  28.2 5.3 %inner.1.kap_ref = f32[512,128]{1,0:T(8,128)S(1)} custom-call(s32[48,128]{1,0:T(8,128)S(1)} %copy-done.5, bf16[160,2048]{1,0:T(8,128)(2,1)S(1)} %get-tuple-element.35.x_ref, f32[96,128]{1,0:T(8,128)S(1)} %get-tuple-element.44.kape_ref, bf16[1024,80]{1,0:T(8,128)(2,1)S(1)} %get-tuple-element.38.wb_ref, bf16[128,144]{1,0:T(8,128)(2,1)S(1)} %get-tuple-element.39.w1_ref, ...), custom_call_target="tpu_custom_call" | custom-call | flops 3000000000 | bytes 6291456 | tf_op jit(solution)/shard_map/inner/pallas_call | solution.py:780
  33.5 0.0 collective-permute-done.4.xlo_ref
  33.5 0.0 collective-permute-done.5.xhi_ref
  33.5 4.6 %diffuse.1 = f32[4096,128]{1,0:T(8,128)} custom-call(f32[2560,128]{1,0:T(8,128)S(1)} %get-tuple-element.42.rest_ref, f32[1536,128]{1,0:T(8,128)S(1)} %get-tuple-element.43.b_ref, f32[512,128]{1,0:T(8,128)S(1)} %inner.1.kap_ref, f32[384,128]{1,0:T(8,128)S(1)} %get-tuple-element.45.yb_ref, f32[128,128]{1,0:T(8,128)S(1)} %get-tuple-element.46.kapy_ref, ...), custom_call_target="tpu_custom_call" | custom-call | tf_op jit(solution)/shard_map/diffuse/pallas_call | solution.py:790
  (7 shorter events, 0.0 us)
Async XLA Ops:
  0.0 9.0 %copy-start = (f32[8,32,16,128]{3,2,1,0:T(8,128)S(1)}, f32[8,32,16,128]{3,2,1,0:T(8,128)}, u32[]{:S(2)}) copy-start(f32[8,32,16,128]{3,2,1,0:T(8,128)} %param.7) | copy-start | bytes 6291460
  3.8 8.9 %collective-permute-start = (bf16[272,128]{1,0:T(8,128)(2,1)}, bf16[272,128]{1,0:T(8,128)(2,1)S(1)}, u32[]{:S(2)}, u32[]{:S(2)}) collective-permute-start(bf16[272,128]{1,0:T(8,128)(2,1)} %get-tuple-element.29), channel_id=1, source_target_pairs={{0,8},{8,16},{16,24},{24,0},{1,9},{9,17},{17,25},{25,1},{2,10},{10... | collective-permute-start | bytes 208904 | tf_op jit(solution)/shard_map/ppermute | solution.py:726
  6.9 5.9 %copy-start.1 = (bf16[2,128,128]{2,1,0:T(8,128)(2,1)S(1)}, bf16[2,128,128]{2,1,0:T(8,128)(2,1)}, u32[]{:S(2)}) copy-start(bf16[2,128,128]{2,1,0:T(8,128)(2,1)} %param.11) | copy-start | bytes 196612
  6.9 5.9 %copy-start.2 = (bf16[8,128]{1,0:T(8,128)(2,1)S(1)}, bf16[8,128]{1,0:T(8,128)(2,1)}, u32[]{:S(2)}) copy-start(bf16[8,128]{1,0:T(8,128)(2,1)} %win_ref.1) | copy-start | bytes 6148
  6.9 5.9 %copy-start.3 = (f32[3,128]{1,0:T(4,128)S(1)}, f32[3,128]{1,0:T(4,128)}, u32[]{:S(2)}) copy-start(f32[3,128]{1,0:T(4,128)} %bias_ref.1) | copy-start | bytes 4612
  6.9 5.9 %copy-start.4 = (bf16[128]{0:T(256)(128)(2,1)S(1)}, bf16[128]{0:T(256)(128)(2,1)}, u32[]{:S(2)}) copy-start(bf16[128]{0:T(256)(128)(2,1)} %param.12) | copy-start | bytes 772
  6.9 5.8 %collective-permute-start.1 = (bf16[272,128]{1,0:T(8,128)(2,1)}, bf16[272,128]{1,0:T(8,128)(2,1)S(1)}, u32[]{:S(2)}, u32[]{:S(2)}) collective-permute-start(bf16[272,128]{1,0:T(8,128)(2,1)} %get-tuple-element.30), channel_id=1, source_target_pairs={{8,0},{16,8},{24,16},{0,24},{9,1},{17,9},{25,17},{1,25},{10,2},{18... | collective-permute-start | bytes 208904 | tf_op jit(solution)/shard_map/ppermute | solution.py:725
  12.7 4.0 %copy-start.5 = (s32[48,128]{1,0:T(8,128)S(1)}, s32[48,128]{1,0:T(8,128)}, u32[]{:S(2)}) copy-start(s32[48,128]{1,0:T(8,128)} %get-tuple-element.27.maps_ref) | copy-start | bytes 73732
  14.0 5.3 %collective-permute-start.2 = (bf16[320,128]{1,0:T(8,128)(2,1)S(1)}, bf16[320,128]{1,0:T(8,128)(2,1)S(1)}, u32[]{:S(2)}, u32[]{:S(2)}) collective-permute-start(bf16[320,128]{1,0:T(8,128)(2,1)S(1)} %get-tuple-element.36), channel_id=1, source_target_pairs={{0,1},{1,2},{2,3},{3,4},{4,5},{5,6},{6,7},{7,0},{8,9},{9,10},{10,1... | collective-permute-start | bytes 245768 | tf_op jit(solution)/shard_map/ppermute | solution.py:752
  14.1 5.3 %collective-permute-start.3 = (bf16[320,128]{1,0:T(8,128)(2,1)S(1)}, bf16[320,128]{1,0:T(8,128)(2,1)S(1)}, u32[]{:S(2)}, u32[]{:S(2)}) collective-permute-start(bf16[320,128]{1,0:T(8,128)(2,1)S(1)} %get-tuple-element.37), channel_id=1, source_target_pairs={{1,0},{2,1},{3,2},{4,3},{5,4},{6,5},{7,6},{0,7},{9,8},{10,9},{11,1... | collective-permute-start | bytes 245768 | tf_op jit(solution)/shard_map/ppermute | solution.py:753
  25.5 8.0 %collective-permute-start.4 = (bf16[640,128]{1,0:T(8,128)(2,1)S(1)}, bf16[640,128]{1,0:T(8,128)(2,1)S(1)}, u32[]{:S(2)}, u32[]{:S(2)}) collective-permute-start(bf16[640,128]{1,0:T(8,128)(2,1)S(1)} %get-tuple-element.47), channel_id=1, source_target_pairs={{0,1},{1,2},{2,3},{3,4},{4,5},{5,6},{6,7},{7,0},{8,9},{9,10},{10,1... | collective-permute-start | bytes 491528 | tf_op jit(solution)/shard_map/ppermute | solution.py:778
  25.9 7.6 %collective-permute-start.5 = (bf16[640,128]{1,0:T(8,128)(2,1)S(1)}, bf16[640,128]{1,0:T(8,128)(2,1)S(1)}, u32[]{:S(2)}, u32[]{:S(2)}) collective-permute-start(bf16[640,128]{1,0:T(8,128)(2,1)S(1)} %get-tuple-element.48), channel_id=1, source_target_pairs={{1,0},{2,1},{3,2},{4,3},{5,4},{6,5},{7,6},{0,7},{9,8},{10,9},{11,1... | collective-permute-start | bytes 491528 | tf_op jit(solution)/shard_map/ppermute | solution.py:777
